TPU v7x, 128 devices: a whole 4x4x4 slice. The times are simulated.
128 devices in a mesh: row: 16 (over y, x), col: 8 (over z, core).
Axes of the slice: x: 4, y: 4, z: 4, core: 2. Of those that a mesh axis runs over, the one named last changes fastest.
Arguments:
- tokens: bfloat16 [2048, 8192], P('row', 'col'), may hold values from -6 to 6
- weight: bfloat16 [8192, 28672], P('row', 'col'), may hold values from -0.0625 to 0.0625
- left_factors: bfloat16 [1024, 8192], P('row', 'col'), may hold values from -6 to 6
- right_factors: bfloat16 [1024, 28672], P('row', 'col'), may hold values from -6 to 6
- fitness: float32 [1024], P('row'), may hold values from -12 to 12
Outputs:
- outputs: bfloat16 [2048, 28672], P('row', 'col')
- update: bfloat16 [8192, 28672], P('row', 'col')
All inputs are finite; a program needn't handle non-finite values.
Results may differ from a plain program's by a relative error of at most 0.005.
Values may be sent and summed in bfloat16 or wider, within the bound.
No kernel may reach another device: no remote copies, remote signals or barrier semaphores. Data moves between devices by JAX's collectives and lax.ppermute only.
A program may use at most 128 MiB of HBM per device.

v0:
```python
import math

import jax
import jax.numpy as jnp
from jax import lax
from jax.sharding import PartitionSpec as P

D = 8192


noise_scale = 0.5
epsilon = 1e-05


def body(tokens, weight, left_factors, right_factors, fitness):
    rows_full, left_full = (
        lax.all_gather(tokens, "col", axis=1, tiled=True),
        lax.all_gather(left_factors, "col", axis=1, tiled=True),
    )
    local_members = left_full.shape[0]
    local_rows = rows_full.shape[0]
    out_cols = weight.shape[1]
    grouped = rows_full.reshape(local_members, local_rows // local_members, rows_full.shape[1])
    probe = jnp.einsum(
        "mtd,md->mt", grouped, left_full, preferred_element_type=jnp.float32
    ) / math.sqrt(D)
    spread_rows, left_cols = (
        lax.all_to_all(rows_full, "row", split_axis=1, concat_axis=0, tiled=True),
        lax.all_to_all(left_full, "row", split_axis=1, concat_axis=0, tiled=True),
    )
    base = lax.psum_scatter(
        jnp.dot(spread_rows, weight, preferred_element_type=jnp.float32),
        "row",
        scatter_dimension=0,
        tiled=True,
    )
    perturbed = (
        base.reshape(local_members, -1, out_cols)
        + noise_scale * probe[:, :, None] * right_factors.astype(jnp.float32)[:, None, :]
    )
    outputs = perturbed.reshape(local_rows, out_cols).astype(jnp.bfloat16)
    total, squares = lax.psum((jnp.sum(fitness), jnp.sum(fitness * fitness)), "row")
    count = fitness.shape[0] * lax.axis_size("row")
    mean = total / count
    spread = squares / count - mean * mean
    shared = (fitness - mean) / jnp.sqrt(spread + epsilon)
    scores = lax.all_gather(shared, "row", axis=0, tiled=True)
    piece = lax.all_gather(right_factors, "row", axis=0, tiled=True)
    weighted = (scores[:, None] * piece.astype(jnp.float32)).astype(jnp.bfloat16)
    summed = lax.dot_general(
        left_cols, weighted, (((0,), (0,)), ((), ())), preferred_element_type=jnp.float32
    )
    update = (summed / math.sqrt(scores.shape[0])).astype(jnp.bfloat16)
    return (outputs, update)


def solution(mesh):
    return jax.shard_map(
        body,
        mesh=mesh,
        in_specs=(P("row", "col"), P("row", "col"), P("row", "col"), P("row", "col"), P("row")),
        out_specs=(P("row", "col"), P("row", "col")),
        check_vma=False,
    )
```

profile of v0, /device:TPU:0, one launch (start us, length us, event | category | flops | bytes accessed | tf_op | source)
XLA Modules:
  0.0 323.5 jit_solution(1694446295023849583)
XLA Ops:
  7.2 0.0 all-gather.4.cloned.1.call-start
  7.2 1.8 copy.18
  9.0 0.0 all-gather.4.cloned.1.call-update
  9.0 0.0 all-gather.6.cloned.1.call-start
  9.1 0.7 all-gather.6.cloned.1.call-update
  9.8 0.0 all-gather.8.cloned.1.call-start
  9.8 0.7 all-gather.8.cloned.1.call-update
  10.5 0.0 reduce-scatter.2.cloned.1.call-start
  10.6 27.6 %all-gather.4.cloned.1.call-done = bf16[128,8192]{0,1:T(8,128)(2,1)} async-done(((bf16[128,1024]{0,1:T(8,128)(2,1)}), bf16[128,8192]{0,1:T(8,128)(2,1)}) %all-gather.4.cloned.1.call-update) | async-done | bytes 2097168 | tf_op jit(solution)/shard_map/all_gather | solution.py:17
  38.2 35.6 %all_to_all.38 = bf16[128,16,512]{0,2,1:T(8,128)(2,1)S(1)} all-to-all(bf16[128,16,512]{0,2,1:T(8,128)(2,1)} %bitcast.20), channel_id=1, replica_groups=mesh['row'=16,'col'=8] {'row'}, dimensions={1} | all-to-all | bytes 4194304 | tf_op jit(solution)/shard_map/all_to_all | solution.py:28
  73.8 2.6 copy.19
  76.4 16.0 %fusion.6 = f32[2048,3584]{1,0:T(8,128)} fusion(bf16[2048,512]{1,0:T(8,128)(2,1)} %bitcast.22, bf16[512,3584]{1,0:T(8,128)(2,1)} %param.6), kind=kOutput, calls=%fused_computation.13 | convolution fusion | flops 7516192768 | bytes 35127296 | tf_op jit(solution)/shard_map/dot_general | solution.py:32
  92.4 0.6 copy-done.4
  93.0 0.6 fusion.5
  93.6 37.9 %all-reduce.1 = (f32[]{:T(128)}, f32[]{:T(128)}) all-reduce(f32[]{:T(128)} %get-tuple-element.13, f32[]{:T(128)} %get-tuple-element.12), channel_id=1, replica_groups=mesh['row'=16,'col'=8] {'row'}, use_global_device_ids=true, to_apply=%region_4.0 | all-reduce | flops 2 | bytes 16 | tf_op jit(solution)/shard_map/psum | solution.py:42
  134.2 0.6 dynamic-slice
  135.4 0.0 all-gather.6.cloned.1.call-done
  135.4 2.4 copy.29
  137.8 4.3 %all-to-all-start.1 = ((bf16[64,16,512]{2,0,1:T(8,128)(2,1)}), bf16[64,16,512]{2,0,1:T(8,128)(2,1)}, u32[]{:S(2)}, u32[]{:S(2)}) async-start(bf16[64,16,512]{2,0,1:T(8,128)(2,1)} %bitcast.19), calls=%async_computation.2 | async-start | bytes 2097152 | tf_op jit(solution)/shard_map/all_to_all | solution.py:29
  142.2 0.1 divide_dynamic-update-slice_fusion
  142.3 1.7 mul.45
  144.0 3.9 %mul.46 = f32[128,3584]{1,0:T(8,128)} reshape(f32[64,2,3584]{2,1,0:T(2,128)} %mul.45) | data formatting | bytes 3670016 | tf_op jit(solution)/shard_map/mul | solution.py:39
  147.9 46.9 %all-reduce = f32[1024]{0:T(1024)S(1)} all-reduce(f32[1024]{0:T(1024)S(1)} %divide_dynamic-update-slice_fusion), channel_id=1, replica_groups=mesh['row'=16,'col'=8] {'row'}, use_global_device_ids=true, to_apply=%add | all-reduce | flops 1024 | bytes 8192
  194.8 2.9 copy.20
  197.7 3.3 %reshape.22 = bf16[64,2,8192]{2,1,0:T(2,128)(2,1)S(1)} reshape(bf16[128,8192]{1,0:T(8,128)(2,1)} %copy.20) | data formatting | bytes 4194304 | tf_op jit(solution)/shard_map/reshape | solution.py:23
  201.0 5.5 %fusion.3 = f32[64,1,2]{2,1,0:T(1,128)S(1)} fusion(bf16[64,2,8192]{2,1,0:T(2,128)(2,1)S(1)} %reshape.22, bf16[64,8192,1]{1,0,2:T(8,128)(2,1)S(1)} %bitcast.24), kind=kOutput, calls=%fused_computation.5 | convolution fusion | flops 2097152 | bytes 3146240 | tf_op jit(solution)/shard_map/mtd,md->mt/dot_general | solution.py:24
  206.5 0.2 mul.43
  206.7 0.0 all-gather.8.cloned.1.call-done
  206.7 9.8 %fusion.2 = bf16[512,3584]{0,1:T(8,128)(2,1)} fusion(bf16[1024,512]{1,0:T(8,128)(2,1)} %bitcast.8, bf16[1024,3584]{1,0:T(8,128)(2,1)} %all-gather.8.cloned.1.call-done, f32[1024]{0:T(1024)S(1)} %all-reduce), kind=kOutput, calls=%fused_computation.4 | convolution fusion | flops 3772776448 | bytes 12062720 | tf_op jit(solution)/shard_map/dot_general | solution.py:50
  216.5 6.1 %copy.22 = bf16[512,3584]{1,0:T(8,128)(2,1)} copy(bf16[512,3584]{0,1:T(8,128)(2,1)} %fusion.2) | data formatting | bytes 7340032
  222.6 91.7 %reduce-scatter.2.cloned.1.call-done = f32[128,3584]{1,0:T(8,128)} async-done(((f32[2048,3584]{1,0:T(8,128)}), f32[128,3584]{1,0:T(8,128)}) %reduce-scatter.2.cloned.1.call-update) | async-done | bytes 1835024 | tf_op jit(solution)/shard_map/reduce_scatter | solution.py:31
  314.3 2.7 add_convert_fusion
  (15 shorter events, 0.1 us)
Async XLA Ops:
  7.2 31.0 %all-gather.4.cloned.1.call-start = ((), (), s32[]{:S(2)}) async-start(), calls=%async_computation.3 | async-start | bytes 2359296 | tf_op jit(solution)/shard_map/all_gather | solution.py:17
  9.0 126.4 %all-gather.6.cloned.1.call-start = ((), (), s32[]{:S(2)}) async-start(), calls=%async_computation.5 | async-start | bytes 1179648 | tf_op jit(solution)/shard_map/all_gather | solution.py:18
  9.8 196.9 %all-gather.8.cloned.1.call-start = ((), (), s32[]{:S(2)}) async-start(), calls=%async_computation.6 | async-start | bytes 7798784 | tf_op jit(solution)/shard_map/all_gather | solution.py:48
  10.5 303.8 %reduce-scatter.2.cloned.1.call-start = ((), (), s32[]{:S(2)}) async-start(), calls=%async_computation.4 | async-start | bytes 31195136 | tf_op jit(solution)/shard_map/reduce_scatter | solution.py:31
  92.4 0.7 copy-start.4
  92.4 41.8 %copy-start.5 = (u32[128]{0:T(128)S(1)}, u32[128]{0:T(128)}, u32[]{:S(2)}) copy-start(u32[128]{0:T(128)} %constant.20) | copy-start | bytes 1540
  135.4 6.8 %copy-start.2 = (bf16[64,3584]{1,0:T(8,128)(2,1)S(1)}, bf16[64,3584]{1,0:T(8,128)(2,1)}, u32[]{:S(2)}) copy-start(bf16[64,3584]{1,0:T(8,128)(2,1)} %param.8) | copy-start | bytes 1376260
  137.8 68.8 %all-to-all-start.1 = ((bf16[64,16,512]{2,0,1:T(8,128)(2,1)}), bf16[64,16,512]{2,0,1:T(8,128)(2,1)}, u32[]{:S(2)}, u32[]{:S(2)}) async-start(bf16[64,16,512]{2,0,1:T(8,128)(2,1)} %bitcast.19), calls=%async_computation.2 | async-start | bytes 2097152 | tf_op jit(solution)/shard_map/all_to_all | solution.py:29
  144.0 50.8 %copy-start = (bf16[128,8192]{0,1:T(8,128)(2,1)S(1)}, bf16[128,8192]{0,1:T(8,128)(2,1)}, u32[]{:S(2)}) copy-start(bf16[128,8192]{0,1:T(8,128)(2,1)} %all-gather.4.cloned.1.call-done) | copy-start | bytes 6291460
  197.7 3.3 %copy-start.3 = (bf16[64,8192]{1,0:T(8,128)(2,1)S(1)}, bf16[64,8192]{1,0:T(8,128)(2,1)}, u32[]{:S(2)}) copy-start(bf16[64,8192]{1,0:T(8,128)(2,1)} %all-gather.6.cloned.1.call-done) | copy-start | bytes 3145732
  216.5 97.8 %copy-start.1 = (f32[128,3584]{1,0:T(8,128)S(1)}, f32[128,3584]{1,0:T(8,128)}, u32[]{:S(2)}) copy-start(f32[128,3584]{1,0:T(8,128)} %mul.46) | copy-start | bytes 5505028
Sparse Core Ops, SparseCore 0:
  10.3 27.8 all-gather.3
  39.9 23.9 all-gather.5
  66.0 66.3 all-gather.7
  135.7 178.5 reduce-scatter.1
where the time goes:
time: 325 us; the launch traced here: 324 us
  waiting for transfers between devices  121 us (37%)
  blocking collectives  120 us (37%)
  matrix products  31.4 us (10%)
  local copies, waits for them, and re-layouts  26 us (8%)
  between operations  17.1 us (5%)
  starting transfers between devices  4.49 us (1%)
  other arithmetic  3.42 us (1%)
    reduce_scatter x1, waiting for transfers between devices, body(): lax.psum_scatter(jnp.dot(spread_rows, weight, preferred_element_type=jnp....  91.7 us
    unnamed x1, blocking collectives  46.9 us
    psum x1, blocking collectives, body(): lax.psum((jnp.sum(fitness), jnp.sum(fitness * fitness)), 'row')  37.9 us
    all_to_all x1, blocking collectives, body(): lax.all_to_all(rows_full, 'row', split_axis=1, concat_axis=0, tiled=True)  35.6 us
    all_gather x1, waiting for transfers between devices, body(): lax.all_gather(tokens, 'col', axis=1, tiled=True)  27.6 us
    dot_general x1, matrix products, body(): jnp.dot(spread_rows, weight, preferred_element_type=jnp.float32)  16 us
    dot_general x1, matrix products, body(): lax.dot_general(left_cols, weighted, (((0,), (0,)), ((), ())), preferred_...  9.82 us
    unnamed x16, local copies, waits for them, and re-layouts  9.11 us
  transfers between devices with their start and end apart: 5, of which 2 were waited for; matrix products, arithmetic and copies ran while one was open for 17% of the time, Pallas kernels for 0%

commit v1 on v0

v1 whole, which is shorter than its diff:
```python
import math

import jax
import jax.numpy as jnp
from jax import lax
from jax.sharding import Mesh, PartitionSpec as P

noise_scale = 0.5
epsilon = 1e-05


def shift(value, axis, by):
    return lax.ppermute(value, axis, [(i, (i + by) % 4) for i in range(4)])


def body(tokens, weight, left_factors, right_factors, fitness):
    y, x, z, c = (lax.axis_index(name) for name in ("y", "x", "z", "c"))
    members, width = left_factors.shape
    out_cols = weight.shape[1]
    quarter = out_cols // 4
    features = width * 8
    population = members * 16

    grouped = tokens.reshape(members, 2, width)
    share = jnp.einsum("mtd,md->mt", grouped, left_factors, preferred_element_type=jnp.float32)
    small = jnp.concatenate([fitness, share.reshape(-1)])
    small_all = lax.all_gather(small, ("y", "x", "z", "c"), axis=0, tiled=False)
    right_all = lax.all_gather(right_factors, ("y", "x"), axis=0, tiled=True)

    weight_x = lax.all_to_all(weight, "x", split_axis=1, concat_axis=0, tiled=True)

    both = jnp.concatenate(
        [tokens.reshape(4, -1, width), left_factors.reshape(4, -1, width)], axis=1
    )
    tok_rows = tokens.shape[0] // 4
    arrived = []
    for s in range(4):
        piece = lax.dynamic_index_in_dim(both, (y + s) % 4, 0, keepdims=False)
        perm = [(4 * yy + zz, 4 * zz + (yy + s) % 4) for yy in range(4) for zz in range(4)]
        arrived.append(lax.ppermute(piece, ("y", "z"), perm))
    arrived = jnp.stack(arrived)
    tok_y = arrived[:, :tok_rows].reshape(4 * tok_rows, width)
    left_y = arrived[:, tok_rows:].reshape(members, width)

    half = width // 2

    def left_for(xx):
        cols = lax.dynamic_slice_in_dim(left_y, (xx % 2) * half, half, 1)
        return jnp.concatenate([cols[: members // 2], cols[members // 2 :]], axis=1)

    slots = []
    for d in range(4):
        sent = jnp.concatenate([tok_y, left_for((x + d) % 4)], axis=0)
        slots.append(sent if d == 0 else shift(sent, "x", d))
    slots = jnp.stack(slots)
    tok_x = slots[:, : 4 * tok_rows].reshape(16 * tok_rows, width)
    left_x = slots[:, 4 * tok_rows :]
    left_x = jnp.concatenate([left_x[..., :half], left_x[..., half:]], axis=1)
    swap = [(0, 1), (1, 0)]
    left_o = lax.ppermute(left_x, "c", swap)
    left_x = jnp.where(c == x // 2, left_x, left_o)
    left_x = left_x.reshape(4 * members, half)
    mine = lax.dynamic_slice_in_dim(left_x, c * 2 * members, 2 * members, 0)
    mine = jnp.concatenate([mine[:members], mine[members:]], axis=1)

    ring = [(2 * zz, 2 * ((zz + 1) % 4)) for zz in range(4)]
    ring += [(2 * zz + 1, 2 * ((zz - 1) % 4) + 1) for zz in range(4)]
    held = [jnp.concatenate([tok_x, mine], axis=0)]
    for _ in range(3):
        held.append(lax.ppermute(held[-1], ("z", "c"), ring))
    other = [lax.ppermute(h, "c", swap) for h in held]
    low = [jnp.where(c == 0, h, o) for h, o in zip(held, other)]
    high = [jnp.where(c == 0, o, h) for h, o in zip(held, other)]
    rows = 16 * tok_rows

    def partial(k):
        top = jnp.dot(low[k][:rows], weight_x[:width], preferred_element_type=jnp.float32)
        bottom = jnp.dot(high[-k % 4][:rows], weight_x[width:], preferred_element_type=jnp.float32)
        return (top + bottom).astype(jnp.bfloat16).reshape(4, 4, tok_rows, quarter)

    sums = {}
    for pair in ((0, 2), (1, 3)):
        parts = [partial(k) for k in pair]

        def block(yy):
            return jnp.stack(
                [
                    lax.dynamic_index_in_dim(p, (z - k - yy) % 4, 1, keepdims=False)
                    for k, p in zip(pair, parts)
                ]
            )

        total = block(y).astype(jnp.float32)
        for dy in range(1, 4):
            total = total + shift(block((y + dy) % 4), "y", dy).astype(jnp.float32)
        for i, k in enumerate(pair):
            sums[k] = total[i].astype(jnp.bfloat16)
    summed = jnp.stack([sums[k] for k in range(4)])
    columns = []
    for d in range(4):
        sent = summed[:, d]
        columns.append(sent if d == 0 else shift(sent, "x", -d))
    columns = jnp.stack(columns)
    columns = jnp.stack([lax.dynamic_index_in_dim(columns, (z - zz) % 4, 1, keepdims=False) for zz in range(4)], 1)
    base = jnp.concatenate(
        [
            lax.dynamic_index_in_dim(columns, (q - x) % 4, 0, keepdims=False).reshape(4 * tok_rows, quarter)
            for q in range(4)
        ],
        axis=1,
    )

    shares = lax.dynamic_slice_in_dim(small_all, (4 * y + x) * 8, 8, 0)[:, members:]
    probe = jnp.sum(shares, axis=0).reshape(members, 2) / math.sqrt(features)
    fit = small_all.reshape(16, 8, -1)[:, 0, :members].reshape(-1)
    outputs = (
        base.astype(jnp.float32).reshape(members, 2, out_cols)
        + noise_scale * probe[:, :, None] * right_factors.astype(jnp.float32)[:, None, :]
    )
    outputs = outputs.reshape(2 * members, out_cols).astype(jnp.bfloat16)

    mean = jnp.sum(fit) / population
    centred = fit - mean
    scores = centred / jnp.sqrt(jnp.sum(centred * centred) / population + epsilon)
    weighted = (scores[:, None] * right_all.astype(jnp.float32)).astype(jnp.bfloat16)

    def left_half(h):
        v = h[rows:]
        return jnp.concatenate([v[:, :half], v[:, half:]], axis=0).reshape(2, 4, members // 4, half)

    by_z = [
        jnp.concatenate([left_half(low[k]), left_half(high[-k % 4])], axis=0) for k in range(4)
    ]
    by_z = jnp.stack(by_z)
    blocks = []
    for zz in range(4):
        blocks.append(lax.dynamic_index_in_dim(by_z, (z - zz) % 4, 0, keepdims=False))
    blocks = jnp.stack(blocks)
    blocks = jnp.stack(
        [lax.dynamic_index_in_dim(blocks, (x - xx) % 4, 1, keepdims=False) for xx in range(4)], 1
    )
    ordered = []
    for yy in range(4):
        ordered.append(jnp.stack([blocks[zz, :, (zz - yy) % 4] for zz in range(4)], 1))
    left_all = jnp.stack(ordered).reshape(population, half)
    total = lax.dot_general(
        left_all, weighted, (((0,), (0,)), ((), ())), preferred_element_type=jnp.float32
    )
    update = (total / math.sqrt(population)).astype(jnp.bfloat16)
    return outputs, update


def solution(mesh):
    grid = Mesh(mesh.devices.reshape(4, 4, 4, 2), ("y", "x", "z", "c"))
    spec = P(("y", "x"), ("z", "c"))
    return jax.shard_map(
        body,
        mesh=grid,
        in_specs=(spec, spec, spec, spec, P(("y", "x"))),
        out_specs=(spec, spec),
        check_vma=False,
    )
```

time: 325 us -> 348 us (1.071)
  blocking collectives: 120 us -> 0 us
  waiting for transfers between devices: 121 us -> 233 us
  starting transfers between devices: 4.49 us -> 38.3 us
  matrix products: 31.4 us -> 21.6 us
  other arithmetic: 3.42 us -> 12.5 us
    unnamed x4 -> x3, waiting for transfers between devices: 1.41 us -> 154 us
    reduce_scatter x1 -> x0, waiting for transfers between devices: 91.7 us -> none  [body(): lax.psum_scatter(jnp.dot(spread_rows, weight, preferred_element_type=jnp....]
    ppermute x0 -> x24, waiting for transfers between devices: none -> 79 us  [the longest x12 60.3 us: shift(): return lax.ppermute(value, axis, [(i, (i + by) % 4) for i in range(4)])]
    unnamed x1 -> x0, blocking collectives: 46.9 us -> none
    psum x1 -> x0, blocking collectives: 37.9 us -> none  [body(): lax.psum((jnp.sum(fitness), jnp.sum(fitness * fitness)), 'row')]
    all_to_all x1 -> x0, blocking collectives: 35.6 us -> none  [body(): lax.all_to_all(rows_full, 'row', split_axis=1, concat_axis=0, tiled=True)]
    ppermute x0 -> x24, starting transfers between devices: none -> 33.4 us  [the longest x12 15 us: shift(): return lax.ppermute(value, axis, [(i, (i + by) % 4) for i in range(4)])]
    all_gather x3 -> x1, waiting for transfers between devices: 27.7 us -> 0.01 us  [body(): right_all = lax.all_gather(right_factors, ('y', 'x'), axis=0, tiled=True)]
  transfers between devices with their start and end apart: 5 -> 27, of which waited for: 2 -> 14; matrix products, arithmetic and copies ran while one was open for 17% -> 13% of each run, Pallas kernels for 0% -> 0%
where the time goes in v1:
time: 348 us
  waiting for transfers between devices  233 us (67%)
  starting transfers between devices  38.3 us (11%)
  local copies, waits for them, and re-layouts  25 us (7%)
  matrix products  21.6 us (6%)
  between operations  17.7 us (5%)
  other arithmetic  12.5 us (4%)
    unnamed x3, waiting for transfers between devices  154 us
    ppermute x12, waiting for transfers between devices, shift(): return lax.ppermute(value, axis, [(i, (i + by) % 4) for i in range(4)])  60.3 us
    ppermute x12, starting transfers between devices, shift(): return lax.ppermute(value, axis, [(i, (i + by) % 4) for i in range(4)])  15 us
    ppermute x4, waiting for transfers between devices, body(): arrived.append(lax.ppermute(piece, ('y', 'z'), perm))  13.3 us
    dot_general x1, matrix products, body(): lax.dot_general(left_all, weighted, (((0,), (0,)), ((), ())), preferred_e...  8.97 us
    ppermute x4, starting transfers between devices, body(): arrived.append(lax.ppermute(piece, ('y', 'z'), perm))  8.94 us
    unnamed x20, local copies, waits for them, and re-layouts  8.88 us
  transfers between devices with their start and end apart: 27, of which 14 were waited for; matrix products, arithmetic and copies ran while one was open for 13% of the time, Pallas kernels for 0%

profile of v1, /device:TPU:0, one launch (start us, length us, event | category | flops | bytes accessed | tf_op | source)
XLA Modules:
  0.0 347.6 jit_solution(11351497212586717289)
XLA Ops:
  9.1 4.2 %collective-permute-start.3 = (bf16[48,1024]{1,0:T(8,128)(2,1)S(1)}, bf16[48,1024]{1,0:T(8,128)(2,1)S(1)}, u32[]{:S(2)}, u32[]{:S(2)}) collective-permute-start(bf16[48,1024]{1,0:T(8,128)(2,1)S(1)} %get-tuple-element.87), channel_id=1, source_target_pairs={{0,6},{2,38},{4,70},{6,102},{32,0},{34,32},{36,64},{38,96},{64,2},... | collective-permute-start | bytes 294920 | tf_op jit(solution)/shard_map/ppermute | solution.py:40
  13.3 4.1 %collective-permute-start.2 = (bf16[48,1024]{1,0:T(8,128)(2,1)S(1)}, bf16[48,1024]{1,0:T(8,128)(2,1)S(1)}, u32[]{:S(2)}, u32[]{:S(2)}) collective-permute-start(bf16[48,1024]{1,0:T(8,128)(2,1)S(1)} %get-tuple-element.86), channel_id=1, source_target_pairs={{0,4},{2,36},{4,68},{6,100},{32,6},{34,38},{36,70},{38,102},{64,0}... | collective-permute-start | bytes 294920 | tf_op jit(solution)/shard_map/ppermute | solution.py:40
  18.2 12.0 %collective-permute-done.2 = bf16[48,1024]{1,0:T(8,128)(2,1)S(1)} collective-permute-done((bf16[48,1024]{1,0:T(8,128)(2,1)S(1)}, bf16[48,1024]{1,0:T(8,128)(2,1)S(1)}, u32[]{:S(2)}, u32[]{:S(2)}) %collective-permute-start.2) | collective-permute-done | bytes 98336 | tf_op jit(solution)/shard_map/ppermute | solution.py:40
  31.8 2.8 collective-permute-start.6
  37.3 11.2 %collective-permute-done.6 = bf16[160,1024]{1,0:T(8,128)(2,1)S(1)} collective-permute-done((bf16[160,1024]{1,0:T(8,128)(2,1)S(1)}, bf16[160,1024]{1,0:T(8,128)(2,1)S(1)}, u32[]{:S(2)}, u32[]{:S(2)}) %collective-permute-start.6) | collective-permute-done | bytes 327712 | tf_op jit(solution)/shard_map/ppermute | solution.py:13
  48.4 3.7 %collective-permute-done.4 = bf16[160,1024]{1,0:T(8,128)(2,1)S(1)} collective-permute-done((bf16[160,1024]{1,0:T(8,128)(2,1)S(1)}, bf16[160,1024]{1,0:T(8,128)(2,1)S(1)}, u32[]{:S(2)}, u32[]{:S(2)}) %collective-permute-start.4) | collective-permute-done | bytes 327712 | tf_op jit(solution)/shard_map/ppermute | solution.py:13
  53.1 5.9 %copy.85 = bf16[512,3584]{0,1:T(8,128)(2,1)} copy(bf16[512,3584]{1,0:T(8,128)(2,1)} %param.6) | data formatting | bytes 7340032 | tf_op args[1]
  59.0 4.8 %all-to-all-start = ((bf16[512,4,896]{0,2,1:T(8,128)(2,1)}), bf16[512,4,896]{0,2,1:T(8,128)(2,1)}, u32[]{:S(2)}, u32[]{:S(2)}) async-start(bf16[512,4,896]{0,2,1:T(8,128)(2,1)} %bitcast.181), calls=%async_computation | async-start | bytes 7340032 | tf_op jit(solution)/shard_map/all_to_all | solution.py:30
  66.0 2.3 collective-permute-start.9
  68.2 2.7 collective-permute-start.8
  71.4 2.6 mul.72
  74.0 153.1 %all-reduce.3.cloned.1.call-done = f32[24576]{0:T(1024)} async-done(((f32[24576]{0:T(1024)}), f32[24576]{0:T(1024)}) %all-reduce.3.cloned.1.call-update) | async-done | bytes 98320
  232.6 2.0 collective-permute-start.10
  234.6 1.8 broadcast_select_fusion.7
  237.5 3.6 %fusion.32 = (bf16[2,512,896]{1,2,0:T(8,128)(2,1)S(1)}, bf16[2,512,896]{1,2,0:T(8,128)(2,1)}) fusion(bf16[4,512,896]{1,2,0:T(8,128)(2,1)} %bitcast.19), kind=kLoop, calls=%fused_computation.162 | loop fusion | bytes 7340032 | tf_op jit(solution)/shard_map/slice | solution.py:77
  241.1 3.6 %copy.87 = bf16[2,512,896]{2,1,0:T(8,128)(2,1)} copy(bf16[2,512,896]{1,2,0:T(8,128)(2,1)} %get-tuple-element.3) | data formatting | bytes 3670016 | tf_op jit(solution)/shard_map/slice | solution.py:78
  244.7 2.3 copy.86
  247.0 3.2 fusion.11
  253.0 1.8 broadcast_select_fusion.3
  257.4 1.4 broadcast_select_fusion.5
  262.4 1.5 collective-permute-start.13
  263.8 5.3 %collective-permute-done.16 = bf16[576,1024]{1,0:T(8,128)(2,1)S(1)} collective-permute-done((bf16[576,1024]{1,0:T(8,128)(2,1)}, bf16[576,1024]{1,0:T(8,128)(2,1)S(1)}, u32[]{:S(2)}, u32[]{:S(2)}) %collective-permute-start.16) | collective-permute-done | bytes 1179680 | tf_op jit(solution)/shard_map/ppermute | solution.py:70
  270.4 4.6 %collective-permute-done.14 = bf16[2,4,32,896]{3,2,0,1:T(8,128)(2,1)S(1)} collective-permute-done((bf16[2,4,32,896]{3,2,0,1:T(8,128)(2,1)S(1)}, bf16[2,4,32,896]{3,2,0,1:T(8,128)(2,1)S(1)}, u32[]{:S(2)}, u32[]{:S(2)}) %collective-permute-start.14) | collective-permute-done | bytes 458784 | tf_op jit(solution)/shard_map/ppermute | solution.py:13
  275.0 2.3 collective-permute-done.13
  277.3 8.8 %collective-permute-done.12 = bf16[2,4,32,896]{3,2,0,1:T(8,128)(2,1)S(1)} collective-permute-done((bf16[2,4,32,896]{3,2,0,1:T(8,128)(2,1)S(1)}, bf16[2,4,32,896]{3,2,0,1:T(8,128)(2,1)S(1)}, u32[]{:S(2)}, u32[]{:S(2)}) %collective-permute-start.12) | collective-permute-done | bytes 458784 | tf_op jit(solution)/shard_map/ppermute | solution.py:13
  293.5 9.3 %collective-permute-done.20 = bf16[2,4,32,896]{3,2,0,1:T(8,128)(2,1)S(1)} collective-permute-done((bf16[2,4,32,896]{3,2,0,1:T(8,128)(2,1)S(1)}, bf16[2,4,32,896]{3,2,0,1:T(8,128)(2,1)S(1)}, u32[]{:S(2)}, u32[]{:S(2)}) %collective-permute-start.20) | collective-permute-done | bytes 458784 | tf_op jit(solution)/shard_map/ppermute | solution.py:13
  302.8 2.5 collective-permute-done.19
  305.3 8.1 %collective-permute-done.18 = bf16[2,4,32,896]{3,2,0,1:T(8,128)(2,1)S(1)} collective-permute-done((bf16[2,4,32,896]{3,2,0,1:T(8,128)(2,1)S(1)}, bf16[2,4,32,896]{3,2,0,1:T(8,128)(2,1)S(1)}, u32[]{:S(2)}, u32[]{:S(2)}) %collective-permute-start.18) | collective-permute-done | bytes 458784 | tf_op jit(solution)/shard_map/ppermute | solution.py:13
  313.9 1.5 collective-permute-start.23
  316.7 1.5 collective-permute-start.21
  318.5 9.2 %collective-permute-done.23 = bf16[4,32,896]{2,1,0:T(8,128)(2,1)S(1)} collective-permute-done((bf16[4,32,896]{2,1,0:T(8,128)(2,1)S(1)}, bf16[4,32,896]{2,1,0:T(8,128)(2,1)S(1)}, u32[]{:S(2)}, u32[]{:S(2)}) %collective-permute-start.23) | collective-permute-done | bytes 229408 | tf_op jit(solution)/shard_map/ppermute | solution.py:13
  331.2 9.0 %multiply_convert_fusion.2 = bf16[512,3584]{1,0:T(8,128)(2,1)} fusion(bf16[1024,512]{1,0:T(8,128)(2,1)S(1)} %bitcast.204, bf16[1024,3584]{1,0:T(8,128)(2,1)} %all-gather.3.cloned.1.call-done, f32[1024]{0:T(1024)S(1)} %div.42), kind=kOutput, calls=%fused_computation.2 | convolution fusion | flops 3772776448 | bytes 12062720 | tf_op jit(solution)/shard_map/dot_general | solution.py:146
  (134 shorter events, 37.4 us)
Async XLA Ops:
  8.0 219.1 %all-reduce.3.cloned.1.call-start = ((), (), s32[]{:S(2)}) async-start(), calls=%async_computation.2 | async-start | bytes 196608
  9.1 9.1 %collective-permute-start.3 = (bf16[48,1024]{1,0:T(8,128)(2,1)S(1)}, bf16[48,1024]{1,0:T(8,128)(2,1)S(1)}, u32[]{:S(2)}, u32[]{:S(2)}) collective-permute-start(bf16[48,1024]{1,0:T(8,128)(2,1)S(1)} %get-tuple-element.87), channel_id=1, source_target_pairs={{0,6},{2,38},{4,70},{6,102},{32,0},{34,32},{36,64},{38,96},{64,2},... | collective-permute-start | bytes 294920 | tf_op jit(solution)/shard_map/ppermute | solution.py:40
  13.3 16.9 %collective-permute-start.2 = (bf16[48,1024]{1,0:T(8,128)(2,1)S(1)}, bf16[48,1024]{1,0:T(8,128)(2,1)S(1)}, u32[]{:S(2)}, u32[]{:S(2)}) collective-permute-start(bf16[48,1024]{1,0:T(8,128)(2,1)S(1)} %get-tuple-element.86), channel_id=1, source_target_pairs={{0,4},{2,36},{4,68},{6,100},{32,6},{34,38},{36,70},{38,102},{64,0}... | collective-permute-start | bytes 294920 | tf_op jit(solution)/shard_map/ppermute | solution.py:40
  17.4 14.1 %collective-permute-start.1 = (bf16[48,1024]{1,0:T(8,128)(2,1)S(1)}, bf16[48,1024]{1,0:T(8,128)(2,1)S(1)}, u32[]{:S(2)}, u32[]{:S(2)}) collective-permute-start(bf16[48,1024]{1,0:T(8,128)(2,1)S(1)} %get-tuple-element.85), channel_id=1, source_target_pairs={{0,2},{2,34},{4,66},{6,98},{32,4},{34,36},{36,68},{38,100},{64,6},... | collective-permute-start | bytes 294920 | tf_op jit(solution)/shard_map/ppermute | solution.py:40
  17.4 14.1 %collective-permute-start = (bf16[48,1024]{1,0:T(8,128)(2,1)S(1)}, bf16[48,1024]{1,0:T(8,128)(2,1)S(1)}, u32[]{:S(2)}, u32[]{:S(2)}) collective-permute-start(bf16[48,1024]{1,0:T(8,128)(2,1)S(1)} %get-tuple-element.84), channel_id=1, source_target_pairs={{0,0},{2,32},{4,64},{6,96},{32,2},{34,34},{36,66},{38,98},{64,4},{... | collective-permute-start | bytes 294920 | tf_op jit(solution)/shard_map/ppermute | solution.py:40
  31.5 4.8 %copy-start.5 = (bf16[128,1024]{1,0:T(8,128)(2,1)S(1)}, bf16[128,1024]{1,0:T(8,128)(2,1)}, u32[]{:S(2)}) copy-start(bf16[128,1024]{1,0:T(8,128)(2,1)} %param.5) | copy-start | bytes 786436
  31.6 4.9 %copy-start.7 = (bf16[64,1024]{1,0:T(8,128)(2,1)S(1)}, bf16[64,1024]{1,0:T(8,128)(2,1)}, u32[]{:S(2)}) copy-start(bf16[64,1024]{1,0:T(8,128)(2,1)} %param.7) | copy-start | bytes 393220
  31.8 16.6 %collective-permute-start.6 = (bf16[160,1024]{1,0:T(8,128)(2,1)S(1)}, bf16[160,1024]{1,0:T(8,128)(2,1)S(1)}, u32[]{:S(2)}, u32[]{:S(2)}) collective-permute-start(bf16[160,1024]{1,0:T(8,128)(2,1)S(1)} %get-tuple-element.93), channel_id=1, source_target_pairs={{0,24},{8,0},{16,8},{24,16},{1,25},{9,1},{17,9},{25,17},{2,26},{10... | collective-permute-start | bytes 983048 | tf_op jit(solution)/shard_map/ppermute | solution.py:13
  34.7 13.8 %collective-permute-start.5 = (bf16[160,1024]{1,0:T(8,128)(2,1)S(1)}, bf16[160,1024]{1,0:T(8,128)(2,1)S(1)}, u32[]{:S(2)}, u32[]{:S(2)}) collective-permute-start(bf16[160,1024]{1,0:T(8,128)(2,1)S(1)} %get-tuple-element.92), channel_id=1, source_target_pairs={{0,16},{8,24},{16,0},{24,8},{1,17},{9,25},{17,1},{25,9},{2,18},{10... | collective-permute-start | bytes 983048 | tf_op jit(solution)/shard_map/ppermute | solution.py:13
  35.5 16.6 %collective-permute-start.4 = (bf16[160,1024]{1,0:T(8,128)(2,1)S(1)}, bf16[160,1024]{1,0:T(8,128)(2,1)S(1)}, u32[]{:S(2)}, u32[]{:S(2)}) collective-permute-start(bf16[160,1024]{1,0:T(8,128)(2,1)S(1)} %get-tuple-element.91), channel_id=1, source_target_pairs={{0,8},{8,16},{16,24},{24,0},{1,9},{9,17},{17,25},{25,1},{2,10},{10... | collective-permute-start | bytes 983048 | tf_op jit(solution)/shard_map/ppermute | solution.py:13
  36.5 15.8 %copy-start.8 = (f32[64]{0:T(128)S(1)}, f32[64]{0:T(128)}, u32[]{:S(2)}) copy-start(f32[64]{0:T(128)} %param.9) | copy-start | bytes 772
  52.1 12.6 %collective-permute-start.7 = (bf16[4,64,512]{2,1,0:T(8,128)(2,1)S(1)}, bf16[4,64,512]{2,1,0:T(8,128)(2,1)S(1)}, u32[]{:S(2)}, u32[]{:S(2)}) collective-permute-start(bf16[4,64,512]{2,1,0:T(8,128)(2,1)S(1)} %fusion.21), channel_id=1, source_target_pairs={{0,1},{1,0},{2,3},{3,2},{4,5},{5,4},{6,7},{7,6},{8,9},{9,8},{10,11... | collective-permute-start | bytes 786440 | tf_op jit(solution)/shard_map/ppermute | solution.py:60
  59.0 178.5 %all-to-all-start = ((bf16[512,4,896]{0,2,1:T(8,128)(2,1)}), bf16[512,4,896]{0,2,1:T(8,128)(2,1)}, u32[]{:S(2)}, u32[]{:S(2)}) async-start(bf16[512,4,896]{0,2,1:T(8,128)(2,1)} %bitcast.181), calls=%async_computation | async-start | bytes 7340032 | tf_op jit(solution)/shard_map/all_to_all | solution.py:30
  63.8 267.4 %all-gather.3.cloned.1.call-start = ((), (), s32[]{:S(2)}) async-start(), calls=%async_computation.1 | async-start | bytes 7798784 | tf_op jit(solution)/shard_map/all_gather | solution.py:28
  64.8 6.2 %copy-start.3 = (bf16[64,3584]{1,0:T(8,128)(2,1)S(1)}, bf16[64,3584]{1,0:T(8,128)(2,1)}, u32[]{:S(2)}) copy-start(bf16[64,3584]{1,0:T(8,128)(2,1)} %param.8) | copy-start | bytes 1376260
  66.0 165.9 %collective-permute-start.9 = (bf16[576,1024]{1,0:T(8,128)(2,1)}, bf16[576,1024]{1,0:T(8,128)(2,1)}, u32[]{:S(2)}, u32[]{:S(2)}) collective-permute-start(bf16[576,1024]{1,0:T(8,128)(2,1)} %maximum_maximum_fusion), channel_id=1, source_target_pairs={{0,2},{2,4},{4,6},{6,0},{1,7},{3,1},{5,3},{7,5},{8,10},{10,12},{12... | collective-permute-start | bytes 3538952 | tf_op jit(solution)/shard_map/ppermute | solution.py:70
  68.2 166.3 %collective-permute-start.8 = (bf16[576,1024]{1,0:T(8,128)(2,1)}, bf16[576,1024]{1,0:T(8,128)(2,1)}, u32[]{:S(2)}, u32[]{:S(2)}) collective-permute-start(bf16[576,1024]{1,0:T(8,128)(2,1)} %maximum_maximum_fusion), channel_id=1, source_target_pairs={{0,1},{1,0},{2,3},{3,2},{4,5},{5,4},{6,7},{7,6},{8,9},{9,8},{10,11... | collective-permute-start | bytes 3538952 | tf_op jit(solution)/shard_map/ppermute | solution.py:71
  231.8 21.2 %collective-permute-start.15 = (bf16[576,1024]{1,0:T(8,128)(2,1)}, bf16[576,1024]{1,0:T(8,128)(2,1)}, u32[]{:S(2)}, u32[]{:S(2)}) collective-permute-start(bf16[576,1024]{1,0:T(8,128)(2,1)} %collective-permute-done.9), channel_id=1, source_target_pairs={{0,1},{1,0},{2,3},{3,2},{4,5},{5,4},{6,7},{7,6},{8,9},{9,8},{10,11... | collective-permute-start | bytes 3538952 | tf_op jit(solution)/shard_map/ppermute | solution.py:71
  232.6 18.9 %collective-permute-start.10 = (bf16[576,1024]{1,0:T(8,128)(2,1)}, bf16[576,1024]{1,0:T(8,128)(2,1)}, u32[]{:S(2)}, u32[]{:S(2)}) collective-permute-start(bf16[576,1024]{1,0:T(8,128)(2,1)} %collective-permute-done.9), channel_id=1, source_target_pairs={{0,2},{2,4},{4,6},{6,0},{1,7},{3,1},{5,3},{7,5},{8,10},{10,12},{12... | collective-permute-start | bytes 3538952 | tf_op jit(solution)/shard_map/ppermute | solution.py:70
  251.5 3.4 copy-start.1
  251.5 17.7 %collective-permute-start.16 = (bf16[576,1024]{1,0:T(8,128)(2,1)}, bf16[576,1024]{1,0:T(8,128)(2,1)S(1)}, u32[]{:S(2)}, u32[]{:S(2)}) collective-permute-start(bf16[576,1024]{1,0:T(8,128)(2,1)} %collective-permute-done.10), channel_id=1, source_target_pairs={{0,2},{2,4},{4,6},{6,0},{1,7},{3,1},{5,3},{7,5},{8,10},{10,12},{12... | collective-permute-start | bytes 3538952 | tf_op jit(solution)/shard_map/ppermute | solution.py:70
  252.8 4.7 %collective-permute-start.11 = (bf16[576,1024]{1,0:T(8,128)(2,1)}, bf16[576,1024]{1,0:T(8,128)(2,1)S(1)}, u32[]{:S(2)}, u32[]{:S(2)}) collective-permute-start(bf16[576,1024]{1,0:T(8,128)(2,1)} %collective-permute-done.10), channel_id=1, source_target_pairs={{0,1},{1,0},{2,3},{3,2},{4,5},{5,4},{6,7},{7,6},{8,9},{9,8},{10,11... | collective-permute-start | bytes 3538952 | tf_op jit(solution)/shard_map/ppermute | solution.py:71
  261.6 13.4 %collective-permute-start.14 = (bf16[2,4,32,896]{3,2,0,1:T(8,128)(2,1)S(1)}, bf16[2,4,32,896]{3,2,0,1:T(8,128)(2,1)S(1)}, u32[]{:S(2)}, u32[]{:S(2)}) collective-permute-start(bf16[2,4,32,896]{3,2,0,1:T(8,128)(2,1)S(1)} %pad_maximum_fusion.10), channel_id=1, source_target_pairs={{0,96},{32,0},{64,32},{96,64},{1,97},{33,1},{65,33},{97,65},{2,98}... | collective-permute-start | bytes 1376264 | tf_op jit(solution)/shard_map/ppermute | solution.py:13
  262.4 15.0 %collective-permute-start.13 = (bf16[2,4,32,896]{3,2,0,1:T(8,128)(2,1)S(1)}, bf16[2,4,32,896]{3,2,0,1:T(8,128)(2,1)S(1)}, u32[]{:S(2)}, u32[]{:S(2)}) collective-permute-start(bf16[2,4,32,896]{3,2,0,1:T(8,128)(2,1)S(1)} %pad_maximum_fusion.9), channel_id=1, source_target_pairs={{0,64},{32,96},{64,0},{96,32},{1,65},{33,97},{65,1},{97,33},{2,66}... | collective-permute-start | bytes 1376264 | tf_op jit(solution)/shard_map/ppermute | solution.py:13
  269.2 17.2 %collective-permute-start.17 = (bf16[576,1024]{1,0:T(8,128)(2,1)S(1)}, bf16[576,1024]{1,0:T(8,128)(2,1)S(1)}, u32[]{:S(2)}, u32[]{:S(2)}) collective-permute-start(bf16[576,1024]{1,0:T(8,128)(2,1)S(1)} %collective-permute-done.16), channel_id=1, source_target_pairs={{0,1},{1,0},{2,3},{3,2},{4,5},{5,4},{6,7},{7,6},{8,9},{9,8},{10,11... | collective-permute-start | bytes 3538952 | tf_op jit(solution)/shard_map/ppermute | solution.py:71
  269.2 16.9 %collective-permute-start.12 = (bf16[2,4,32,896]{3,2,0,1:T(8,128)(2,1)S(1)}, bf16[2,4,32,896]{3,2,0,1:T(8,128)(2,1)S(1)}, u32[]{:S(2)}, u32[]{:S(2)}) collective-permute-start(bf16[2,4,32,896]{3,2,0,1:T(8,128)(2,1)S(1)} %pad_maximum_fusion.8), channel_id=1, source_target_pairs={{0,32},{32,64},{64,96},{96,0},{1,33},{33,65},{65,97},{97,1},{2,34}... | collective-permute-start | bytes 1376264 | tf_op jit(solution)/shard_map/ppermute | solution.py:13
  289.4 13.4 %collective-permute-start.20 = (bf16[2,4,32,896]{3,2,0,1:T(8,128)(2,1)S(1)}, bf16[2,4,32,896]{3,2,0,1:T(8,128)(2,1)S(1)}, u32[]{:S(2)}, u32[]{:S(2)}) collective-permute-start(bf16[2,4,32,896]{3,2,0,1:T(8,128)(2,1)S(1)} %pad_maximum_fusion.13), channel_id=1, source_target_pairs={{0,96},{32,0},{64,32},{96,64},{1,97},{33,1},{65,33},{97,65},{2,98}... | collective-permute-start | bytes 1376264 | tf_op jit(solution)/shard_map/ppermute | solution.py:13
  290.2 15.1 %collective-permute-start.19 = (bf16[2,4,32,896]{3,2,0,1:T(8,128)(2,1)S(1)}, bf16[2,4,32,896]{3,2,0,1:T(8,128)(2,1)S(1)}, u32[]{:S(2)}, u32[]{:S(2)}) collective-permute-start(bf16[2,4,32,896]{3,2,0,1:T(8,128)(2,1)S(1)} %pad_maximum_fusion.12), channel_id=1, source_target_pairs={{0,64},{32,96},{64,0},{96,32},{1,65},{33,97},{65,1},{97,33},{2,66}... | collective-permute-start | bytes 1376264 | tf_op jit(solution)/shard_map/ppermute | solution.py:13
  291.6 21.8 %collective-permute-start.18 = (bf16[2,4,32,896]{3,2,0,1:T(8,128)(2,1)S(1)}, bf16[2,4,32,896]{3,2,0,1:T(8,128)(2,1)S(1)}, u32[]{:S(2)}, u32[]{:S(2)}) collective-permute-start(bf16[2,4,32,896]{3,2,0,1:T(8,128)(2,1)S(1)} %pad_maximum_fusion.11), channel_id=1, source_target_pairs={{0,32},{32,64},{64,96},{96,0},{1,33},{33,65},{65,97},{97,1},{2,34}... | collective-permute-start | bytes 1376264 | tf_op jit(solution)/shard_map/ppermute | solution.py:13
  313.9 13.7 %collective-permute-start.23 = (bf16[4,32,896]{2,1,0:T(8,128)(2,1)S(1)}, bf16[4,32,896]{2,1,0:T(8,128)(2,1)S(1)}, u32[]{:S(2)}, u32[]{:S(2)}) collective-permute-start(bf16[4,32,896]{2,1,0:T(8,128)(2,1)S(1)} %get-tuple-element.61), channel_id=1, source_target_pairs={{0,8},{8,16},{16,24},{24,0},{1,9},{9,17},{17,25},{25,1},{2,10},{10... | collective-permute-start | bytes 688136 | tf_op jit(solution)/shard_map/ppermute | solution.py:13
  315.4 12.3 %collective-permute-start.22 = (bf16[4,32,896]{2,1,0:T(8,128)(2,1)S(1)}, bf16[4,32,896]{2,1,0:T(8,128)(2,1)S(1)}, u32[]{:S(2)}, u32[]{:S(2)}) collective-permute-start(bf16[4,32,896]{2,1,0:T(8,128)(2,1)S(1)} %get-tuple-element.62), channel_id=1, source_target_pairs={{0,16},{8,24},{16,0},{24,8},{1,17},{9,25},{17,1},{25,9},{2,18},{10... | collective-permute-start | bytes 688136 | tf_op jit(solution)/shard_map/ppermute | solution.py:13
  316.7 11.5 %collective-permute-start.21 = (bf16[4,32,896]{2,1,0:T(8,128)(2,1)S(1)}, bf16[4,32,896]{2,1,0:T(8,128)(2,1)S(1)}, u32[]{:S(2)}, u32[]{:S(2)}) collective-permute-start(bf16[4,32,896]{2,1,0:T(8,128)(2,1)S(1)} %get-tuple-element.63), channel_id=1, source_target_pairs={{0,24},{8,0},{16,8},{24,16},{1,25},{9,1},{17,9},{25,17},{2,26},{10... | collective-permute-start | bytes 688136 | tf_op jit(solution)/shard_map/ppermute | solution.py:13
  (4 other events, 6.4 us)
Sparse Core Ops, SparseCore 0:
  53.2 173.8 all-reduce.2
Sparse Core Ops, SparseCore 1:
  66.7 86.5 all-gather.2

commit v2 on v0

v2 whole, which is shorter than its diff:
```python
import math

import jax
import jax.numpy as jnp
from jax import lax
from jax.experimental import pallas as pl
from jax.experimental.pallas import tpu as pltpu
from jax.sharding import Mesh, PartitionSpec as P

noise_scale = 0.5
epsilon = 1e-05
F32, BF16 = jnp.float32, jnp.bfloat16
VMEM = 48 * 2**20
SWAP = [(0, 1), (1, 0)]


def shift(value, axis, by):
    return lax.ppermute(value, axis, [(i, (i + by) % 4) for i in range(4)])


def apart(value, axis, up, down):
    perm = [(2 * i, 2 * ((i + up) % 4)) for i in range(4)]
    perm += [(2 * i + 1, 2 * ((i + down) % 4) + 1) for i in range(4)]
    return lax.ppermute(value, (axis, "c"), perm)


def after(value, *others):
    return lax.optimization_barrier((value, *others))[0]


def together(*values):
    return lax.optimization_barrier(values)


def pick(value, index):
    return lax.dynamic_index_in_dim(value, index, 0, keepdims=False)


def whole(shape):
    return pl.BlockSpec(shape, lambda i, s: (0,) * len(shape))


def base_kernel(s_ref, own0, other0, own1, other1, mine, near, far, across0, across1, *out_refs):
    nx, _, rows, _ = out_refs[0].shape
    ny = len(out_refs)
    depth = mine.shape[0]
    x, c = s_ref[1], s_ref[3]
    away = jnp.where(c == 0, 1, -1)
    low = depth // 2
    for k, (own, other) in enumerate(((own0, other0), (own1, other1))):
        total = None
        for piece, by, skip in (
            (mine, 0, 0), (near, -away, 0), (far, away, 0), (across0, 2, 0), (across1, 2, low)
        ):
            block = lax.rem(x + by + 4, 4)
            at = pl.ds(pl.multiple_of(lax.rem(block, 2) * depth + skip, 128), piece.shape[0])
            tok = jnp.where(lax.div(block, 2) == c, own[:, at], other[:, at])
            term = jnp.dot(tok, piece[...], preferred_element_type=F32)
            total = term if total is None else total + term
        total = total.astype(BF16)
        for d in range(nx):
            parts = [total[(d * ny + s) * rows : (d * ny + s + 1) * rows] for s in range(ny)]
            out_refs[0][d, k] = jnp.where(c == 0, parts[1], parts[3])
            out_refs[1][d, k] = parts[2]
            out_refs[2][d, k] = jnp.where(c == 0, parts[3], parts[1])
            out_refs[3][d, k] = parts[0]


def base_part(place, own0, other0, own1, other1, weight, moved):
    depth, cols = moved[0].shape
    height, width = own0.shape
    rows = height // 16
    return pl.pallas_call(
        base_kernel,
        grid_spec=pltpu.PrefetchScalarGridSpec(
            num_scalar_prefetch=1,
            grid=(1,),
            in_specs=[whole((height, width))] * 4
            + [pl.BlockSpec((depth, cols), lambda i, s: (0, s[1]))]
            + [whole(m.shape) for m in moved],
            out_specs=[whole((4, 2, rows, cols))] * 4,
        ),
        out_shape=[jax.ShapeDtypeStruct((4, 2, rows, cols), BF16)] * 4,
        compiler_params=pltpu.CompilerParams(vmem_limit_bytes=VMEM),
        cost_estimate=pl.CostEstimate(
            flops=16 * height * depth * cols,
            bytes_accessed=16 * height * depth + 4 * height * cols + 8 * depth * cols,
            transcendentals=0,
        ),
        name="base",
    )(place, own0, other0, own1, other1, weight, *moved)


def output_kernel(s_ref, sums_ref, probe_ref, right_ref, out_ref):
    z, c = s_ref[2], s_ref[3]
    rows = sums_ref.shape[2]
    members = right_ref.shape[0]
    row = lax.broadcasted_iota(jnp.int32, (2 * members, members), 0)
    member = lax.broadcasted_iota(jnp.int32, (2 * members, members), 1)
    twice = jnp.where(lax.div(row, 2) == member, 1.0, 0.0).astype(BF16)
    right = jnp.dot(twice, right_ref[...], preferred_element_type=F32)
    for zz in range(4):
        k = lax.rem(jnp.where(c == 0, z - zz, zz - z) + 4, 4)
        at = slice(zz * rows, (zz + 1) * rows)
        out = sums_ref[0, lax.rem(k, 2) * 2 + lax.div(k, 2)].astype(F32)
        out_ref[at] = (out + probe_ref[at] * right[at]).astype(BF16)


def output_part(place, sums, probe, right):
    _, _, rows, cols = sums.shape
    members = right.shape[0]
    return pl.pallas_call(
        output_kernel,
        grid_spec=pltpu.PrefetchScalarGridSpec(
            num_scalar_prefetch=1,
            grid=(4,),
            in_specs=[
                pl.BlockSpec((1, 4, rows, cols), lambda i, s: (lax.rem(i - s[1] + 4, 4), 0, 0, 0)),
                whole((4 * rows, 1)),
                pl.BlockSpec((members, cols), lambda i, s: (0, i)),
            ],
            out_specs=pl.BlockSpec((4 * rows, cols), lambda i, s: (0, i)),
        ),
        out_shape=jax.ShapeDtypeStruct((4 * rows, 4 * cols), BF16),
        compiler_params=pltpu.CompilerParams(vmem_limit_bytes=VMEM),
        name="outputs",
    )(place, sums, probe, right)


def update_kernel(s_ref, left0, left1, left2, left3, left_other, *refs):
    rights, fits = refs[:4], refs[4:8]
    out_ref, ordered, turned, scores = refs[-4:]
    population, cols = ordered.shape
    depth = population // 4

    @pl.when(pl.program_id(0) == 0)
    def _():
        z, c = s_ref[2], s_ref[3]
        count = population // 64
        for k, left in enumerate((left0, left1, left2, left3)):
            zz = lax.rem(jnp.where(c == 0, z - k, z + k) + 4, 4)
            for p in range(2):
                first = 2 * (c if p == 0 else 1 - c)
                for dd in range(2):
                    d = first + dd
                    d = jnp.where(c == 0, d, lax.rem(4 - d, 4))
                    for s in range(4):
                        slot = d * 4 + jnp.where(c == 0, s, -s % 4)
                        at = pl.multiple_of((slot * 4 + zz) * count, count)
                        rows, lanes = slice(s * count, (s + 1) * count), slice(dd * cols, (dd + 1) * cols)
                        ordered[pl.ds(at, count)] = left[rows, lanes] if p == 0 else left_other[-k % 4, rows, lanes]
        turned[...] = ordered[...].T
        fit = jnp.concatenate([f[...].astype(F32) for f in fits], axis=0)
        fit = fit[:, 0:1] + fit[:, 1:2] + fit[:, 2:3]
        mean = jnp.sum(fit, axis=0, keepdims=True) / population
        centred = fit - mean
        spread = jnp.sum(centred * centred, axis=0, keepdims=True) / population
        scores[...] = centred / jnp.sqrt(spread + epsilon)

    total = jnp.zeros(out_ref.shape, F32)
    for i in range(4):
        at = slice(i * depth, (i + 1) * depth)
        weighted = (scores[at] * rights[i][...].astype(F32)).astype(BF16)
        total += jnp.dot(turned[:, at], weighted, preferred_element_type=F32)
    out_ref[...] = (total * (1.0 / math.sqrt(population))).astype(BF16)


def update_part(place, left, left_other, rights, fits, fit_at, out_cols, first, cols, so_far=None):
    block = rights[0].shape[0]
    population = 4 * block
    depth = left[0].shape[1] // 2
    tile = 512
    extra = [] if so_far is None else [so_far]
    inputs = [*left, left_other, *rights, *fits, *extra]
    return pl.pallas_call(
        update_kernel,
        grid_spec=pltpu.PrefetchScalarGridSpec(
            num_scalar_prefetch=1,
            grid=(cols // tile,),
            in_specs=[whole(left[0].shape)] * 4
            + [whole(left_other.shape)]
            + [pl.BlockSpec((block, tile), lambda i, s: (0, i))] * 4
            + [pl.BlockSpec((block, 128), lambda i, s: (0, fit_at // 128))] * 4
            + [pl.BlockSpec(memory_space=pl.ANY)] * len(extra),
            out_specs=pl.BlockSpec((depth, tile), lambda i, s: (0, i + first // tile)),
            scratch_shapes=[
                pltpu.VMEM((population, depth), BF16),
                pltpu.VMEM((depth, population), BF16),
                pltpu.VMEM((population, 1), F32),
            ],
        ),
        out_shape=jax.ShapeDtypeStruct((depth, out_cols), BF16),
        input_output_aliases={len(inputs): 0} if extra else {},
        compiler_params=pltpu.CompilerParams(vmem_limit_bytes=VMEM),
        cost_estimate=pl.CostEstimate(
            flops=2 * population * depth * cols,
            bytes_accessed=2 * (population * (cols + depth) + depth * cols),
            transcendentals=0,
        ),
        name="update",
    )(place, *inputs)


def pieces(value):
    out = []
    for _ in range(3):
        top = lax.reduce_precision(value, 8, 7)
        out.append(top.astype(BF16))
        value = value - top
    return out


def body(tokens, weight, left_factors, right_factors, fitness):
    y, x, z, c = (lax.axis_index(name) for name in ("y", "x", "z", "c"))
    place = jnp.stack([y, x, z, c]).astype(jnp.int32)
    members, width = left_factors.shape
    depth, out_cols = weight.shape
    quarter = out_cols // 4
    features = width * 8
    population = members * 16
    rows = tokens.shape[0] // 4

    half = width // 2

    first = 4 * (out_cols // 7)
    beside = jnp.stack(pieces(fitness), axis=1)
    beside = jnp.pad(beside, ((0, 0), (0, 128 - beside.shape[1])))
    right = [jnp.concatenate([right_factors[:, :first], beside, right_factors[:, first:]], axis=1)]

    away = jnp.where(c == 0, 1, -1)

    def cols_of(source, xx):
        return lax.dynamic_slice_in_dim(source, (xx % 4) * quarter, quarter, 1)

    both = jnp.concatenate(
        [tokens.reshape(4, rows, width), left_factors.reshape(4, members // 4, width)], axis=1
    )
    own = pick(both, z)
    by_z = [own] + [shift(pick(both, (z + d) % 4), "z", d) for d in range(1, 4)]
    by_z = jnp.stack(by_z)
    near = apart(cols_of(after(weight, own), x + away), "x", 1, -1)
    by_z, weight, right[0] = together(by_z, weight, right[0])

    by_y = [pick(by_z, (z - y) % 4)] + [shift(pick(by_z, (z - y - d) % 4), "y", d) for d in range(1, 4)]
    by_y = jnp.stack(by_y)
    far = apart(cols_of(weight, x - away), "x", -1, 1)
    by_y, near, weight, right[0] = together(by_y, near, weight, right[0])

    tok_y = by_y[:, :rows].reshape(4 * rows, width)
    left_y = by_y[:, rows:].reshape(members, width)

    def left_for(xx):
        cols = lax.dynamic_slice_in_dim(left_y, (xx % 2) * half, half, 1)
        return jnp.concatenate([cols[: members // 2], cols[members // 2 :]], axis=1)

    slots = []
    for d in range(4):
        sent = jnp.concatenate([tok_y, left_for((x + d) % 4)], axis=0)
        slots.append(sent if d == 0 else shift(sent, "x", d))
    slots = jnp.stack(slots)
    right.append(apart(right[-1], "y", 1, -1))
    share = jnp.einsum(
        "mtd,md->mt", tokens.reshape(members, 2, width), left_factors, preferred_element_type=F32
    ).reshape(1, 2 * members)
    slots, far, share, right[1], weight = together(slots, far, share, right[1], weight)

    held = [slots[:, : 4 * rows].reshape(16 * rows, width)]
    held.append(apart(held[0], "z", 1, -1))
    other = [lax.ppermute(held[0], "c", SWAP)]
    across = cols_of(weight, x + 2)
    across = [apart(across[: depth // 2], "x", 2, 2), across[depth // 2 :]]
    right.append(apart(right[-1], "y", 1, -1))
    left_x = slots[:, 4 * rows :]
    left_x = jnp.concatenate([left_x[..., :half], left_x[..., half:]], axis=1)
    left_x = jnp.where(c == x // 2, left_x, lax.ppermute(left_x, "c", SWAP))
    mine = lax.dynamic_slice_in_dim(left_x, c * 2, 2, 0)
    below = jnp.concatenate(pieces(share), axis=1)
    below = jnp.pad(below, ((0, 15), (0, width - below.shape[1])))
    left = [jnp.concatenate([jnp.concatenate([mine[0], mine[1]], axis=1), below], axis=0)]
    held[1], other[0], across[0], across[1], right[2], left[0] = together(
        held[1], other[0], across[0], across[1], right[2], left[0]
    )

    held.append(apart(held[1], "z", 1, -1))
    other.append(lax.ppermute(held[1], "c", SWAP))
    across[1] = apart(across[1], "x", 2, 2)
    right.append(apart(right[-1], "y", 1, -1))
    left.append(apart(left[0], "z", 1, -1))
    held[2], other[1], across[1], right[3], left[1] = together(held[2], other[1], across[1], right[3], left[1])

    held.append(apart(held[2], "z", 1, -1))
    other.append(lax.ppermute(held[2], "c", SWAP))
    right = jnp.concatenate(right, axis=0)
    right_a, right_b = [right[:, : first + 128]], [right[:, first + 128 :]]
    right_a.append(apart(right_a[-1], "x", 1, -1))
    right_b.append(apart(right_b[-1], "x", 1, -1))
    left.append(apart(left[1], "z", 1, -1))
    moved = [near, far, *across]
    part_a = base_part(place, held[0], other[0], held[2], other[2], weight, moved)
    held[3] = after(held[3], part_a[0])
    right_a[1] = after(right_a[1], part_a[0])
    right_b[1] = after(right_b[1], part_a[0])
    other.append(lax.ppermute(held[3], "c", SWAP))
    right_a.append(apart(right_a[-1], "x", 1, -1))
    right_b.append(apart(right_b[-1], "x", 1, -1))

    part_b = base_part(place, held[1], other[3], held[3], other[1], weight, moved)
    right_a[2] = after(right_a[2], part_b[0])
    right_b[2] = after(right_b[2], part_b[0])
    right_a.append(apart(right_a[-1], "x", 1, -1))
    right_b.append(apart(right_b[-1], "x", 1, -1))
    left[2] = after(left[2], part_b[0])
    left.append(apart(left[2], "z", 1, -1))

    def onward(total, part):
        return (apart(total, "y", 1, -1).astype(F32) + part.astype(F32)).astype(BF16)

    def across_x(total):
        return jnp.stack([total[0]] + [shift(total[d], "x", -d) for d in range(1, 4)])

    sum_a = onward(part_a[0], part_a[1])
    sum_b = onward(part_b[0], part_b[1])
    sum_a = onward(sum_a, part_a[2])
    sum_b = onward(sum_b, part_b[2])
    sum_a = onward(sum_a, part_a[3])
    left[3], sum_a = together(left[3], sum_a)
    columns_a = across_x(sum_a)
    left_other = lax.ppermute(jnp.stack(left), "c", SWAP)
    sum_b = after(onward(sum_b, part_b[3]), columns_a, left_other)
    columns = jnp.concatenate([columns_a, across_x(sum_b)], axis=1)

    shares = jnp.stack([v[members, : 6 * members] for v in left])
    shares = jnp.concatenate([shares, left_other[:, members, : 6 * members]]).astype(F32)
    share = jnp.sum(shares, axis=0).reshape(3, 2 * members)
    probe = jnp.sum(share, axis=0).reshape(2 * members, 1) * (noise_scale / math.sqrt(features))
    outputs = output_part(place, columns, probe, right_factors)
    update = update_part(place, left, left_other, right_a, right_a, first, out_cols, 0, first)
    update = update_part(place, left, left_other, right_b, right_a, first, out_cols, first, out_cols - first, update)
    return outputs, update


def solution(mesh):
    grid = Mesh(mesh.devices.reshape(4, 4, 4, 2), ("y", "x", "z", "c"))
    spec = P(("y", "x"), ("z", "c"))
    return jax.shard_map(
        body,
        mesh=grid,
        in_specs=(spec, spec, spec, spec, P(("y", "x"))),
        out_specs=(spec, spec),
        check_vma=False,
    )
```

time: 325 us -> 192 us (0.59)
  blocking collectives: 120 us -> 0 us
  starting transfers between devices: 4.49 us -> 41.2 us
  Pallas kernels: 0 us -> 30.2 us
  matrix products: 31.4 us -> 1.6 us
  waiting for transfers between devices: 121 us -> 92.1 us
  between operations: 17.1 us -> 1.54 us
  local copies, waits for them, and re-layouts: 26 us -> 17.2 us
  other arithmetic: 3.42 us -> 7.78 us
    ppermute x0 -> x46, waiting for transfers between devices: none -> 92.1 us  [the longest x25 77.6 us: apart(): return lax.ppermute(value, (axis, 'c'), perm)]
    reduce_scatter x1 -> x0, waiting for transfers between devices: 91.7 us -> none  [body(): lax.psum_scatter(jnp.dot(spread_rows, weight, preferred_element_type=jnp....]
    unnamed x1 -> x0, blocking collectives: 46.9 us -> none
    ppermute x0 -> x46, starting transfers between devices: none -> 41.2 us  [the longest x15 24.7 us: shift(): return lax.ppermute(value, axis, [(i, (i + by) % 4) for i in range(4)])]
    psum x1 -> x0, blocking collectives: 37.9 us -> none  [body(): lax.psum((jnp.sum(fitness), jnp.sum(fitness * fitness)), 'row')]
    all_to_all x1 -> x0, blocking collectives: 35.6 us -> none  [body(): lax.all_to_all(rows_full, 'row', split_axis=1, concat_axis=0, tiled=True)]
    pallas_call x0 -> x5, Pallas kernels: none -> 30.2 us  [the longest x2 14.4 us: base_part(): pl.pallas_call(base_kernel, grid_spec=pltpu.PrefetchScalarGridSpec(num_sc...]
    dot_general x3 -> x1, matrix products: 31.4 us -> 1.6 us  [body(): jnp.einsum('mtd,md->mt', tokens.reshape(members, 2, width), left_factors,...]
  transfers between devices with their start and end apart: 5 -> 46, of which waited for: 2 -> 16; matrix products, arithmetic and copies ran while one was open for 17% -> 8% of each run, Pallas kernels for 0% -> 14%
where the time goes in v2:
time: 192 us
  waiting for transfers between devices  92.1 us (48%)
  starting transfers between devices  41.2 us (21%)
  Pallas kernels  30.2 us (16%)
  local copies, waits for them, and re-layouts  17.2 us (9%)
  other arithmetic  7.78 us (4%)
    ppermute x25, waiting for transfers between devices, apart(): return lax.ppermute(value, (axis, 'c'), perm)  77.6 us
    ppermute x15, starting transfers between devices, shift(): return lax.ppermute(value, axis, [(i, (i + by) % 4) for i in range(4)])  24.7 us
    ppermute x25, starting transfers between devices, apart(): return lax.ppermute(value, (axis, 'c'), perm)  15.9 us
    pallas_call x2, Pallas kernels, base_part(): pl.pallas_call(base_kernel, grid_spec=pltpu.PrefetchScalarGridSpec(num_sc...  14.4 us
    pallas_call x2, Pallas kernels, update_part(): pl.pallas_call(update_kernel, grid_spec=pltpu.PrefetchScalarGridSpec(num_...  13.2 us
    ppermute x15, waiting for transfers between devices, shift(): return lax.ppermute(value, axis, [(i, (i + by) % 4) for i in range(4)])  12.9 us
    unnamed x72, local copies, waits for them, and re-layouts  8.52 us
    dynamic_slice x2, local copies, waits for them, and re-layouts, cols_of(): return lax.dynamic_slice_in_dim(source, xx % 4 * quarter, quarter, 1)  4.35 us
  transfers between devices with their start and end apart: 46, of which 16 were waited for; matrix products, arithmetic and copies ran while one was open for 8% of the time, Pallas kernels for 14%

profile of v2, /device:TPU:0, one launch (start us, length us, event | category | flops | bytes accessed | tf_op | source)
XLA Modules:
  0.0 191.6 jit_solution(5650103567901558279)
XLA Ops:
  1.8 2.1 %collective-permute-start = (bf16[48,1024]{1,0:T(8,128)(2,1)S(1)}, bf16[48,1024]{1,0:T(8,128)(2,1)S(1)}, u32[]{:S(2)}, u32[]{:S(2)}) collective-permute-start(bf16[48,1024]{1,0:T(8,128)(2,1)S(1)} %get-tuple-element.99), channel_id=1, source_target_pairs={{0,2},{2,4},{4,6},{6,0},{1,3},{3,5},{5,7},{7,1},{8,10},{10,12},{12... | collective-permute-start | bytes 294920 | tf_op jit(solution)/shard_map/ppermute | solution.py:18
  3.8 3.6 %collective-permute-start.1 = (bf16[48,1024]{1,0:T(8,128)(2,1)S(1)}, bf16[48,1024]{1,0:T(8,128)(2,1)S(1)}, u32[]{:S(2)}, u32[]{:S(2)}) collective-permute-start(bf16[48,1024]{1,0:T(8,128)(2,1)S(1)} %get-tuple-element.100), channel_id=1, source_target_pairs={{0,4},{2,6},{4,0},{6,2},{1,5},{3,7},{5,1},{7,3},{8,12},{10,14},{12... | collective-permute-start | bytes 294920 | tf_op jit(solution)/shard_map/ppermute | solution.py:18
  8.4 2.2 %constant_dynamic-slice_fusion.4 = bf16[512,896]{1,0:T(8,128)(2,1)} fusion(bf16[512,3584]{1,0:T(8,128)(2,1)} %mine.1, s32[]{:T(128)S(6)} %select_n.155), kind=kLoop, calls=%fused_computation.75 | loop fusion | bytes 1835012 | tf_op jit(solution)/shard_map/dynamic_slice | solution.py:233
  12.6 3.1 %collective-permute-start.5 = (bf16[48,1024]{1,0:T(8,128)(2,1)S(1)}, bf16[48,1024]{1,0:T(8,128)(2,1)S(1)}, u32[]{:S(2)}, u32[]{:S(2)}) collective-permute-start(bf16[48,1024]{1,0:T(8,128)(2,1)S(1)} %get-tuple-element.95), channel_id=1, source_target_pairs={{0,96},{32,0},{64,32},{96,64},{1,97},{33,1},{65,33},{97,65},{2,98}... | collective-permute-start | bytes 294920 | tf_op jit(solution)/shard_map/ppermute | solution.py:18
  17.2 2.2 %constant_dynamic-slice_fusion.1 = bf16[512,896]{1,0:T(8,128)(2,1)} fusion(bf16[512,3584]{1,0:T(8,128)(2,1)} %mine.1, s32[]{:T(128)S(6)} %select_n.169), kind=kLoop, calls=%fused_computation.72 | loop fusion | bytes 1835012 | tf_op jit(solution)/shard_map/dynamic_slice | solution.py:233
  19.4 2.3 %collective-permute-start.10 = (bf16[512,896]{1,0:T(8,128)(2,1)}, bf16[512,896]{1,0:T(8,128)(2,1)S(1)}, u32[]{:S(2)}, u32[]{:S(2)}) collective-permute-start(bf16[512,896]{1,0:T(8,128)(2,1)} %constant_dynamic-slice_fusion.1), channel_id=1, source_target_pairs={{0,24},{8,0},{16,8},{24,16},{1,9},{9,17},{17,25},{25,1},{2,26},{10... | collective-permute-start | bytes 2752520 | tf_op jit(solution)/shard_map/ppermute | solution.py:24
  23.7 4.5 %collective-permute-done.6.near = bf16[512,896]{1,0:T(8,128)(2,1)S(1)} collective-permute-done((bf16[512,896]{1,0:T(8,128)(2,1)}, bf16[512,896]{1,0:T(8,128)(2,1)S(1)}, u32[]{:S(2)}, u32[]{:S(2)}) %collective-permute-start.6) | collective-permute-done | bytes 917536 | tf_op jit(solution)/shard_map/ppermute | solution.py:24
  30.7 1.5 collective-permute-start.7
  32.2 3.2 %collective-permute-start.8 = (bf16[160,1024]{1,0:T(8,128)(2,1)}, bf16[160,1024]{1,0:T(8,128)(2,1)}, u32[]{:S(2)}, u32[]{:S(2)}) collective-permute-start(bf16[160,1024]{1,0:T(8,128)(2,1)} %get-tuple-element.104), channel_id=1, source_target_pairs={{0,16},{8,24},{16,0},{24,8},{1,17},{9,25},{17,1},{25,9},{2,18},{10... | collective-permute-start | bytes 983048 | tf_op jit(solution)/shard_map/ppermute | solution.py:18
  37.7 1.6 fusion.4
  39.5 3.0 %collective-permute-done.7 = bf16[160,1024]{1,0:T(8,128)(2,1)} collective-permute-done((bf16[160,1024]{1,0:T(8,128)(2,1)}, bf16[160,1024]{1,0:T(8,128)(2,1)}, u32[]{:S(2)}, u32[]{:S(2)}) %collective-permute-start.7) | collective-permute-done | bytes 327712 | tf_op jit(solution)/shard_map/ppermute | solution.py:18
  42.4 8.0 %collective-permute-done.8 = bf16[160,1024]{1,0:T(8,128)(2,1)} collective-permute-done((bf16[160,1024]{1,0:T(8,128)(2,1)}, bf16[160,1024]{1,0:T(8,128)(2,1)}, u32[]{:S(2)}, u32[]{:S(2)}) %collective-permute-start.8) | collective-permute-done | bytes 327712 | tf_op jit(solution)/shard_map/ppermute | solution.py:18
  54.8 1.7 collective-permute-start.15
  59.0 13.5 %collective-permute-done.14.across0 = bf16[256,896]{1,0:T(8,128)(2,1)S(1)} collective-permute-done((bf16[256,896]{1,0:T(8,128)(2,1)S(1)}, bf16[256,896]{1,0:T(8,128)(2,1)S(1)}, u32[]{:S(2)}, u32[]{:S(2)}) %collective-permute-start.14) | collective-permute-done | bytes 458784 | tf_op jit(solution)/shard_map/ppermute | solution.py:24
  75.7 14.8 %collective-permute-done.21.left1 = bf16[80,1024]{1,0:T(8,128)(2,1)S(1)} collective-permute-done((bf16[80,1024]{1,0:T(8,128)(2,1)S(1)}, bf16[80,1024]{1,0:T(8,128)(2,1)S(1)}, u32[]{:S(2)}, u32[]{:S(2)}) %collective-permute-start.21) | collective-permute-done | bytes 163872 | tf_op jit(solution)/shard_map/ppermute | solution.py:24
  91.8 1.6 collective-permute-done.24.other1
  94.4 7.2 %base.2 = (bf16[4,2,32,896]{3,2,1,0:T(8,128)(2,1)S(1)}, bf16[4,2,32,896]{3,2,1,0:T(8,128)(2,1)S(1)}, bf16[4,2,32,896]{3,2,1,0:T(8,128)(2,1)S(1)}, bf16[4,2,32,896]{3,2,1,0:T(8,128)(2,1)S(1)}) custom-call(s32[4]{0:T(128)S(1)} %pad_add_fusion.s_ref, bf16[512,1024]{1,0:T(8,128)(2,1)S(1)} %bitcast.81, bf16[512,1024]{1,0:T(8,128)(2,1)} %copy-done.29, ...), custom_call_target="tpu_custom_call" | custom-call | flops 3758096384 | bytes 9699328 | tf_op jit(solution)/shard_map/base/pallas_call | solution.py:73
  102.0 5.0 %collective-permute-done.23.own1 = bf16[512,1024]{1,0:T(8,128)(2,1)S(1)} collective-permute-done((bf16[512,1024]{1,0:T(8,128)(2,1)}, bf16[512,1024]{1,0:T(8,128)(2,1)S(1)}, u32[]{:S(2)}, u32[]{:S(2)}) %collective-permute-start.23) | collective-permute-done | bytes 1048608 | tf_op jit(solution)/shard_map/ppermute | solution.py:24
  107.0 4.4 %collective-permute-done.27 = bf16[4,2,32,896]{3,2,1,0:T(8,128)(2,1)S(1)} collective-permute-done((bf16[4,2,32,896]{3,2,1,0:T(8,128)(2,1)S(1)}, bf16[4,2,32,896]{3,2,1,0:T(8,128)(2,1)S(1)}, u32[]{:S(2)}, u32[]{:S(2)}) %collective-permute-start.27) | collective-permute-done | bytes 458784 | tf_op jit(solution)/shard_map/ppermute | solution.py:24
  112.9 8.4 %collective-permute-done.28 = bf16[4,2,32,896]{3,2,1,0:T(8,128)(2,1)S(1)} collective-permute-done((bf16[4,2,32,896]{3,2,1,0:T(8,128)(2,1)S(1)}, bf16[4,2,32,896]{3,2,1,0:T(8,128)(2,1)S(1)}, u32[]{:S(2)}, u32[]{:S(2)}) %collective-permute-start.28) | collective-permute-done | bytes 458784 | tf_op jit(solution)/shard_map/ppermute | solution.py:24
  122.5 7.2 %base.3 = (bf16[4,2,32,896]{3,2,1,0:T(8,128)(2,1)S(1)}, bf16[4,2,32,896]{3,2,1,0:T(8,128)(2,1)S(1)}, bf16[4,2,32,896]{3,2,1,0:T(8,128)(2,1)S(1)}, bf16[4,2,32,896]{3,2,1,0:T(8,128)(2,1)S(1)}) custom-call(s32[4]{0:T(128)S(1)} %pad_add_fusion.s_ref, bf16[512,1024]{1,0:T(8,128)(2,1)S(1)} %collective-permute-done.12.own0, bf16[512,1024]{1,0:T(8,128)(2,1)} %copy-done.32, ...), custom_call_target="tpu_custom_call" | custom-call | flops 3758096384 | bytes 9699328 | tf_op jit(solution)/shard_map/base/pallas_call | solution.py:73
  130.1 6.7 %collective-permute-done.40.refs_1_ = bf16[256,1536]{1,0:T(8,128)(2,1)S(1)} collective-permute-done((bf16[256,1536]{1,0:T(8,128)(2,1)S(1)}, bf16[256,1536]{1,0:T(8,128)(2,1)S(1)}, u32[]{:S(2)}, u32[]{:S(2)}) %collective-permute-start.40) | collective-permute-done | bytes 786464 | tf_op jit(solution)/shard_map/ppermute | solution.py:24
  137.5 5.9 %collective-permute-done.26.left3 = bf16[80,1024]{1,0:T(8,128)(2,1)S(1)} collective-permute-done((bf16[80,1024]{1,0:T(8,128)(2,1)S(1)}, bf16[80,1024]{1,0:T(8,128)(2,1)S(1)}, u32[]{:S(2)}, u32[]{:S(2)}) %collective-permute-start.26) | collective-permute-done | bytes 163872 | tf_op jit(solution)/shard_map/ppermute | solution.py:24
  144.3 5.9 %collective-permute-done.41.refs_2_ = bf16[256,1536]{1,0:T(8,128)(2,1)} collective-permute-done((bf16[256,1536]{1,0:T(8,128)(2,1)S(1)}, bf16[256,1536]{1,0:T(8,128)(2,1)}, u32[]{:S(2)}, u32[]{:S(2)}) %collective-permute-start.41) | collective-permute-done | bytes 786464 | tf_op jit(solution)/shard_map/ppermute | solution.py:24
  151.0 2.3 %collective-permute-done.34 = bf16[4,2,32,896]{3,2,1,0:T(8,128)(2,1)S(1)} collective-permute-done((bf16[4,2,32,896]{3,2,1,0:T(8,128)(2,1)S(1)}, bf16[4,2,32,896]{3,2,1,0:T(8,128)(2,1)S(1)}, u32[]{:S(2)}, u32[]{:S(2)}) %collective-permute-start.34) | collective-permute-done | bytes 458784 | tf_op jit(solution)/shard_map/ppermute | solution.py:24
  153.4 2.4 %collective-permute-start.31 = (bf16[2,32,896]{2,1,0:T(8,128)(2,1)}, bf16[2,32,896]{2,1,0:T(8,128)(2,1)}, u32[]{:S(2)}, u32[]{:S(2)}) collective-permute-start(bf16[2,32,896]{2,1,0:T(8,128)(2,1)} %get-tuple-element.88), channel_id=1, source_target_pairs={{0,16},{8,24},{16,0},{24,8},{1,17},{9,25},{17,1},{25,9},{2,18},{10... | collective-permute-start | bytes 344072 | tf_op jit(solution)/shard_map/ppermute | solution.py:18
  158.4 6.1 %collective-permute-done.45.refs_3_.refs_7_ = bf16[256,2176]{1,0:T(8,128)(2,1)} collective-permute-done((bf16[256,2176]{1,0:T(8,128)(2,1)S(1)}, bf16[256,2176]{1,0:T(8,128)(2,1)}, u32[]{:S(2)}, u32[]{:S(2)}) %collective-permute-start.45) | collective-permute-done | bytes 1114144 | tf_op jit(solution)/shard_map/ppermute | solution.py:24
  168.4 7.0 %update.2.refs_8_ = bf16[512,3584]{1,0:T(8,128)(2,1)} custom-call(s32[4]{0:T(128)S(1)} %pad_add_fusion.s_ref, bf16[80,1024]{1,0:T(8,128)(2,1)S(1)} %pad_maximum_fusion.5.left0, bf16[80,1024]{1,0:T(8,128)(2,1)S(1)} %copy-done.8, bf16[80,1024]{1,0:T(8,128)(2,1)S(1)} %copy-done.10, bf16[80,1024]{1,0:T(8,128)(2,1)S(1)} %copy-done.12, ...), custom_call_target="tpu_custom_call" | custom-call | flops 2147483648 | bytes 7340032 | tf_op jit(solution)/shard_map/update/pallas_call | solution.py:175
  176.8 2.1 %collective-permute-start.39 = (bf16[2,32,896]{2,1,0:T(8,128)(2,1)S(1)}, bf16[2,32,896]{2,1,0:T(8,128)(2,1)S(1)}, u32[]{:S(2)}, u32[]{:S(2)}) collective-permute-start(bf16[2,32,896]{2,1,0:T(8,128)(2,1)S(1)} %get-tuple-element.91), channel_id=1, source_target_pairs={{0,8},{8,16},{16,24},{24,0},{1,9},{9,17},{17,25},{25,1},{2,10},{10... | collective-permute-start | bytes 344072 | tf_op jit(solution)/shard_map/ppermute | solution.py:18
  178.9 2.8 %collective-permute-start.37 = (bf16[2,32,896]{2,1,0:T(8,128)(2,1)S(1)}, bf16[2,32,896]{2,1,0:T(8,128)(2,1)S(1)}, u32[]{:S(2)}, u32[]{:S(2)}) collective-permute-start(bf16[2,32,896]{2,1,0:T(8,128)(2,1)S(1)} %get-tuple-element.93), channel_id=1, source_target_pairs={{0,24},{8,0},{16,8},{24,16},{1,25},{9,1},{17,9},{25,17},{2,26},{10... | collective-permute-start | bytes 344072 | tf_op jit(solution)/shard_map/ppermute | solution.py:18
  181.7 6.1 %update.3 = bf16[512,3584]{1,0:T(8,128)(2,1)} custom-call(s32[4]{0:T(128)S(1)} %pad_add_fusion.s_ref, bf16[80,1024]{1,0:T(8,128)(2,1)S(1)} %pad_maximum_fusion.5.left0, bf16[80,1024]{1,0:T(8,128)(2,1)S(1)} %copy-done.8, bf16[80,1024]{1,0:T(8,128)(2,1)S(1)} %copy-done.10, bf16[80,1024]{1,0:T(8,128)(2,1)S(1)} %copy-done.12, ...), custom_call_target="tpu_custom_call", output_to_operand_aliasing={{}: (14, {})} | custom-call | flops 1610612736 | bytes 5767168 | tf_op jit(solution)/shard_map/update/pallas_call | solution.py:175
  189.0 2.6 %outputs.1 = bf16[128,3584]{1,0:T(8,128)(2,1)} custom-call(s32[4]{0:T(128)S(1)} %pad_add_fusion.s_ref, bf16[4,4,32,896]{3,2,1,0:T(8,128)(2,1)S(1)} %maximum_maximum_fusion.sums_ref, f32[128,1]{1,0:T(8,128)S(1)} %copy-done.17, bf16[64,3584]{1,0:T(8,128)(2,1)S(1)} %copy-done.6), custom_call_target="tpu_custom_call" | custom-call | tf_op jit(solution)/shard_map/outputs/pallas_call | solution.py:112
  (192 shorter events, 39.0 us)
Async XLA Ops:
  1.8 10.6 %collective-permute-start = (bf16[48,1024]{1,0:T(8,128)(2,1)S(1)}, bf16[48,1024]{1,0:T(8,128)(2,1)S(1)}, u32[]{:S(2)}, u32[]{:S(2)}) collective-permute-start(bf16[48,1024]{1,0:T(8,128)(2,1)S(1)} %get-tuple-element.99), channel_id=1, source_target_pairs={{0,2},{2,4},{4,6},{6,0},{1,3},{3,5},{5,7},{7,1},{8,10},{10,12},{12... | collective-permute-start | bytes 294920 | tf_op jit(solution)/shard_map/ppermute | solution.py:18
  10.6 17.6 %collective-permute-start.6 = (bf16[512,896]{1,0:T(8,128)(2,1)}, bf16[512,896]{1,0:T(8,128)(2,1)S(1)}, u32[]{:S(2)}, u32[]{:S(2)}) collective-permute-start(bf16[512,896]{1,0:T(8,128)(2,1)} %constant_dynamic-slice_fusion.4), channel_id=1, source_target_pairs={{0,8},{8,16},{16,24},{24,0},{1,25},{9,1},{17,9},{25,17},{2,10},{10... | collective-permute-start | bytes 2752520 | tf_op jit(solution)/shard_map/ppermute | solution.py:24
  19.4 32.3 %collective-permute-start.10 = (bf16[512,896]{1,0:T(8,128)(2,1)}, bf16[512,896]{1,0:T(8,128)(2,1)S(1)}, u32[]{:S(2)}, u32[]{:S(2)}) collective-permute-start(bf16[512,896]{1,0:T(8,128)(2,1)} %constant_dynamic-slice_fusion.1), channel_id=1, source_target_pairs={{0,24},{8,0},{16,8},{24,16},{1,9},{9,17},{17,25},{25,1},{2,26},{10... | collective-permute-start | bytes 2752520 | tf_op jit(solution)/shard_map/ppermute | solution.py:24
  28.3 24.4 %collective-permute-start.11 = (bf16[64,3712]{1,0:T(8,128)(2,1)S(1)}, bf16[64,3712]{1,0:T(8,128)(2,1)S(1)}, u32[]{:S(2)}, u32[]{:S(2)}) collective-permute-start(bf16[64,3712]{1,0:T(8,128)(2,1)S(1)} %fusion.3), channel_id=1, source_target_pairs={{0,32},{32,64},{64,96},{96,0},{1,97},{33,1},{65,33},{97,65},{2,34}... | collective-permute-start | bytes 1425416 | tf_op jit(solution)/shard_map/ppermute | solution.py:24
  30.7 11.7 %collective-permute-start.7 = (bf16[160,1024]{1,0:T(8,128)(2,1)}, bf16[160,1024]{1,0:T(8,128)(2,1)}, u32[]{:S(2)}, u32[]{:S(2)}) collective-permute-start(bf16[160,1024]{1,0:T(8,128)(2,1)} %get-tuple-element.103), channel_id=1, source_target_pairs={{0,8},{8,16},{16,24},{24,0},{1,9},{9,17},{17,25},{25,1},{2,10},{10... | collective-permute-start | bytes 983048 | tf_op jit(solution)/shard_map/ppermute | solution.py:18
  32.2 18.2 %collective-permute-start.8 = (bf16[160,1024]{1,0:T(8,128)(2,1)}, bf16[160,1024]{1,0:T(8,128)(2,1)}, u32[]{:S(2)}, u32[]{:S(2)}) collective-permute-start(bf16[160,1024]{1,0:T(8,128)(2,1)} %get-tuple-element.104), channel_id=1, source_target_pairs={{0,16},{8,24},{16,0},{24,8},{1,17},{9,25},{17,1},{25,9},{2,18},{10... | collective-permute-start | bytes 983048 | tf_op jit(solution)/shard_map/ppermute | solution.py:18
  35.5 14.9 %collective-permute-start.9 = (bf16[160,1024]{1,0:T(8,128)(2,1)}, bf16[160,1024]{1,0:T(8,128)(2,1)}, u32[]{:S(2)}, u32[]{:S(2)}) collective-permute-start(bf16[160,1024]{1,0:T(8,128)(2,1)} %get-tuple-element.105), channel_id=1, source_target_pairs={{0,24},{8,0},{16,8},{24,16},{1,25},{9,1},{17,9},{25,17},{2,26},{10... | collective-permute-start | bytes 983048 | tf_op jit(solution)/shard_map/ppermute | solution.py:18
  53.6 18.9 %collective-permute-start.13 = (bf16[512,1024]{1,0:T(8,128)(2,1)S(1)}, bf16[512,1024]{1,0:T(8,128)(2,1)S(1)}, u32[]{:S(2)}, u32[]{:S(2)}) collective-permute-start(bf16[512,1024]{1,0:T(8,128)(2,1)S(1)} %bitcast.79), channel_id=1, source_target_pairs={{0,1},{1,0},{2,3},{3,2},{4,5},{5,4},{6,7},{7,6},{8,9},{9,8},{10,11... | collective-permute-start | bytes 3145736 | tf_op jit(solution)/shard_map/ppermute | solution.py:269
  53.7 18.8 %collective-permute-start.12 = (bf16[512,1024]{1,0:T(8,128)(2,1)S(1)}, bf16[512,1024]{1,0:T(8,128)(2,1)S(1)}, u32[]{:S(2)}, u32[]{:S(2)}) collective-permute-start(bf16[512,1024]{1,0:T(8,128)(2,1)S(1)} %bitcast.80), channel_id=1, source_target_pairs={{0,2},{2,4},{4,6},{6,0},{1,7},{3,1},{5,3},{7,5},{8,10},{10,12},{12... | collective-permute-start | bytes 3145736 | tf_op jit(solution)/shard_map/ppermute | solution.py:24
  54.8 17.7 %collective-permute-start.15 = (bf16[64,3712]{1,0:T(8,128)(2,1)S(1)}, bf16[64,3712]{1,0:T(8,128)(2,1)S(1)}, u32[]{:S(2)}, u32[]{:S(2)}) collective-permute-start(bf16[64,3712]{1,0:T(8,128)(2,1)S(1)} %copy-done.26), channel_id=1, source_target_pairs={{0,32},{32,64},{64,96},{96,0},{1,97},{33,1},{65,33},{97,65},{2,34}... | collective-permute-start | bytes 1425416 | tf_op jit(solution)/shard_map/ppermute | solution.py:24
  57.8 14.7 %collective-permute-start.14 = (bf16[256,896]{1,0:T(8,128)(2,1)S(1)}, bf16[256,896]{1,0:T(8,128)(2,1)S(1)}, u32[]{:S(2)}, u32[]{:S(2)}) collective-permute-start(bf16[256,896]{1,0:T(8,128)(2,1)S(1)} %get-tuple-element.83), channel_id=1, source_target_pairs={{0,16},{8,24},{16,0},{24,8},{1,17},{9,25},{17,1},{25,9},{2,18},{10... | collective-permute-start | bytes 1376264 | tf_op jit(solution)/shard_map/ppermute | solution.py:24
  72.5 18.0 %collective-permute-start.18 = (bf16[512,1024]{1,0:T(8,128)(2,1)S(1)}, bf16[512,1024]{1,0:T(8,128)(2,1)S(1)}, u32[]{:S(2)}, u32[]{:S(2)}) collective-permute-start(bf16[512,1024]{1,0:T(8,128)(2,1)S(1)} %collective-permute-done.12.own0), channel_id=1, source_target_pairs={{0,1},{1,0},{2,3},{3,2},{4,5},{5,4},{6,7},{7,6},{8,9},{9,8},{10,11... | collective-permute-start | bytes 3145736 | tf_op jit(solution)/shard_map/ppermute | solution.py:285
  72.7 17.8 %collective-permute-start.17 = (bf16[512,1024]{1,0:T(8,128)(2,1)S(1)}, bf16[512,1024]{1,0:T(8,128)(2,1)}, u32[]{:S(2)}, u32[]{:S(2)}) collective-permute-start(bf16[512,1024]{1,0:T(8,128)(2,1)S(1)} %collective-permute-done.12.own0), channel_id=1, source_target_pairs={{0,2},{2,4},{4,6},{6,0},{1,7},{3,1},{5,3},{7,5},{8,10},{10,12},{12... | collective-permute-start | bytes 3145736 | tf_op jit(solution)/shard_map/ppermute | solution.py:24
  73.8 16.7 %collective-permute-start.20 = (bf16[64,3712]{1,0:T(8,128)(2,1)S(1)}, bf16[64,3712]{1,0:T(8,128)(2,1)S(1)}, u32[]{:S(2)}, u32[]{:S(2)}) collective-permute-start(bf16[64,3712]{1,0:T(8,128)(2,1)S(1)} %collective-permute-done.15), channel_id=1, source_target_pairs={{0,32},{32,64},{64,96},{96,0},{1,97},{33,1},{65,33},{97,65},{2,34}... | collective-permute-start | bytes 1425416 | tf_op jit(solution)/shard_map/ppermute | solution.py:24
  73.8 16.6 %collective-permute-start.21 = (bf16[80,1024]{1,0:T(8,128)(2,1)S(1)}, bf16[80,1024]{1,0:T(8,128)(2,1)S(1)}, u32[]{:S(2)}, u32[]{:S(2)}) collective-permute-start(bf16[80,1024]{1,0:T(8,128)(2,1)S(1)} %pad_maximum_fusion.5.left0), channel_id=1, source_target_pairs={{0,2},{2,4},{4,6},{6,0},{1,7},{3,1},{5,3},{7,5},{8,10},{10,12},{12... | collective-permute-start | bytes 491528 | tf_op jit(solution)/shard_map/ppermute | solution.py:24
  74.8 15.7 %collective-permute-start.19 = (bf16[256,896]{1,0:T(8,128)(2,1)S(1)}, bf16[256,896]{1,0:T(8,128)(2,1)S(1)}, u32[]{:S(2)}, u32[]{:S(2)}) collective-permute-start(bf16[256,896]{1,0:T(8,128)(2,1)S(1)} %get-tuple-element.53), channel_id=1, source_target_pairs={{0,16},{8,24},{16,0},{24,8},{1,17},{9,25},{17,1},{25,9},{2,18},{10... | collective-permute-start | bytes 1376264 | tf_op jit(solution)/shard_map/ppermute | solution.py:24
  90.7 16.3 %collective-permute-start.23 = (bf16[512,1024]{1,0:T(8,128)(2,1)}, bf16[512,1024]{1,0:T(8,128)(2,1)S(1)}, u32[]{:S(2)}, u32[]{:S(2)}) collective-permute-start(bf16[512,1024]{1,0:T(8,128)(2,1)} %collective-permute-done.17.own1), channel_id=1, source_target_pairs={{0,2},{2,4},{4,6},{6,0},{1,7},{3,1},{5,3},{7,5},{8,10},{10,12},{12... | collective-permute-start | bytes 3145736 | tf_op jit(solution)/shard_map/ppermute | solution.py:24
  91.6 20.1 %collective-permute-start.43 = (bf16[256,2176]{1,0:T(8,128)(2,1)S(1)}, bf16[256,2176]{1,0:T(8,128)(2,1)S(1)}, u32[]{:S(2)}, u32[]{:S(2)}) collective-permute-start(bf16[256,2176]{1,0:T(8,128)(2,1)S(1)} %slice.143.refs_0_.refs_4_), channel_id=1, source_target_pairs={{0,8},{8,16},{16,24},{24,0},{1,25},{9,1},{17,9},{25,17},{2,10},{10... | collective-permute-start | bytes 3342344 | tf_op jit(solution)/shard_map/ppermute | solution.py:24
  107.0 14.5 %collective-permute-start.25 = (bf16[512,1024]{1,0:T(8,128)(2,1)S(1)}, bf16[512,1024]{1,0:T(8,128)(2,1)S(1)}, u32[]{:S(2)}, u32[]{:S(2)}) collective-permute-start(bf16[512,1024]{1,0:T(8,128)(2,1)S(1)} %collective-permute-done.23.own1), channel_id=1, source_target_pairs={{0,1},{1,0},{2,3},{3,2},{4,5},{5,4},{6,7},{7,6},{8,9},{9,8},{10,11... | collective-permute-start | bytes 3145736 | tf_op jit(solution)/shard_map/ppermute | solution.py:303
  111.6 25.8 %collective-permute-start.44 = (bf16[256,2176]{1,0:T(8,128)(2,1)S(1)}, bf16[256,2176]{1,0:T(8,128)(2,1)S(1)}, u32[]{:S(2)}, u32[]{:S(2)}) collective-permute-start(bf16[256,2176]{1,0:T(8,128)(2,1)S(1)} %collective-permute-done.43.refs_1_.refs_5_), channel_id=1, source_target_pairs={{0,8},{8,16},{16,24},{24,0},{1,25},{9,1},{17,9},{25,17},{2,10},{10... | collective-permute-start | bytes 3342344 | tf_op jit(solution)/shard_map/ppermute | solution.py:24
  111.8 25.1 %collective-permute-start.40 = (bf16[256,1536]{1,0:T(8,128)(2,1)S(1)}, bf16[256,1536]{1,0:T(8,128)(2,1)S(1)}, u32[]{:S(2)}, u32[]{:S(2)}) collective-permute-start(bf16[256,1536]{1,0:T(8,128)(2,1)S(1)} %slice.142.refs_0_), channel_id=1, source_target_pairs={{0,8},{8,16},{16,24},{24,0},{1,25},{9,1},{17,9},{25,17},{2,10},{10... | collective-permute-start | bytes 2359304 | tf_op jit(solution)/shard_map/ppermute | solution.py:24
  121.4 16.0 %collective-permute-start.29 = (bf16[4,2,32,896]{3,2,1,0:T(8,128)(2,1)S(1)}, bf16[4,2,32,896]{3,2,1,0:T(8,128)(2,1)S(1)}, u32[]{:S(2)}, u32[]{:S(2)}) collective-permute-start(bf16[4,2,32,896]{3,2,1,0:T(8,128)(2,1)S(1)} %add_convert_fusion.4), channel_id=1, source_target_pairs={{0,32},{32,64},{64,96},{96,0},{1,97},{33,1},{65,33},{97,65},{2,34}... | collective-permute-start | bytes 1376264 | tf_op jit(solution)/shard_map/ppermute | solution.py:24
  129.7 13.8 %collective-permute-start.33 = (bf16[4,2,32,896]{3,2,1,0:T(8,128)(2,1)S(1)}, bf16[4,2,32,896]{3,2,1,0:T(8,128)(2,1)S(1)}, u32[]{:S(2)}, u32[]{:S(2)}) collective-permute-start(bf16[4,2,32,896]{3,2,1,0:T(8,128)(2,1)S(1)} %get-tuple-element.66), channel_id=1, source_target_pairs={{0,32},{32,64},{64,96},{96,0},{1,97},{33,1},{65,33},{97,65},{2,34}... | collective-permute-start | bytes 1376264 | tf_op jit(solution)/shard_map/ppermute | solution.py:24
  136.9 13.3 %collective-permute-start.41 = (bf16[256,1536]{1,0:T(8,128)(2,1)S(1)}, bf16[256,1536]{1,0:T(8,128)(2,1)}, u32[]{:S(2)}, u32[]{:S(2)}) collective-permute-start(bf16[256,1536]{1,0:T(8,128)(2,1)S(1)} %collective-permute-done.40.refs_1_), channel_id=1, source_target_pairs={{0,8},{8,16},{16,24},{24,0},{1,25},{9,1},{17,9},{25,17},{2,10},{10... | collective-permute-start | bytes 2359304 | tf_op jit(solution)/shard_map/ppermute | solution.py:24
  137.4 27.2 %collective-permute-start.45 = (bf16[256,2176]{1,0:T(8,128)(2,1)S(1)}, bf16[256,2176]{1,0:T(8,128)(2,1)}, u32[]{:S(2)}, u32[]{:S(2)}) collective-permute-start(bf16[256,2176]{1,0:T(8,128)(2,1)S(1)} %collective-permute-done.44.refs_2_.refs_6_), channel_id=1, source_target_pairs={{0,8},{8,16},{16,24},{24,0},{1,25},{9,1},{17,9},{25,17},{2,10},{10... | collective-permute-start | bytes 3342344 | tf_op jit(solution)/shard_map/ppermute | solution.py:24
  144.1 12.5 %collective-permute-start.36 = (bf16[4,80,1024]{2,1,0:T(8,128)(2,1)S(1)}, bf16[4,80,1024]{2,1,0:T(8,128)(2,1)S(1)}, u32[]{:S(2)}, u32[]{:S(2)}) collective-permute-start(bf16[4,80,1024]{2,1,0:T(8,128)(2,1)S(1)} %pad_maximum_fusion.1), channel_id=1, source_target_pairs={{0,1},{1,0},{2,3},{3,2},{4,5},{5,4},{6,7},{7,6},{8,9},{9,8},{10,11... | collective-permute-start | bytes 1966088 | tf_op jit(solution)/shard_map/ppermute | solution.py:328
  150.2 28.7 %collective-permute-start.42 = (bf16[256,1536]{1,0:T(8,128)(2,1)}, bf16[256,1536]{1,0:T(8,128)(2,1)}, u32[]{:S(2)}, u32[]{:S(2)}) collective-permute-start(bf16[256,1536]{1,0:T(8,128)(2,1)} %collective-permute-done.41.refs_2_), channel_id=1, source_target_pairs={{0,8},{8,16},{16,24},{24,0},{1,25},{9,1},{17,9},{25,17},{2,10},{10... | collective-permute-start | bytes 2359304 | tf_op jit(solution)/shard_map/ppermute | solution.py:24
  151.0 27.9 %collective-permute-start.32 = (bf16[2,32,896]{2,1,0:T(8,128)(2,1)}, bf16[2,32,896]{2,1,0:T(8,128)(2,1)}, u32[]{:S(2)}, u32[]{:S(2)}) collective-permute-start(bf16[2,32,896]{2,1,0:T(8,128)(2,1)} %get-tuple-element.87), channel_id=1, source_target_pairs={{0,8},{8,16},{16,24},{24,0},{1,9},{9,17},{17,25},{25,1},{2,10},{10... | collective-permute-start | bytes 344072 | tf_op jit(solution)/shard_map/ppermute | solution.py:18
  153.4 34.4 %collective-permute-start.31 = (bf16[2,32,896]{2,1,0:T(8,128)(2,1)}, bf16[2,32,896]{2,1,0:T(8,128)(2,1)}, u32[]{:S(2)}, u32[]{:S(2)}) collective-permute-start(bf16[2,32,896]{2,1,0:T(8,128)(2,1)} %get-tuple-element.88), channel_id=1, source_target_pairs={{0,16},{8,24},{16,0},{24,8},{1,17},{9,25},{17,1},{25,9},{2,18},{10... | collective-permute-start | bytes 344072 | tf_op jit(solution)/shard_map/ppermute | solution.py:18
  156.6 18.8 %collective-permute-start.35 = (bf16[4,2,32,896]{3,2,1,0:T(8,128)(2,1)}, bf16[4,2,32,896]{3,2,1,0:T(8,128)(2,1)}, u32[]{:S(2)}, u32[]{:S(2)}) collective-permute-start(bf16[4,2,32,896]{3,2,1,0:T(8,128)(2,1)} %add_convert_fusion.1), channel_id=1, source_target_pairs={{0,32},{32,64},{64,96},{96,0},{1,97},{33,1},{65,33},{97,65},{2,34}... | collective-permute-start | bytes 1376264 | tf_op jit(solution)/shard_map/ppermute | solution.py:24
  164.6 23.2 %collective-permute-start.30 = (bf16[2,32,896]{2,1,0:T(8,128)(2,1)}, bf16[2,32,896]{2,1,0:T(8,128)(2,1)S(1)}, u32[]{:S(2)}, u32[]{:S(2)}) collective-permute-start(bf16[2,32,896]{2,1,0:T(8,128)(2,1)} %get-tuple-element.89), channel_id=1, source_target_pairs={{0,24},{8,0},{16,8},{24,16},{1,25},{9,1},{17,9},{25,17},{2,26},{10... | collective-permute-start | bytes 344072 | tf_op jit(solution)/shard_map/ppermute | solution.py:18
  176.8 11.0 %collective-permute-start.39 = (bf16[2,32,896]{2,1,0:T(8,128)(2,1)S(1)}, bf16[2,32,896]{2,1,0:T(8,128)(2,1)S(1)}, u32[]{:S(2)}, u32[]{:S(2)}) collective-permute-start(bf16[2,32,896]{2,1,0:T(8,128)(2,1)S(1)} %get-tuple-element.91), channel_id=1, source_target_pairs={{0,8},{8,16},{16,24},{24,0},{1,9},{9,17},{17,25},{25,1},{2,10},{10... | collective-permute-start | bytes 344072 | tf_op jit(solution)/shard_map/ppermute | solution.py:18
  (50 other events, 487.4 us)

commit v3 on v2

--- a/solution.py
+++ b/solution.py
@@ -10,7 +10,7 @@
 noise_scale = 0.5
 epsilon = 1e-05
 F32, BF16 = jnp.float32, jnp.bfloat16
-VMEM = 48 * 2**20
+VMEM = 60 * 2**20
 SWAP = [(0, 1), (1, 0)]
 
 
@@ -59,11 +59,9 @@
             total = term if total is None else total + term
         total = total.astype(BF16)
         for d in range(nx):
-            parts = [total[(d * ny + s) * rows : (d * ny + s + 1) * rows] for s in range(ny)]
-            out_refs[0][d, k] = jnp.where(c == 0, parts[1], parts[3])
-            out_refs[1][d, k] = parts[2]
-            out_refs[2][d, k] = jnp.where(c == 0, parts[3], parts[1])
-            out_refs[3][d, k] = parts[0]
+            for s in range(ny):
+                at = (d * ny + s) * rows
+                out_refs[s][d, k] = total[at : at + rows]
 
 
 def base_part(place, own0, other0, own1, other1, weight, moved):
@@ -91,47 +89,46 @@
     )(place, own0, other0, own1, other1, weight, *moved)
 
 
-def output_kernel(s_ref, sums_ref, probe_ref, right_ref, out_ref):
-    z, c = s_ref[2], s_ref[3]
-    rows = sums_ref.shape[2]
+def output_kernel(s_ref, *refs):
+    sums, (probe_ref, right_ref, out_ref) = refs[:4], refs[4:]
+    x, z, c = s_ref[1], s_ref[2], s_ref[3]
+    _, rows, cols = sums[0].shape
     members = right_ref.shape[0]
     row = lax.broadcasted_iota(jnp.int32, (2 * members, members), 0)
     member = lax.broadcasted_iota(jnp.int32, (2 * members, members), 1)
     twice = jnp.where(lax.div(row, 2) == member, 1.0, 0.0).astype(BF16)
-    right = jnp.dot(twice, right_ref[...], preferred_element_type=F32)
-    for zz in range(4):
-        k = lax.rem(jnp.where(c == 0, z - zz, zz - z) + 4, 4)
-        at = slice(zz * rows, (zz + 1) * rows)
-        out = sums_ref[0, lax.rem(k, 2) * 2 + lax.div(k, 2)].astype(F32)
-        out_ref[at] = (out + probe_ref[at] * right[at]).astype(BF16)
+    for d in range(4):
+        lanes = pl.ds(pl.multiple_of(lax.rem(x + d, 4) * cols, 128), cols)
+        right = jnp.dot(twice, right_ref[:, lanes], preferred_element_type=F32)
+        for zz in range(4):
+            k = lax.rem(jnp.where(c == 0, z - zz, zz - z) + 4, 4)
+            at = slice(zz * rows, (zz + 1) * rows)
+            out = sums[d][lax.rem(k, 2) * 2 + lax.div(k, 2)].astype(F32)
+            out_ref[at, lanes] = (out + probe_ref[at] * right[at]).astype(BF16)
 
 
 def output_part(place, sums, probe, right):
-    _, _, rows, cols = sums.shape
-    members = right.shape[0]
+    _, rows, cols = sums[0].shape
+    out = (4 * rows, 4 * cols)
     return pl.pallas_call(
         output_kernel,
         grid_spec=pltpu.PrefetchScalarGridSpec(
             num_scalar_prefetch=1,
-            grid=(4,),
-            in_specs=[
-                pl.BlockSpec((1, 4, rows, cols), lambda i, s: (lax.rem(i - s[1] + 4, 4), 0, 0, 0)),
-                whole((4 * rows, 1)),
-                pl.BlockSpec((members, cols), lambda i, s: (0, i)),
-            ],
-            out_specs=pl.BlockSpec((4 * rows, cols), lambda i, s: (0, i)),
-        ),
-        out_shape=jax.ShapeDtypeStruct((4 * rows, 4 * cols), BF16),
+            grid=(1,),
+            in_specs=[whole(v.shape) for v in (*sums, probe, right)],
+            out_specs=whole(out),
+        ),
+        out_shape=jax.ShapeDtypeStruct(out, BF16),
         compiler_params=pltpu.CompilerParams(vmem_limit_bytes=VMEM),
+        cost_estimate=pl.CostEstimate(flops=64 * 128 * out[1], bytes_accessed=8 * out[0] * out[1], transcendentals=0),
         name="outputs",
-    )(place, sums, probe, right)
+    )(place, *sums, probe, right)
 
 
 def update_kernel(s_ref, left0, left1, left2, left3, left_other, *refs):
-    rights, fits = refs[:4], refs[4:8]
-    out_ref, ordered, turned, scores = refs[-4:]
+    *inputs, out_ref, ordered, turned, weighted, scores = refs
+    rights, fits = inputs[: len(inputs) // 2], inputs[len(inputs) // 2 :]
     population, cols = ordered.shape
-    depth = population // 4
 
     @pl.when(pl.program_id(0) == 0)
     def _():
@@ -157,48 +154,45 @@
         spread = jnp.sum(centred * centred, axis=0, keepdims=True) / population
         scores[...] = centred / jnp.sqrt(spread + epsilon)
 
-    total = jnp.zeros(out_ref.shape, F32)
-    for i in range(4):
-        at = slice(i * depth, (i + 1) * depth)
-        weighted = (scores[at] * rights[i][...].astype(F32)).astype(BF16)
-        total += jnp.dot(turned[:, at], weighted, preferred_element_type=F32)
+    at = 0
+    for right in rights:
+        rows = slice(at, at + right.shape[0])
+        weighted[rows] = (scores[rows] * right[...].astype(F32)).astype(BF16)
+        at += right.shape[0]
+    total = jnp.dot(turned[...], weighted[...], preferred_element_type=F32)
     out_ref[...] = (total * (1.0 / math.sqrt(population))).astype(BF16)
 
 
-def update_part(place, left, left_other, rights, fits, fit_at, out_cols, first, cols, so_far=None):
-    block = rights[0].shape[0]
-    population = 4 * block
+def update_part(place, left, left_other, rights, out_cols):
+    population = sum(r.shape[0] for r in rights)
     depth = left[0].shape[1] // 2
     tile = 512
-    extra = [] if so_far is None else [so_far]
-    inputs = [*left, left_other, *rights, *fits, *extra]
     return pl.pallas_call(
         update_kernel,
         grid_spec=pltpu.PrefetchScalarGridSpec(
             num_scalar_prefetch=1,
-            grid=(cols // tile,),
+            grid=(out_cols // tile,),
             in_specs=[whole(left[0].shape)] * 4
             + [whole(left_other.shape)]
-            + [pl.BlockSpec((block, tile), lambda i, s: (0, i))] * 4
-            + [pl.BlockSpec((block, 128), lambda i, s: (0, fit_at // 128))] * 4
-            + [pl.BlockSpec(memory_space=pl.ANY)] * len(extra),
-            out_specs=pl.BlockSpec((depth, tile), lambda i, s: (0, i + first // tile)),
+            + [pl.BlockSpec((r.shape[0], tile), lambda i, s: (0, i)) for r in rights]
+            + [pl.BlockSpec((r.shape[0], 128), lambda i, s: (0, out_cols // 128)) for r in rights],
+            out_specs=pl.BlockSpec((depth, tile), lambda i, s: (0, i)),
             scratch_shapes=[
                 pltpu.VMEM((population, depth), BF16),
                 pltpu.VMEM((depth, population), BF16),
+                pltpu.VMEM((population, tile), BF16),
                 pltpu.VMEM((population, 1), F32),
             ],
         ),
         out_shape=jax.ShapeDtypeStruct((depth, out_cols), BF16),
-        input_output_aliases={len(inputs): 0} if extra else {},
         compiler_params=pltpu.CompilerParams(vmem_limit_bytes=VMEM),
         cost_estimate=pl.CostEstimate(
-            flops=2 * population * depth * cols,
-            bytes_accessed=2 * (population * (cols + depth) + depth * cols),
+            flops=2 * population * depth * out_cols,
+            bytes_accessed=2 * (population * (out_cols + depth) + depth * out_cols),
             transcendentals=0,
         ),
         name="update",
-    )(place, *inputs)
+    )(place, *left, left_other, *rights, *rights)
 
 
 def pieces(value):
@@ -222,10 +216,9 @@
 
     half = width // 2
 
-    first = 4 * (out_cols // 7)
     beside = jnp.stack(pieces(fitness), axis=1)
     beside = jnp.pad(beside, ((0, 0), (0, 128 - beside.shape[1])))
-    right = [jnp.concatenate([right_factors[:, :first], beside, right_factors[:, first:]], axis=1)]
+    right = [jnp.concatenate([right_factors, beside], axis=1)]
 
     away = jnp.where(c == 0, 1, -1)
 
@@ -243,7 +236,6 @@
 
     by_y = [pick(by_z, (z - y) % 4)] + [shift(pick(by_z, (z - y - d) % 4), "y", d) for d in range(1, 4)]
     by_y = jnp.stack(by_y)
-    far = apart(cols_of(weight, x - away), "x", -1, 1)
     by_y, near, weight, right[0] = together(by_y, near, weight, right[0])
 
     tok_y = by_y[:, :rows].reshape(4 * rows, width)
@@ -258,11 +250,12 @@
         sent = jnp.concatenate([tok_y, left_for((x + d) % 4)], axis=0)
         slots.append(sent if d == 0 else shift(sent, "x", d))
     slots = jnp.stack(slots)
+    far = apart(cols_of(weight, x - away), "x", -1, 1)
     right.append(apart(right[-1], "y", 1, -1))
     share = jnp.einsum(
         "mtd,md->mt", tokens.reshape(members, 2, width), left_factors, preferred_element_type=F32
     ).reshape(1, 2 * members)
-    slots, far, share, right[1], weight = together(slots, far, share, right[1], weight)
+    slots, share, right[1], weight = together(slots, share, right[1], weight)
 
     held = [slots[:, : 4 * rows].reshape(16 * rows, width)]
     held.append(apart(held[0], "z", 1, -1))
@@ -277,65 +270,57 @@
     below = jnp.concatenate(pieces(share), axis=1)
     below = jnp.pad(below, ((0, 15), (0, width - below.shape[1])))
     left = [jnp.concatenate([jnp.concatenate([mine[0], mine[1]], axis=1), below], axis=0)]
-    held[1], other[0], across[0], across[1], right[2], left[0] = together(
-        held[1], other[0], across[0], across[1], right[2], left[0]
+    held[1], other[0], far, across[0], across[1], right[2], left[0] = together(
+        held[1], other[0], far, across[0], across[1], right[2], left[0]
     )
 
     held.append(apart(held[1], "z", 1, -1))
     other.append(lax.ppermute(held[1], "c", SWAP))
     across[1] = apart(across[1], "x", 2, 2)
     right.append(apart(right[-1], "y", 1, -1))
-    left.append(apart(left[0], "z", 1, -1))
-    held[2], other[1], across[1], right[3], left[1] = together(held[2], other[1], across[1], right[3], left[1])
+    held[2], other[1], across[1], right[3], left[0] = together(held[2], other[1], across[1], right[3], left[0])
 
     held.append(apart(held[2], "z", 1, -1))
     other.append(lax.ppermute(held[2], "c", SWAP))
-    right = jnp.concatenate(right, axis=0)
-    right_a, right_b = [right[:, : first + 128]], [right[:, first + 128 :]]
-    right_a.append(apart(right_a[-1], "x", 1, -1))
-    right_b.append(apart(right_b[-1], "x", 1, -1))
-    left.append(apart(left[1], "z", 1, -1))
+    right = [jnp.concatenate(right, axis=0)]
+    right.append(apart(right[-1], "x", 1, -1))
     moved = [near, far, *across]
     part_a = base_part(place, held[0], other[0], held[2], other[2], weight, moved)
-    held[3] = after(held[3], part_a[0])
-    right_a[1] = after(right_a[1], part_a[0])
-    right_b[1] = after(right_b[1], part_a[0])
+    held[3], *part_a = together(held[3], *part_a)
     other.append(lax.ppermute(held[3], "c", SWAP))
-    right_a.append(apart(right_a[-1], "x", 1, -1))
-    right_b.append(apart(right_b[-1], "x", 1, -1))
-
+
+    def along_y(part):
+        return [part[0]] + [shift(part[-d], "y", d) for d in range(1, 4)]
+
+    def total_of(terms):
+        return sum(t.astype(F32) for t in terms[1:]) + terms[0].astype(F32)
+
+    terms_a = along_y(part_a)
+    right[1], other[3] = together(right[1], other[3])
+    right.append(apart(right[-1], "x", 1, -1))
     part_b = base_part(place, held[1], other[3], held[3], other[1], weight, moved)
-    right_a[2] = after(right_a[2], part_b[0])
-    right_b[2] = after(right_b[2], part_b[0])
-    right_a.append(apart(right_a[-1], "x", 1, -1))
-    right_b.append(apart(right_b[-1], "x", 1, -1))
-    left[2] = after(left[2], part_b[0])
-    left.append(apart(left[2], "z", 1, -1))
-
-    def onward(total, part):
-        return (apart(total, "y", 1, -1).astype(F32) + part.astype(F32)).astype(BF16)
-
-    def across_x(total):
-        return jnp.stack([total[0]] + [shift(total[d], "x", -d) for d in range(1, 4)])
-
-    sum_a = onward(part_a[0], part_a[1])
-    sum_b = onward(part_b[0], part_b[1])
-    sum_a = onward(sum_a, part_a[2])
-    sum_b = onward(sum_b, part_b[2])
-    sum_a = onward(sum_a, part_a[3])
-    left[3], sum_a = together(left[3], sum_a)
-    columns_a = across_x(sum_a)
+    terms_a[0], left[0], _ = together(terms_a[0], left[0], part_b[0])
+    sum_a = total_of(terms_a).astype(BF16)
+    sum_a, right[2], left[0], *part_b = together(sum_a, right[2], left[0], *part_b)
+    right.append(apart(right[-1], "x", 1, -1))
+    terms_b = along_y(part_b)
+    for _ in range(3):
+        left.append(apart(left[-1], "z", 1, -1))
+    sum_b = total_of(terms_b).astype(BF16)
+    sum_b, left[3], right[3] = together(sum_b, left[3], right[3])
     left_other = lax.ppermute(jnp.stack(left), "c", SWAP)
-    sum_b = after(onward(sum_b, part_b[3]), columns_a, left_other)
-    columns = jnp.concatenate([columns_a, across_x(sum_b)], axis=1)
+
+    total = jnp.concatenate([sum_a, sum_b], axis=1)
+    columns = [total[0]] + [shift(total[d], "x", -d) for d in range(1, 4)]
 
     shares = jnp.stack([v[members, : 6 * members] for v in left])
     shares = jnp.concatenate([shares, left_other[:, members, : 6 * members]]).astype(F32)
     share = jnp.sum(shares, axis=0).reshape(3, 2 * members)
     probe = jnp.sum(share, axis=0).reshape(2 * members, 1) * (noise_scale / math.sqrt(features))
+    left_other, columns[0], probe = together(left_other, columns[0], probe)
+    update = update_part(place, left, left_other, right, out_cols)
+    update, *columns = together(update, *columns)
     outputs = output_part(place, columns, probe, right_factors)
-    update = update_part(place, left, left_other, right_a, right_a, first, out_cols, 0, first)
-    update = update_part(place, left, left_other, right_b, right_a, first, out_cols, first, out_cols - first, update)
     return outputs, update
 
 

time: 192 us -> 183 us (0.953)
  local copies, waits for them, and re-layouts: 17.2 us -> 8.94 us
  Pallas kernels: 30.2 us -> 34.3 us
  other arithmetic: 7.78 us -> 5.26 us
    ppermute x25 -> x16, waiting for transfers between devices: 77.6 us -> 55 us  [apart(): return lax.ppermute(value, (axis, 'c'), perm)]
    ppermute x15 -> x18, waiting for transfers between devices: 12.9 us -> 34.9 us  [shift(): return lax.ppermute(value, axis, [(i, (i + by) % 4) for i in range(4)])]
    unnamed x72 -> x65, local copies, waits for them, and re-layouts: 8.52 us -> 1.9 us
    pallas_call x2, Pallas kernels: 14.4 us -> 19.3 us  [base_part(): pl.pallas_call(base_kernel, grid_spec=pltpu.PrefetchScalarGridSpec(num_sc...]
    ppermute x25 -> x16, starting transfers between devices: 15.9 us -> 11.3 us  [apart(): return lax.ppermute(value, (axis, 'c'), perm)]
    ppermute x15 -> x18, starting transfers between devices: 24.7 us -> 28.8 us  [shift(): return lax.ppermute(value, axis, [(i, (i + by) % 4) for i in range(4)])]
    pallas_call x2 -> x1, Pallas kernels: 13.2 us -> 11.5 us  [update_part(): pl.pallas_call(update_kernel, grid_spec=pltpu.PrefetchScalarGridSpec(num_...]
  transfers between devices with their start and end apart: 46 -> 40, of which waited for: 16 -> 19; matrix products, arithmetic and copies ran while one was open for 8% -> 6% of each run, Pallas kernels for 14% -> 17%
where the time goes in v3:
time: 183 us; the launch traced here: 182 us
  waiting for transfers between devices  90.9 us (50%)
  starting transfers between devices  40.5 us (22%)
  Pallas kernels  34.3 us (19%)
  local copies, waits for them, and re-layouts  8.94 us (5%)
  other arithmetic  5.26 us (3%)
    ppermute x16, waiting for transfers between devices, apart(): return lax.ppermute(value, (axis, 'c'), perm)  55 us
    ppermute x18, waiting for transfers between devices, shift(): return lax.ppermute(value, axis, [(i, (i + by) % 4) for i in range(4)])  34.9 us
    ppermute x18, starting transfers between devices, shift(): return lax.ppermute(value, axis, [(i, (i + by) % 4) for i in range(4)])  28.8 us
    pallas_call x2, Pallas kernels, base_part(): pl.pallas_call(base_kernel, grid_spec=pltpu.PrefetchScalarGridSpec(num_sc...  19.3 us
    pallas_call x1, Pallas kernels, update_part(): pl.pallas_call(update_kernel, grid_spec=pltpu.PrefetchScalarGridSpec(num_...  11.5 us
    ppermute x16, starting transfers between devices, apart(): return lax.ppermute(value, (axis, 'c'), perm)  11.3 us
  transfers between devices with their start and end apart: 40, of which 19 were waited for; matrix products, arithmetic and copies ran while one was open for 6% of the time, Pallas kernels for 17%

profile of v3, /device:TPU:0, one launch (start us, length us, event | category | flops | bytes accessed | tf_op | source)
XLA Modules:
  0.0 181.9 jit_solution(6613216754518776328)
XLA Ops:
  1.7 2.1 %collective-permute-start = (bf16[48,1024]{1,0:T(8,128)(2,1)S(1)}, bf16[48,1024]{1,0:T(8,128)(2,1)S(1)}, u32[]{:S(2)}, u32[]{:S(2)}) collective-permute-start(bf16[48,1024]{1,0:T(8,128)(2,1)S(1)} %get-tuple-element.131), channel_id=1, source_target_pairs={{0,2},{2,4},{4,6},{6,0},{1,3},{3,5},{5,7},{7,1},{8,10},{10,12},{12... | collective-permute-start | bytes 294920 | tf_op jit(solution)/shard_map/ppermute | solution.py:18
  3.8 3.6 %collective-permute-start.1 = (bf16[48,1024]{1,0:T(8,128)(2,1)S(1)}, bf16[48,1024]{1,0:T(8,128)(2,1)S(1)}, u32[]{:S(2)}, u32[]{:S(2)}) collective-permute-start(bf16[48,1024]{1,0:T(8,128)(2,1)S(1)} %get-tuple-element.132), channel_id=1, source_target_pairs={{0,4},{2,6},{4,0},{6,2},{1,5},{3,7},{5,1},{7,3},{8,12},{10,14},{12... | collective-permute-start | bytes 294920 | tf_op jit(solution)/shard_map/ppermute | solution.py:18
  9.6 1.6 collective-permute-start.6
  12.1 3.1 %collective-permute-start.5 = (bf16[48,1024]{1,0:T(8,128)(2,1)S(1)}, bf16[48,1024]{1,0:T(8,128)(2,1)S(1)}, u32[]{:S(2)}, u32[]{:S(2)}) collective-permute-start(bf16[48,1024]{1,0:T(8,128)(2,1)S(1)} %get-tuple-element.127), channel_id=1, source_target_pairs={{0,96},{32,0},{64,32},{96,64},{1,97},{33,1},{65,33},{97,65},{2,98}... | collective-permute-start | bytes 294920 | tf_op jit(solution)/shard_map/ppermute | solution.py:18
  17.6 1.5 collective-permute-done.5
  19.0 2.7 %collective-permute-done.4 = bf16[48,1024]{1,0:T(8,128)(2,1)S(1)} collective-permute-done((bf16[48,1024]{1,0:T(8,128)(2,1)S(1)}, bf16[48,1024]{1,0:T(8,128)(2,1)S(1)}, u32[]{:S(2)}, u32[]{:S(2)}) %collective-permute-start.4) | collective-permute-done | bytes 98336 | tf_op jit(solution)/shard_map/ppermute | solution.py:18
  22.8 1.6 collective-permute-done.6.near
  24.5 1.6 collective-permute-start.10
  26.7 2.7 %collective-permute-start.8 = (bf16[160,1024]{1,0:T(8,128)(2,1)S(1)}, bf16[160,1024]{1,0:T(8,128)(2,1)}, u32[]{:S(2)}, u32[]{:S(2)}) collective-permute-start(bf16[160,1024]{1,0:T(8,128)(2,1)S(1)} %get-tuple-element.136), channel_id=1, source_target_pairs={{0,16},{8,24},{16,0},{24,8},{1,17},{9,25},{17,1},{25,9},{2,18},{10... | collective-permute-start | bytes 983048 | tf_op jit(solution)/shard_map/ppermute | solution.py:18
  29.4 1.4 collective-permute-start.9
  33.0 4.2 %collective-permute-done.7 = bf16[160,1024]{1,0:T(8,128)(2,1)} collective-permute-done((bf16[160,1024]{1,0:T(8,128)(2,1)S(1)}, bf16[160,1024]{1,0:T(8,128)(2,1)}, u32[]{:S(2)}, u32[]{:S(2)}) %collective-permute-start.7) | collective-permute-done | bytes 327712 | tf_op jit(solution)/shard_map/ppermute | solution.py:18
  37.1 7.9 %collective-permute-done.8 = bf16[160,1024]{1,0:T(8,128)(2,1)} collective-permute-done((bf16[160,1024]{1,0:T(8,128)(2,1)S(1)}, bf16[160,1024]{1,0:T(8,128)(2,1)}, u32[]{:S(2)}, u32[]{:S(2)}) %collective-permute-start.8) | collective-permute-done | bytes 327712 | tf_op jit(solution)/shard_map/ppermute | solution.py:18
  45.1 1.3 pad_maximum_fusion
  47.9 1.7 collective-permute-start.15
  51.8 2.3 %collective-permute-done.13.far = bf16[512,896]{1,0:T(8,128)(2,1)S(1)} collective-permute-done((bf16[512,896]{1,0:T(8,128)(2,1)S(1)}, bf16[512,896]{1,0:T(8,128)(2,1)S(1)}, u32[]{:S(2)}, u32[]{:S(2)}) %collective-permute-start.13) | collective-permute-done | bytes 917536 | tf_op jit(solution)/shard_map/ppermute | solution.py:24
  54.1 11.2 %collective-permute-done.14.across0 = bf16[256,896]{1,0:T(8,128)(2,1)S(1)} collective-permute-done((bf16[256,896]{1,0:T(8,128)(2,1)S(1)}, bf16[256,896]{1,0:T(8,128)(2,1)S(1)}, u32[]{:S(2)}, u32[]{:S(2)}) %collective-permute-start.14) | collective-permute-done | bytes 458784 | tf_op jit(solution)/shard_map/ppermute | solution.py:24
  67.6 12.4 %collective-permute-done.19.across1 = bf16[256,896]{1,0:T(8,128)(2,1)S(1)} collective-permute-done((bf16[256,896]{1,0:T(8,128)(2,1)S(1)}, bf16[256,896]{1,0:T(8,128)(2,1)S(1)}, u32[]{:S(2)}, u32[]{:S(2)}) %collective-permute-start.19) | collective-permute-done | bytes 458784 | tf_op jit(solution)/shard_map/ppermute | solution.py:24
  80.0 1.6 collective-permute-done.17.own1
  84.6 9.7 %base.2 = (bf16[4,2,32,896]{3,2,1,0:T(8,128)(2,1)}, bf16[4,2,32,896]{3,2,1,0:T(8,128)(2,1)}, bf16[4,2,32,896]{3,2,1,0:T(8,128)(2,1)}, bf16[4,2,32,896]{3,2,1,0:T(8,128)(2,1)}) custom-call(s32[4]{0:T(128)} %pad_add_fusion.s_ref, bf16[512,1024]{1,0:T(8,128)(2,1)} %bitcast.71, bf16[512,1024]{1,0:T(8,128)(2,1)} %copy-done.20, ...), custom_call_target="tpu_custom_call" | custom-call | flops 3758096384 | bytes 9699328 | tf_op jit(solution)/shard_map/base/pallas_call | solution.py:71
  94.3 3.6 %collective-permute-done.21.own1 = bf16[512,1024]{1,0:T(8,128)(2,1)S(1)} collective-permute-done((bf16[512,1024]{1,0:T(8,128)(2,1)}, bf16[512,1024]{1,0:T(8,128)(2,1)S(1)}, u32[]{:S(2)}, u32[]{:S(2)}) %collective-permute-start.21) | collective-permute-done | bytes 1048608 | tf_op jit(solution)/shard_map/ppermute | solution.py:24
  97.9 10.0 %collective-permute-done.26.refs_1_.refs_5_ = bf16[256,3712]{1,0:T(8,128)(2,1)} collective-permute-done((bf16[256,3712]{1,0:T(8,128)(2,1)S(1)}, bf16[256,3712]{1,0:T(8,128)(2,1)}, u32[]{:S(2)}, u32[]{:S(2)}) %collective-permute-start.26) | collective-permute-done | bytes 1900576 | tf_op jit(solution)/shard_map/ppermute | solution.py:24
  108.9 1.3 collective-permute-start.23
  110.2 2.0 %collective-permute-start.24 = (bf16[4,2,32,896]{3,2,1,0:T(8,128)(2,1)}, bf16[4,2,32,896]{3,2,1,0:T(8,128)(2,1)S(1)}, u32[]{:S(2)}, u32[]{:S(2)}) collective-permute-start(bf16[4,2,32,896]{3,2,1,0:T(8,128)(2,1)} %get-tuple-element.85), channel_id=1, source_target_pairs={{0,64},{32,96},{64,0},{96,32},{1,65},{33,97},{65,1},{97,33},{2,66}... | collective-permute-start | bytes 1376264 | tf_op jit(solution)/shard_map/ppermute | solution.py:18
  113.2 9.7 %base.3 = (bf16[4,2,32,896]{3,2,1,0:T(8,128)(2,1)}, bf16[4,2,32,896]{3,2,1,0:T(8,128)(2,1)}, bf16[4,2,32,896]{3,2,1,0:T(8,128)(2,1)}, bf16[4,2,32,896]{3,2,1,0:T(8,128)(2,1)}) custom-call(s32[4]{0:T(128)} %pad_add_fusion.s_ref, bf16[512,1024]{1,0:T(8,128)(2,1)} %copy-done.19, bf16[512,1024]{1,0:T(8,128)(2,1)} %copy-done.23, bf16[512,1024]{1,0:T(8,128)(2,1)} %copy-done.22, ...), custom_call_target="tpu_custom_call" | custom-call | flops 3758096384 | bytes 9699328 | tf_op jit(solution)/shard_map/base/pallas_call | solution.py:71
  122.9 9.2 %collective-permute-done.23 = bf16[4,2,32,896]{3,2,1,0:T(8,128)(2,1)S(1)} collective-permute-done((bf16[4,2,32,896]{3,2,1,0:T(8,128)(2,1)}, bf16[4,2,32,896]{3,2,1,0:T(8,128)(2,1)S(1)}, u32[]{:S(2)}, u32[]{:S(2)}) %collective-permute-start.23) | collective-permute-done | bytes 458784 | tf_op jit(solution)/shard_map/ppermute | solution.py:18
  135.3 3.6 %collective-permute-start.32 = (bf16[4,2,32,896]{3,2,1,0:T(8,128)(2,1)S(1)}, bf16[4,2,32,896]{3,2,1,0:T(8,128)(2,1)S(1)}, u32[]{:S(2)}, u32[]{:S(2)}) collective-permute-start(bf16[4,2,32,896]{3,2,1,0:T(8,128)(2,1)S(1)} %copy-done.28), channel_id=1, source_target_pairs={{0,64},{32,96},{64,0},{96,32},{1,65},{33,97},{65,1},{97,33},{2,66}... | collective-permute-start | bytes 1376264 | tf_op jit(solution)/shard_map/ppermute | solution.py:18
  139.7 5.7 %collective-permute-done.29.left1 = bf16[80,1024]{1,0:T(8,128)(2,1)S(1)} collective-permute-done((bf16[80,1024]{1,0:T(8,128)(2,1)S(1)}, bf16[80,1024]{1,0:T(8,128)(2,1)S(1)}, u32[]{:S(2)}, u32[]{:S(2)}) %collective-permute-start.29) | collective-permute-done | bytes 163872 | tf_op jit(solution)/shard_map/ppermute | solution.py:24
  145.4 6.5 %collective-permute-done.30.left2 = bf16[80,1024]{1,0:T(8,128)(2,1)S(1)} collective-permute-done((bf16[80,1024]{1,0:T(8,128)(2,1)S(1)}, bf16[80,1024]{1,0:T(8,128)(2,1)S(1)}, u32[]{:S(2)}, u32[]{:S(2)}) %collective-permute-start.30) | collective-permute-done | bytes 163872 | tf_op jit(solution)/shard_map/ppermute | solution.py:24
  151.9 7.2 %collective-permute-done.32 = bf16[4,2,32,896]{3,2,1,0:T(8,128)(2,1)S(1)} collective-permute-done((bf16[4,2,32,896]{3,2,1,0:T(8,128)(2,1)S(1)}, bf16[4,2,32,896]{3,2,1,0:T(8,128)(2,1)S(1)}, u32[]{:S(2)}, u32[]{:S(2)}) %collective-permute-start.32) | collective-permute-done | bytes 458784 | tf_op jit(solution)/shard_map/ppermute | solution.py:18
  161.7 2.2 %collective-permute-start.38 = (bf16[4,32,896]{2,1,0:T(8,128)(2,1)S(1)}, bf16[4,32,896]{2,1,0:T(8,128)(2,1)S(1)}, u32[]{:S(2)}, u32[]{:S(2)}) collective-permute-start(bf16[4,32,896]{2,1,0:T(8,128)(2,1)S(1)} %get-tuple-element.123), channel_id=1, source_target_pairs={{0,16},{8,24},{16,0},{24,8},{1,17},{9,25},{17,1},{25,9},{2,18},{10... | collective-permute-start | bytes 688136 | tf_op jit(solution)/shard_map/ppermute | solution.py:18
  166.0 11.5 %update.1 = bf16[512,3584]{1,0:T(8,128)(2,1)} custom-call(s32[4]{0:T(128)} %pad_add_fusion.s_ref, bf16[80,1024]{1,0:T(8,128)(2,1)} %copy-done.4, bf16[80,1024]{1,0:T(8,128)(2,1)} %copy-done.8, bf16[80,1024]{1,0:T(8,128)(2,1)} %copy-done.9, bf16[80,1024]{1,0:T(8,128)(2,1)} %copy-done.10, bf16[4,80,1024]{2,1,0:T(8,128)(2,1)} %copy-done.7, ...), custom_call_target="tpu_custom_call" | custom-call | flops 3758096384 | bytes 12058624 | tf_op jit(solution)/shard_map/update/pallas_call | solution.py:170
  178.5 3.4 %outputs.1 = bf16[128,3584]{1,0:T(8,128)(2,1)} custom-call(s32[4]{0:T(128)} %pad_add_fusion.s_ref, bf16[4,32,896]{2,1,0:T(8,128)(2,1)} %get-tuple-element.112.refs_0_, bf16[4,32,896]{2,1,0:T(8,128)(2,1)} %copy-done.16, bf16[4,32,896]{2,1,0:T(8,128)(2,1)} %copy-done.15, bf16[4,32,896]{2,1,0:T(8,128)(2,1)} %copy-done.14, f32[128,1]{1,0:T(8,128)} %copy.18.refs_4_, ...), custom_call_target="tpu_custom_call" | custom-call | flops 29360128 | bytes 3670016 | tf_op jit(solution)/shard_map/outputs/pallas_call | solution.py:113
  (161 shorter events, 30.3 us)
Async XLA Ops:
  1.7 9.8 %collective-permute-start = (bf16[48,1024]{1,0:T(8,128)(2,1)S(1)}, bf16[48,1024]{1,0:T(8,128)(2,1)S(1)}, u32[]{:S(2)}, u32[]{:S(2)}) collective-permute-start(bf16[48,1024]{1,0:T(8,128)(2,1)S(1)} %get-tuple-element.131), channel_id=1, source_target_pairs={{0,2},{2,4},{4,6},{6,0},{1,3},{3,5},{5,7},{7,1},{8,10},{10,12},{12... | collective-permute-start | bytes 294920 | tf_op jit(solution)/shard_map/ppermute | solution.py:18
  3.8 8.2 %collective-permute-start.1 = (bf16[48,1024]{1,0:T(8,128)(2,1)S(1)}, bf16[48,1024]{1,0:T(8,128)(2,1)S(1)}, u32[]{:S(2)}, u32[]{:S(2)}) collective-permute-start(bf16[48,1024]{1,0:T(8,128)(2,1)S(1)} %get-tuple-element.132), channel_id=1, source_target_pairs={{0,4},{2,6},{4,0},{6,2},{1,5},{3,7},{5,1},{7,3},{8,12},{10,14},{12... | collective-permute-start | bytes 294920 | tf_op jit(solution)/shard_map/ppermute | solution.py:18
  9.6 14.8 %collective-permute-start.6 = (bf16[512,896]{1,0:T(8,128)(2,1)S(1)}, bf16[512,896]{1,0:T(8,128)(2,1)}, u32[]{:S(2)}, u32[]{:S(2)}) collective-permute-start(bf16[512,896]{1,0:T(8,128)(2,1)S(1)} %constant_dynamic-slice_fusion.4), channel_id=1, source_target_pairs={{0,8},{8,16},{16,24},{24,0},{1,25},{9,1},{17,9},{25,17},{2,10},{10... | collective-permute-start | bytes 2752520 | tf_op jit(solution)/shard_map/ppermute | solution.py:24
  12.1 7.0 %collective-permute-start.5 = (bf16[48,1024]{1,0:T(8,128)(2,1)S(1)}, bf16[48,1024]{1,0:T(8,128)(2,1)S(1)}, u32[]{:S(2)}, u32[]{:S(2)}) collective-permute-start(bf16[48,1024]{1,0:T(8,128)(2,1)S(1)} %get-tuple-element.127), channel_id=1, source_target_pairs={{0,96},{32,0},{64,32},{96,64},{1,97},{33,1},{65,33},{97,65},{2,98}... | collective-permute-start | bytes 294920 | tf_op jit(solution)/shard_map/ppermute | solution.py:18
  24.5 21.9 %collective-permute-start.10 = (bf16[64,3712]{1,0:T(8,128)(2,1)S(1)}, bf16[64,3712]{1,0:T(8,128)(2,1)S(1)}, u32[]{:S(2)}, u32[]{:S(2)}) collective-permute-start(bf16[64,3712]{1,0:T(8,128)(2,1)S(1)} %fusion.1), channel_id=1, source_target_pairs={{0,32},{32,64},{64,96},{96,0},{1,97},{33,1},{65,33},{97,65},{2,34}... | collective-permute-start | bytes 1425416 | tf_op jit(solution)/shard_map/ppermute | solution.py:24
  26.3 10.8 %collective-permute-start.7 = (bf16[160,1024]{1,0:T(8,128)(2,1)S(1)}, bf16[160,1024]{1,0:T(8,128)(2,1)}, u32[]{:S(2)}, u32[]{:S(2)}) collective-permute-start(bf16[160,1024]{1,0:T(8,128)(2,1)S(1)} %get-tuple-element.135), channel_id=1, source_target_pairs={{0,8},{8,16},{16,24},{24,0},{1,9},{9,17},{17,25},{25,1},{2,10},{10... | collective-permute-start | bytes 983048 | tf_op jit(solution)/shard_map/ppermute | solution.py:18
  26.7 18.4 %collective-permute-start.8 = (bf16[160,1024]{1,0:T(8,128)(2,1)S(1)}, bf16[160,1024]{1,0:T(8,128)(2,1)}, u32[]{:S(2)}, u32[]{:S(2)}) collective-permute-start(bf16[160,1024]{1,0:T(8,128)(2,1)S(1)} %get-tuple-element.136), channel_id=1, source_target_pairs={{0,16},{8,24},{16,0},{24,8},{1,17},{9,25},{17,1},{25,9},{2,18},{10... | collective-permute-start | bytes 983048 | tf_op jit(solution)/shard_map/ppermute | solution.py:18
  29.4 15.7 %collective-permute-start.9 = (bf16[160,1024]{1,0:T(8,128)(2,1)S(1)}, bf16[160,1024]{1,0:T(8,128)(2,1)}, u32[]{:S(2)}, u32[]{:S(2)}) collective-permute-start(bf16[160,1024]{1,0:T(8,128)(2,1)S(1)} %get-tuple-element.137), channel_id=1, source_target_pairs={{0,24},{8,0},{16,8},{24,16},{1,25},{9,1},{17,9},{25,17},{2,26},{10... | collective-permute-start | bytes 983048 | tf_op jit(solution)/shard_map/ppermute | solution.py:18
  32.9 21.2 %collective-permute-start.13 = (bf16[512,896]{1,0:T(8,128)(2,1)S(1)}, bf16[512,896]{1,0:T(8,128)(2,1)S(1)}, u32[]{:S(2)}, u32[]{:S(2)}) collective-permute-start(bf16[512,896]{1,0:T(8,128)(2,1)S(1)} %constant_dynamic-slice_fusion.1), channel_id=1, source_target_pairs={{0,24},{8,0},{16,8},{24,16},{1,9},{9,17},{17,25},{25,1},{2,26},{10... | collective-permute-start | bytes 2752520 | tf_op jit(solution)/shard_map/ppermute | solution.py:24
  46.5 18.7 %collective-permute-start.12 = (bf16[512,1024]{1,0:T(8,128)(2,1)S(1)}, bf16[512,1024]{1,0:T(8,128)(2,1)S(1)}, u32[]{:S(2)}, u32[]{:S(2)}) collective-permute-start(bf16[512,1024]{1,0:T(8,128)(2,1)S(1)} %bitcast.69), channel_id=1, source_target_pairs={{0,1},{1,0},{2,3},{3,2},{4,5},{5,4},{6,7},{7,6},{8,9},{9,8},{10,11... | collective-permute-start | bytes 3145736 | tf_op jit(solution)/shard_map/ppermute | solution.py:262
  46.6 18.7 %collective-permute-start.11 = (bf16[512,1024]{1,0:T(8,128)(2,1)S(1)}, bf16[512,1024]{1,0:T(8,128)(2,1)S(1)}, u32[]{:S(2)}, u32[]{:S(2)}) collective-permute-start(bf16[512,1024]{1,0:T(8,128)(2,1)S(1)} %bitcast.70), channel_id=1, source_target_pairs={{0,2},{2,4},{4,6},{6,0},{1,7},{3,1},{5,3},{7,5},{8,10},{10,12},{12... | collective-permute-start | bytes 3145736 | tf_op jit(solution)/shard_map/ppermute | solution.py:24
  47.9 17.4 %collective-permute-start.15 = (bf16[64,3712]{1,0:T(8,128)(2,1)S(1)}, bf16[64,3712]{1,0:T(8,128)(2,1)S(1)}, u32[]{:S(2)}, u32[]{:S(2)}) collective-permute-start(bf16[64,3712]{1,0:T(8,128)(2,1)S(1)} %collective-permute-done.10), channel_id=1, source_target_pairs={{0,32},{32,64},{64,96},{96,0},{1,97},{33,1},{65,33},{97,65},{2,34}... | collective-permute-start | bytes 1425416 | tf_op jit(solution)/shard_map/ppermute | solution.py:24
  50.8 14.4 %collective-permute-start.14 = (bf16[256,896]{1,0:T(8,128)(2,1)S(1)}, bf16[256,896]{1,0:T(8,128)(2,1)S(1)}, u32[]{:S(2)}, u32[]{:S(2)}) collective-permute-start(bf16[256,896]{1,0:T(8,128)(2,1)S(1)} %get-tuple-element.119), channel_id=1, source_target_pairs={{0,16},{8,24},{16,0},{24,8},{1,17},{9,25},{17,1},{25,9},{2,18},{10... | collective-permute-start | bytes 1376264 | tf_op jit(solution)/shard_map/ppermute | solution.py:24
  65.3 14.6 %collective-permute-start.18 = (bf16[512,1024]{1,0:T(8,128)(2,1)S(1)}, bf16[512,1024]{1,0:T(8,128)(2,1)S(1)}, u32[]{:S(2)}, u32[]{:S(2)}) collective-permute-start(bf16[512,1024]{1,0:T(8,128)(2,1)S(1)} %collective-permute-done.11.own0), channel_id=1, source_target_pairs={{0,1},{1,0},{2,3},{3,2},{4,5},{5,4},{6,7},{7,6},{8,9},{9,8},{10,11... | collective-permute-start | bytes 3145736 | tf_op jit(solution)/shard_map/ppermute | solution.py:278
  65.4 16.2 %collective-permute-start.17 = (bf16[512,1024]{1,0:T(8,128)(2,1)S(1)}, bf16[512,1024]{1,0:T(8,128)(2,1)}, u32[]{:S(2)}, u32[]{:S(2)}) collective-permute-start(bf16[512,1024]{1,0:T(8,128)(2,1)S(1)} %collective-permute-done.11.own0), channel_id=1, source_target_pairs={{0,2},{2,4},{4,6},{6,0},{1,7},{3,1},{5,3},{7,5},{8,10},{10,12},{12... | collective-permute-start | bytes 3145736 | tf_op jit(solution)/shard_map/ppermute | solution.py:24
  66.1 13.9 %collective-permute-start.20 = (bf16[64,3712]{1,0:T(8,128)(2,1)S(1)}, bf16[64,3712]{1,0:T(8,128)(2,1)S(1)}, u32[]{:S(2)}, u32[]{:S(2)}) collective-permute-start(bf16[64,3712]{1,0:T(8,128)(2,1)S(1)} %collective-permute-done.15), channel_id=1, source_target_pairs={{0,32},{32,64},{64,96},{96,0},{1,97},{33,1},{65,33},{97,65},{2,34}... | collective-permute-start | bytes 1425416 | tf_op jit(solution)/shard_map/ppermute | solution.py:24
  66.6 13.3 %collective-permute-start.19 = (bf16[256,896]{1,0:T(8,128)(2,1)S(1)}, bf16[256,896]{1,0:T(8,128)(2,1)S(1)}, u32[]{:S(2)}, u32[]{:S(2)}) collective-permute-start(bf16[256,896]{1,0:T(8,128)(2,1)S(1)} %get-tuple-element.71), channel_id=1, source_target_pairs={{0,16},{8,24},{16,0},{24,8},{1,17},{9,25},{17,1},{25,9},{2,18},{10... | collective-permute-start | bytes 1376264 | tf_op jit(solution)/shard_map/ppermute | solution.py:24
  81.6 16.3 %collective-permute-start.21 = (bf16[512,1024]{1,0:T(8,128)(2,1)}, bf16[512,1024]{1,0:T(8,128)(2,1)S(1)}, u32[]{:S(2)}, u32[]{:S(2)}) collective-permute-start(bf16[512,1024]{1,0:T(8,128)(2,1)} %collective-permute-done.17.own1), channel_id=1, source_target_pairs={{0,2},{2,4},{4,6},{6,0},{1,7},{3,1},{5,3},{7,5},{8,10},{10,12},{12... | collective-permute-start | bytes 3145736 | tf_op jit(solution)/shard_map/ppermute | solution.py:24
  82.5 25.5 %collective-permute-start.26 = (bf16[256,3712]{1,0:T(8,128)(2,1)S(1)}, bf16[256,3712]{1,0:T(8,128)(2,1)}, u32[]{:S(2)}, u32[]{:S(2)}) collective-permute-start(bf16[256,3712]{1,0:T(8,128)(2,1)S(1)} %constant_dynamic-update-slice_fusion.refs_0_.refs_4_), channel_id=1, source_target_pairs={{0,8},{8,16},{16,24},{24,0},{1,25},{9,1},{17,9},{25,17},{2,10},{10... | collective-permute-start | bytes 5701640 | tf_op jit(solution)/shard_map/ppermute | solution.py:24
  97.9 10.0 %collective-permute-start.27 = (bf16[512,1024]{1,0:T(8,128)(2,1)S(1)}, bf16[512,1024]{1,0:T(8,128)(2,1)S(1)}, u32[]{:S(2)}, u32[]{:S(2)}) collective-permute-start(bf16[512,1024]{1,0:T(8,128)(2,1)S(1)} %collective-permute-done.21.own1), channel_id=1, source_target_pairs={{0,1},{1,0},{2,3},{3,2},{4,5},{5,4},{6,7},{7,6},{8,9},{9,8},{10,11... | collective-permute-start | bytes 3145736 | tf_op jit(solution)/shard_map/ppermute | solution.py:290
  108.0 26.2 %collective-permute-start.28 = (bf16[256,3712]{1,0:T(8,128)(2,1)}, bf16[256,3712]{1,0:T(8,128)(2,1)S(1)}, u32[]{:S(2)}, u32[]{:S(2)}) collective-permute-start(bf16[256,3712]{1,0:T(8,128)(2,1)} %collective-permute-done.26.refs_1_.refs_5_), channel_id=1, source_target_pairs={{0,8},{8,16},{16,24},{24,0},{1,25},{9,1},{17,9},{25,17},{2,10},{10... | collective-permute-start | bytes 5701640 | tf_op jit(solution)/shard_map/ppermute | solution.py:24
  108.9 23.2 %collective-permute-start.23 = (bf16[4,2,32,896]{3,2,1,0:T(8,128)(2,1)}, bf16[4,2,32,896]{3,2,1,0:T(8,128)(2,1)S(1)}, u32[]{:S(2)}, u32[]{:S(2)}) collective-permute-start(bf16[4,2,32,896]{3,2,1,0:T(8,128)(2,1)} %get-tuple-element.84), channel_id=1, source_target_pairs={{0,32},{32,64},{64,96},{96,0},{1,33},{33,65},{65,97},{97,1},{2,34}... | collective-permute-start | bytes 1376264 | tf_op jit(solution)/shard_map/ppermute | solution.py:18
  110.2 21.9 %collective-permute-start.24 = (bf16[4,2,32,896]{3,2,1,0:T(8,128)(2,1)}, bf16[4,2,32,896]{3,2,1,0:T(8,128)(2,1)S(1)}, u32[]{:S(2)}, u32[]{:S(2)}) collective-permute-start(bf16[4,2,32,896]{3,2,1,0:T(8,128)(2,1)} %get-tuple-element.85), channel_id=1, source_target_pairs={{0,64},{32,96},{64,0},{96,32},{1,65},{33,97},{65,1},{97,33},{2,66}... | collective-permute-start | bytes 1376264 | tf_op jit(solution)/shard_map/ppermute | solution.py:18
  112.2 20.6 %collective-permute-start.25 = (bf16[4,2,32,896]{3,2,1,0:T(8,128)(2,1)}, bf16[4,2,32,896]{3,2,1,0:T(8,128)(2,1)}, u32[]{:S(2)}, u32[]{:S(2)}) collective-permute-start(bf16[4,2,32,896]{3,2,1,0:T(8,128)(2,1)} %get-tuple-element.86), channel_id=1, source_target_pairs={{0,96},{32,0},{64,32},{96,64},{1,97},{33,1},{65,33},{97,65},{2,98}... | collective-permute-start | bytes 1376264 | tf_op jit(solution)/shard_map/ppermute | solution.py:18
  134.1 25.2 %collective-permute-start.35 = (bf16[256,3712]{1,0:T(8,128)(2,1)S(1)}, bf16[256,3712]{1,0:T(8,128)(2,1)S(1)}, u32[]{:S(2)}, u32[]{:S(2)}) collective-permute-start(bf16[256,3712]{1,0:T(8,128)(2,1)S(1)} %collective-permute-done.28.refs_2_.refs_6_), channel_id=1, source_target_pairs={{0,8},{8,16},{16,24},{24,0},{1,25},{9,1},{17,9},{25,17},{2,10},{10... | collective-permute-start | bytes 5701640 | tf_op jit(solution)/shard_map/ppermute | solution.py:24
  134.5 17.4 %collective-permute-start.31 = (bf16[4,2,32,896]{3,2,1,0:T(8,128)(2,1)S(1)}, bf16[4,2,32,896]{3,2,1,0:T(8,128)(2,1)S(1)}, u32[]{:S(2)}, u32[]{:S(2)}) collective-permute-start(bf16[4,2,32,896]{3,2,1,0:T(8,128)(2,1)S(1)} %copy-done.29), channel_id=1, source_target_pairs={{0,32},{32,64},{64,96},{96,0},{1,33},{33,65},{65,97},{97,1},{2,34}... | collective-permute-start | bytes 1376264 | tf_op jit(solution)/shard_map/ppermute | solution.py:18
  135.3 23.8 %collective-permute-start.32 = (bf16[4,2,32,896]{3,2,1,0:T(8,128)(2,1)S(1)}, bf16[4,2,32,896]{3,2,1,0:T(8,128)(2,1)S(1)}, u32[]{:S(2)}, u32[]{:S(2)}) collective-permute-start(bf16[4,2,32,896]{3,2,1,0:T(8,128)(2,1)S(1)} %copy-done.28), channel_id=1, source_target_pairs={{0,64},{32,96},{64,0},{96,32},{1,65},{33,97},{65,1},{97,33},{2,66}... | collective-permute-start | bytes 1376264 | tf_op jit(solution)/shard_map/ppermute | solution.py:18
  138.8 20.3 %collective-permute-start.33 = (bf16[4,2,32,896]{3,2,1,0:T(8,128)(2,1)S(1)}, bf16[4,2,32,896]{3,2,1,0:T(8,128)(2,1)S(1)}, u32[]{:S(2)}, u32[]{:S(2)}) collective-permute-start(bf16[4,2,32,896]{3,2,1,0:T(8,128)(2,1)S(1)} %copy-done.27), channel_id=1, source_target_pairs={{0,96},{32,0},{64,32},{96,64},{1,97},{33,1},{65,33},{97,65},{2,98}... | collective-permute-start | bytes 1376264 | tf_op jit(solution)/shard_map/ppermute | solution.py:18
  151.9 7.5 %collective-permute-start.34 = (bf16[80,1024]{1,0:T(8,128)(2,1)S(1)}, bf16[80,1024]{1,0:T(8,128)(2,1)S(1)}, u32[]{:S(2)}, u32[]{:S(2)}) collective-permute-start(bf16[80,1024]{1,0:T(8,128)(2,1)S(1)} %collective-permute-done.30.left2), channel_id=1, source_target_pairs={{0,2},{2,4},{4,6},{6,0},{1,7},{3,1},{5,3},{7,5},{8,10},{10,12},{12... | collective-permute-start | bytes 491528 | tf_op jit(solution)/shard_map/ppermute | solution.py:24
  160.8 16.7 %collective-permute-start.39 = (bf16[4,32,896]{2,1,0:T(8,128)(2,1)S(1)}, bf16[4,32,896]{2,1,0:T(8,128)(2,1)S(1)}, u32[]{:S(2)}, u32[]{:S(2)}) collective-permute-start(bf16[4,32,896]{2,1,0:T(8,128)(2,1)S(1)} %get-tuple-element.122), channel_id=1, source_target_pairs={{0,8},{8,16},{16,24},{24,0},{1,9},{9,17},{17,25},{25,1},{2,10},{10... | collective-permute-start | bytes 688136 | tf_op jit(solution)/shard_map/ppermute | solution.py:18
  161.7 15.9 %collective-permute-start.38 = (bf16[4,32,896]{2,1,0:T(8,128)(2,1)S(1)}, bf16[4,32,896]{2,1,0:T(8,128)(2,1)S(1)}, u32[]{:S(2)}, u32[]{:S(2)}) collective-permute-start(bf16[4,32,896]{2,1,0:T(8,128)(2,1)S(1)} %get-tuple-element.123), channel_id=1, source_target_pairs={{0,16},{8,24},{16,0},{24,8},{1,17},{9,25},{17,1},{25,9},{2,18},{10... | collective-permute-start | bytes 688136 | tf_op jit(solution)/shard_map/ppermute | solution.py:18
  163.9 13.7 %collective-permute-start.37 = (bf16[4,32,896]{2,1,0:T(8,128)(2,1)S(1)}, bf16[4,32,896]{2,1,0:T(8,128)(2,1)S(1)}, u32[]{:S(2)}, u32[]{:S(2)}) collective-permute-start(bf16[4,32,896]{2,1,0:T(8,128)(2,1)S(1)} %get-tuple-element.124), channel_id=1, source_target_pairs={{0,24},{8,0},{16,8},{24,16},{1,25},{9,1},{17,9},{25,17},{2,26},{10... | collective-permute-start | bytes 688136 | tf_op jit(solution)/shard_map/ppermute | solution.py:18
  (38 other events, 474.6 us)

commit v4 on v3

--- a/solution.py
+++ b/solution.py
@@ -104,7 +104,7 @@
             k = lax.rem(jnp.where(c == 0, z - zz, zz - z) + 4, 4)
             at = slice(zz * rows, (zz + 1) * rows)
             out = sums[d][lax.rem(k, 2) * 2 + lax.div(k, 2)].astype(F32)
-            out_ref[at, lanes] = (out + probe_ref[at] * right[at]).astype(BF16)
+            out_ref[at, lanes] = (out + probe_ref[at, 0:1] * right[at]).astype(BF16)
 
 
 def output_part(place, sums, probe, right):
@@ -166,7 +166,7 @@
 def update_part(place, left, left_other, rights, out_cols):
     population = sum(r.shape[0] for r in rights)
     depth = left[0].shape[1] // 2
-    tile = 512
+    tile = 896
     return pl.pallas_call(
         update_kernel,
         grid_spec=pltpu.PrefetchScalarGridSpec(
@@ -278,7 +278,7 @@
     other.append(lax.ppermute(held[1], "c", SWAP))
     across[1] = apart(across[1], "x", 2, 2)
     right.append(apart(right[-1], "y", 1, -1))
-    held[2], other[1], across[1], right[3], left[0] = together(held[2], other[1], across[1], right[3], left[0])
+    held[2], other[1], across[1], left[0] = together(held[2], other[1], across[1], left[0])
 
     held.append(apart(held[2], "z", 1, -1))
     other.append(lax.ppermute(held[2], "c", SWAP))
@@ -301,13 +301,13 @@
     part_b = base_part(place, held[1], other[3], held[3], other[1], weight, moved)
     terms_a[0], left[0], _ = together(terms_a[0], left[0], part_b[0])
     sum_a = total_of(terms_a).astype(BF16)
-    sum_a, right[2], left[0], *part_b = together(sum_a, right[2], left[0], *part_b)
+    sum_a, right[2], left[0] = together(sum_a, right[2], left[0])
     right.append(apart(right[-1], "x", 1, -1))
     terms_b = along_y(part_b)
     for _ in range(3):
         left.append(apart(left[-1], "z", 1, -1))
     sum_b = total_of(terms_b).astype(BF16)
-    sum_b, left[3], right[3] = together(sum_b, left[3], right[3])
+    sum_b, left[3] = together(sum_b, left[3])
     left_other = lax.ppermute(jnp.stack(left), "c", SWAP)
 
     total = jnp.concatenate([sum_a, sum_b], axis=1)
@@ -317,7 +317,8 @@
     shares = jnp.concatenate([shares, left_other[:, members, : 6 * members]]).astype(F32)
     share = jnp.sum(shares, axis=0).reshape(3, 2 * members)
     probe = jnp.sum(share, axis=0).reshape(2 * members, 1) * (noise_scale / math.sqrt(features))
-    left_other, columns[0], probe = together(left_other, columns[0], probe)
+    probe = jnp.broadcast_to(probe, (2 * members, 128))
+    right[3], left_other, columns[0], probe = together(right[3], left_other, columns[0], probe)
     update = update_part(place, left, left_other, right, out_cols)
     update, *columns = together(update, *columns)
     outputs = output_part(place, columns, probe, right_factors)

time: 183 us -> 182 us (level)
  waiting for transfers between devices: 90.9 us -> 84.2 us
  starting transfers between devices: 40.5 us -> 44.3 us
  local copies, waits for them, and re-layouts: 8.94 us -> 11.2 us
    ppermute x18, waiting for transfers between devices: 34.9 us -> 25.4 us  [shift(): return lax.ppermute(value, axis, [(i, (i + by) % 4) for i in range(4)])]
    ppermute x18, starting transfers between devices: 28.8 us -> 34 us  [shift(): return lax.ppermute(value, axis, [(i, (i + by) % 4) for i in range(4)])]
    unnamed x65 -> x59, local copies, waits for them, and re-layouts: 1.9 us -> 5.03 us
    ppermute x16, waiting for transfers between devices: 55 us -> 57.4 us  [apart(): return lax.ppermute(value, (axis, 'c'), perm)]
  transfers between devices with their start and end apart: 40 -> 40, of which waited for: 19 -> 21; matrix products, arithmetic and copies ran while one was open for 6% -> 6% of each run, Pallas kernels for 17% -> 17%
where the time goes in v4:
time: 182 us; the launch traced here: 181 us
  waiting for transfers between devices  84.2 us (46%)
  starting transfers between devices  44.3 us (24%)
  Pallas kernels  33.5 us (18%)
  local copies, waits for them, and re-layouts  11.2 us (6%)
  other arithmetic  5.26 us (3%)
    ppermute x16, waiting for transfers between devices, apart(): return lax.ppermute(value, (axis, 'c'), perm)  57.4 us
    ppermute x18, starting transfers between devices, shift(): return lax.ppermute(value, axis, [(i, (i + by) % 4) for i in range(4)])  34 us
    ppermute x18, waiting for transfers between devices, shift(): return lax.ppermute(value, axis, [(i, (i + by) % 4) for i in range(4)])  25.4 us
    pallas_call x2, Pallas kernels, base_part(): pl.pallas_call(base_kernel, grid_spec=pltpu.PrefetchScalarGridSpec(num_sc...  19.4 us
    pallas_call x1, Pallas kernels, update_part(): pl.pallas_call(update_kernel, grid_spec=pltpu.PrefetchScalarGridSpec(num_...  10.7 us
    ppermute x16, starting transfers between devices, apart(): return lax.ppermute(value, (axis, 'c'), perm)  9.92 us
    unnamed x59, local copies, waits for them, and re-layouts  5.03 us
  transfers between devices with their start and end apart: 40, of which 21 were waited for; matrix products, arithmetic and copies ran while one was open for 6% of the time, Pallas kernels for 17%

profile of v4, /device:TPU:0, one launch (start us, length us, event | category | flops | bytes accessed | tf_op | source)
XLA Modules:
  0.0 180.5 jit_solution(6426914148781383566)
XLA Ops:
  1.7 2.1 %collective-permute-start = (bf16[48,1024]{1,0:T(8,128)(2,1)S(1)}, bf16[48,1024]{1,0:T(8,128)(2,1)S(1)}, u32[]{:S(2)}, u32[]{:S(2)}) collective-permute-start(bf16[48,1024]{1,0:T(8,128)(2,1)S(1)} %get-tuple-element.121), channel_id=1, source_target_pairs={{0,2},{2,4},{4,6},{6,0},{1,3},{3,5},{5,7},{7,1},{8,10},{10,12},{12... | collective-permute-start | bytes 294920 | tf_op jit(solution)/shard_map/ppermute | solution.py:18
  3.8 3.6 %collective-permute-start.1 = (bf16[48,1024]{1,0:T(8,128)(2,1)S(1)}, bf16[48,1024]{1,0:T(8,128)(2,1)S(1)}, u32[]{:S(2)}, u32[]{:S(2)}) collective-permute-start(bf16[48,1024]{1,0:T(8,128)(2,1)S(1)} %get-tuple-element.122), channel_id=1, source_target_pairs={{0,4},{2,6},{4,0},{6,2},{1,5},{3,7},{5,1},{7,3},{8,12},{10,14},{12... | collective-permute-start | bytes 294920 | tf_op jit(solution)/shard_map/ppermute | solution.py:18
  9.6 1.6 collective-permute-start.6
  12.1 3.1 %collective-permute-start.5 = (bf16[48,1024]{1,0:T(8,128)(2,1)S(1)}, bf16[48,1024]{1,0:T(8,128)(2,1)S(1)}, u32[]{:S(2)}, u32[]{:S(2)}) collective-permute-start(bf16[48,1024]{1,0:T(8,128)(2,1)S(1)} %get-tuple-element.117), channel_id=1, source_target_pairs={{0,96},{32,0},{64,32},{96,64},{1,97},{33,1},{65,33},{97,65},{2,98}... | collective-permute-start | bytes 294920 | tf_op jit(solution)/shard_map/ppermute | solution.py:18
  16.9 2.1 %collective-permute-done.5 = bf16[48,1024]{1,0:T(8,128)(2,1)S(1)} collective-permute-done((bf16[48,1024]{1,0:T(8,128)(2,1)S(1)}, bf16[48,1024]{1,0:T(8,128)(2,1)S(1)}, u32[]{:S(2)}, u32[]{:S(2)}) %collective-permute-start.5) | collective-permute-done | bytes 98336 | tf_op jit(solution)/shard_map/ppermute | solution.py:18
  19.0 2.7 %collective-permute-done.4 = bf16[48,1024]{1,0:T(8,128)(2,1)S(1)} collective-permute-done((bf16[48,1024]{1,0:T(8,128)(2,1)S(1)}, bf16[48,1024]{1,0:T(8,128)(2,1)S(1)}, u32[]{:S(2)}, u32[]{:S(2)}) %collective-permute-start.4) | collective-permute-done | bytes 98336 | tf_op jit(solution)/shard_map/ppermute | solution.py:18
  22.8 1.7 collective-permute-done.6.near
  24.5 1.6 collective-permute-start.10
  26.7 2.7 %collective-permute-start.8 = (bf16[160,1024]{1,0:T(8,128)(2,1)S(1)}, bf16[160,1024]{1,0:T(8,128)(2,1)}, u32[]{:S(2)}, u32[]{:S(2)}) collective-permute-start(bf16[160,1024]{1,0:T(8,128)(2,1)S(1)} %get-tuple-element.126), channel_id=1, source_target_pairs={{0,16},{8,24},{16,0},{24,8},{1,17},{9,25},{17,1},{25,9},{2,18},{10... | collective-permute-start | bytes 983048 | tf_op jit(solution)/shard_map/ppermute | solution.py:18
  29.4 1.4 collective-permute-start.9
  32.9 4.2 %collective-permute-done.7 = bf16[160,1024]{1,0:T(8,128)(2,1)} collective-permute-done((bf16[160,1024]{1,0:T(8,128)(2,1)S(1)}, bf16[160,1024]{1,0:T(8,128)(2,1)}, u32[]{:S(2)}, u32[]{:S(2)}) %collective-permute-start.7) | collective-permute-done | bytes 327712 | tf_op jit(solution)/shard_map/ppermute | solution.py:18
  37.1 7.9 %collective-permute-done.8 = bf16[160,1024]{1,0:T(8,128)(2,1)} collective-permute-done((bf16[160,1024]{1,0:T(8,128)(2,1)S(1)}, bf16[160,1024]{1,0:T(8,128)(2,1)}, u32[]{:S(2)}, u32[]{:S(2)}) %collective-permute-start.8) | collective-permute-done | bytes 327712 | tf_op jit(solution)/shard_map/ppermute | solution.py:18
  48.6 1.7 collective-permute-start.15
  53.6 12.5 %collective-permute-done.14.across0 = bf16[256,896]{1,0:T(8,128)(2,1)S(1)} collective-permute-done((bf16[256,896]{1,0:T(8,128)(2,1)S(1)}, bf16[256,896]{1,0:T(8,128)(2,1)S(1)}, u32[]{:S(2)}, u32[]{:S(2)}) %collective-permute-start.14) | collective-permute-done | bytes 458784 | tf_op jit(solution)/shard_map/ppermute | solution.py:24
  68.9 13.4 %collective-permute-done.19.across1 = bf16[256,896]{1,0:T(8,128)(2,1)S(1)} collective-permute-done((bf16[256,896]{1,0:T(8,128)(2,1)S(1)}, bf16[256,896]{1,0:T(8,128)(2,1)S(1)}, u32[]{:S(2)}, u32[]{:S(2)}) %collective-permute-start.19) | collective-permute-done | bytes 458784 | tf_op jit(solution)/shard_map/ppermute | solution.py:24
  84.4 1.5 collective-permute-done.21.other1
  86.8 9.7 %base.2 = (bf16[4,2,32,896]{3,2,1,0:T(8,128)(2,1)}, bf16[4,2,32,896]{3,2,1,0:T(8,128)(2,1)}, bf16[4,2,32,896]{3,2,1,0:T(8,128)(2,1)}, bf16[4,2,32,896]{3,2,1,0:T(8,128)(2,1)}) custom-call(s32[4]{0:T(128)} %pad_add_fusion.s_ref, bf16[512,1024]{1,0:T(8,128)(2,1)} %bitcast.69, bf16[512,1024]{1,0:T(8,128)(2,1)} %copy-done.20, ...), custom_call_target="tpu_custom_call" | custom-call | flops 3758096384 | bytes 9699328 | tf_op jit(solution)/shard_map/base/pallas_call | solution.py:71
  96.5 2.9 %collective-permute-done.20.own1 = bf16[512,1024]{1,0:T(8,128)(2,1)} collective-permute-done((bf16[512,1024]{1,0:T(8,128)(2,1)}, bf16[512,1024]{1,0:T(8,128)(2,1)}, u32[]{:S(2)}, u32[]{:S(2)}) %collective-permute-start.20) | collective-permute-done | bytes 1048608 | tf_op jit(solution)/shard_map/ppermute | solution.py:24
  99.4 9.3 %collective-permute-done.26.refs_1_.refs_5_ = bf16[256,3712]{1,0:T(8,128)(2,1)} collective-permute-done((bf16[256,3712]{1,0:T(8,128)(2,1)S(1)}, bf16[256,3712]{1,0:T(8,128)(2,1)}, u32[]{:S(2)}, u32[]{:S(2)}) %collective-permute-start.26) | collective-permute-done | bytes 1900576 | tf_op jit(solution)/shard_map/ppermute | solution.py:24
  109.8 3.0 %collective-permute-start.23 = (bf16[4,2,32,896]{3,2,1,0:T(8,128)(2,1)}, bf16[4,2,32,896]{3,2,1,0:T(8,128)(2,1)S(1)}, u32[]{:S(2)}, u32[]{:S(2)}) collective-permute-start(bf16[4,2,32,896]{3,2,1,0:T(8,128)(2,1)} %get-tuple-element.79), channel_id=1, source_target_pairs={{0,64},{32,96},{64,0},{96,32},{1,65},{33,97},{65,1},{97,33},{2,66}... | collective-permute-start | bytes 1376264 | tf_op jit(solution)/shard_map/ppermute | solution.py:18
  112.7 1.3 collective-permute-start.24
  114.1 9.7 %base.3 = (bf16[4,2,32,896]{3,2,1,0:T(8,128)(2,1)}, bf16[4,2,32,896]{3,2,1,0:T(8,128)(2,1)}, bf16[4,2,32,896]{3,2,1,0:T(8,128)(2,1)}, bf16[4,2,32,896]{3,2,1,0:T(8,128)(2,1)}) custom-call(s32[4]{0:T(128)} %pad_add_fusion.s_ref, bf16[512,1024]{1,0:T(8,128)(2,1)} %copy-done.19, bf16[512,1024]{1,0:T(8,128)(2,1)} %copy-done.22, ...), custom_call_target="tpu_custom_call" | custom-call | flops 3758096384 | bytes 9699328 | tf_op jit(solution)/shard_map/base/pallas_call | solution.py:71
  124.5 6.8 %collective-permute-start.32 = (bf16[4,2,32,896]{3,2,1,0:T(8,128)(2,1)}, bf16[4,2,32,896]{3,2,1,0:T(8,128)(2,1)S(1)}, u32[]{:S(2)}, u32[]{:S(2)}) collective-permute-start(bf16[4,2,32,896]{3,2,1,0:T(8,128)(2,1)} %get-tuple-element.93), channel_id=1, source_target_pairs={{0,64},{32,96},{64,0},{96,32},{1,65},{33,97},{65,1},{97,33},{2,66}... | collective-permute-start | bytes 1376264 | tf_op jit(solution)/shard_map/ppermute | solution.py:18
  131.2 3.0 %collective-permute-done.23 = bf16[4,2,32,896]{3,2,1,0:T(8,128)(2,1)S(1)} collective-permute-done((bf16[4,2,32,896]{3,2,1,0:T(8,128)(2,1)}, bf16[4,2,32,896]{3,2,1,0:T(8,128)(2,1)S(1)}, u32[]{:S(2)}, u32[]{:S(2)}) %collective-permute-start.23) | collective-permute-done | bytes 458784 | tf_op jit(solution)/shard_map/ppermute | solution.py:18
  137.3 6.0 %collective-permute-done.29.left1 = bf16[80,1024]{1,0:T(8,128)(2,1)S(1)} collective-permute-done((bf16[80,1024]{1,0:T(8,128)(2,1)S(1)}, bf16[80,1024]{1,0:T(8,128)(2,1)S(1)}, u32[]{:S(2)}, u32[]{:S(2)}) %collective-permute-start.29) | collective-permute-done | bytes 163872 | tf_op jit(solution)/shard_map/ppermute | solution.py:24
  143.3 6.5 %collective-permute-done.30.left2 = bf16[80,1024]{1,0:T(8,128)(2,1)S(1)} collective-permute-done((bf16[80,1024]{1,0:T(8,128)(2,1)S(1)}, bf16[80,1024]{1,0:T(8,128)(2,1)S(1)}, u32[]{:S(2)}, u32[]{:S(2)}) %collective-permute-start.30) | collective-permute-done | bytes 163872 | tf_op jit(solution)/shard_map/ppermute | solution.py:24
  149.9 2.2 %collective-permute-done.32 = bf16[4,2,32,896]{3,2,1,0:T(8,128)(2,1)S(1)} collective-permute-done((bf16[4,2,32,896]{3,2,1,0:T(8,128)(2,1)}, bf16[4,2,32,896]{3,2,1,0:T(8,128)(2,1)S(1)}, u32[]{:S(2)}, u32[]{:S(2)}) %collective-permute-start.32) | collective-permute-done | bytes 458784 | tf_op jit(solution)/shard_map/ppermute | solution.py:18
  153.0 3.4 %collective-permute-done.34.left3 = bf16[80,1024]{1,0:T(8,128)(2,1)S(1)} collective-permute-done((bf16[80,1024]{1,0:T(8,128)(2,1)S(1)}, bf16[80,1024]{1,0:T(8,128)(2,1)S(1)}, u32[]{:S(2)}, u32[]{:S(2)}) %collective-permute-start.34) | collective-permute-done | bytes 163872 | tf_op jit(solution)/shard_map/ppermute | solution.py:24
  157.8 4.6 %collective-permute-start.38 = (bf16[4,32,896]{2,1,0:T(8,128)(2,1)}, bf16[4,32,896]{2,1,0:T(8,128)(2,1)S(1)}, u32[]{:S(2)}, u32[]{:S(2)}) collective-permute-start(bf16[4,32,896]{2,1,0:T(8,128)(2,1)} %get-tuple-element.113), channel_id=1, source_target_pairs={{0,16},{8,24},{16,0},{24,8},{1,17},{9,25},{17,1},{25,9},{2,18},{10... | collective-permute-start | bytes 688136 | tf_op jit(solution)/shard_map/ppermute | solution.py:18
  162.4 1.6 collective-permute-start.37
  164.9 10.7 %update.1 = bf16[512,3584]{1,0:T(8,128)(2,1)} custom-call(s32[4]{0:T(128)} %pad_add_fusion.s_ref, bf16[80,1024]{1,0:T(8,128)(2,1)} %copy-done.3, bf16[80,1024]{1,0:T(8,128)(2,1)} %copy-done.7, bf16[80,1024]{1,0:T(8,128)(2,1)} %copy-done.8, bf16[80,1024]{1,0:T(8,128)(2,1)} %copy-done.9, bf16[4,80,1024]{2,1,0:T(8,128)(2,1)} %copy-done.6, ...), custom_call_target="tpu_custom_call" | custom-call | flops 3758096384 | bytes 12058624 | tf_op jit(solution)/shard_map/update/pallas_call | solution.py:170
  177.1 3.4 %outputs.1 = bf16[128,3584]{1,0:T(8,128)(2,1)} custom-call(s32[4]{0:T(128)} %pad_add_fusion.s_ref, bf16[4,32,896]{2,1,0:T(8,128)(2,1)} %get-tuple-element.102.refs_0_, bf16[4,32,896]{2,1,0:T(8,128)(2,1)} %copy-done.16, bf16[4,32,896]{2,1,0:T(8,128)(2,1)} %copy-done.15, bf16[4,32,896]{2,1,0:T(8,128)(2,1)} %copy-done.14, f32[128,128]{1,0:T(8,128)} %broadcast_in_dim.2.refs_4_, ...), custom_call_target="tpu_custom_call" | custom-call | flops 29360128 | bytes 3670016 | tf_op jit(solution)/shard_map/outputs/pallas_call | solution.py:113
  (155 shorter events, 31.2 us)
Async XLA Ops:
  1.7 9.8 %collective-permute-start = (bf16[48,1024]{1,0:T(8,128)(2,1)S(1)}, bf16[48,1024]{1,0:T(8,128)(2,1)S(1)}, u32[]{:S(2)}, u32[]{:S(2)}) collective-permute-start(bf16[48,1024]{1,0:T(8,128)(2,1)S(1)} %get-tuple-element.121), channel_id=1, source_target_pairs={{0,2},{2,4},{4,6},{6,0},{1,3},{3,5},{5,7},{7,1},{8,10},{10,12},{12... | collective-permute-start | bytes 294920 | tf_op jit(solution)/shard_map/ppermute | solution.py:18
  3.8 8.2 %collective-permute-start.1 = (bf16[48,1024]{1,0:T(8,128)(2,1)S(1)}, bf16[48,1024]{1,0:T(8,128)(2,1)S(1)}, u32[]{:S(2)}, u32[]{:S(2)}) collective-permute-start(bf16[48,1024]{1,0:T(8,128)(2,1)S(1)} %get-tuple-element.122), channel_id=1, source_target_pairs={{0,4},{2,6},{4,0},{6,2},{1,5},{3,7},{5,1},{7,3},{8,12},{10,14},{12... | collective-permute-start | bytes 294920 | tf_op jit(solution)/shard_map/ppermute | solution.py:18
  9.6 14.8 %collective-permute-start.6 = (bf16[512,896]{1,0:T(8,128)(2,1)S(1)}, bf16[512,896]{1,0:T(8,128)(2,1)}, u32[]{:S(2)}, u32[]{:S(2)}) collective-permute-start(bf16[512,896]{1,0:T(8,128)(2,1)S(1)} %constant_dynamic-slice_fusion.4), channel_id=1, source_target_pairs={{0,8},{8,16},{16,24},{24,0},{1,25},{9,1},{17,9},{25,17},{2,10},{10... | collective-permute-start | bytes 2752520 | tf_op jit(solution)/shard_map/ppermute | solution.py:24
  12.1 7.0 %collective-permute-start.5 = (bf16[48,1024]{1,0:T(8,128)(2,1)S(1)}, bf16[48,1024]{1,0:T(8,128)(2,1)S(1)}, u32[]{:S(2)}, u32[]{:S(2)}) collective-permute-start(bf16[48,1024]{1,0:T(8,128)(2,1)S(1)} %get-tuple-element.117), channel_id=1, source_target_pairs={{0,96},{32,0},{64,32},{96,64},{1,97},{33,1},{65,33},{97,65},{2,98}... | collective-permute-start | bytes 294920 | tf_op jit(solution)/shard_map/ppermute | solution.py:18
  24.5 22.0 %collective-permute-start.10 = (bf16[64,3712]{1,0:T(8,128)(2,1)S(1)}, bf16[64,3712]{1,0:T(8,128)(2,1)S(1)}, u32[]{:S(2)}, u32[]{:S(2)}) collective-permute-start(bf16[64,3712]{1,0:T(8,128)(2,1)S(1)} %fusion.1), channel_id=1, source_target_pairs={{0,32},{32,64},{64,96},{96,0},{1,97},{33,1},{65,33},{97,65},{2,34}... | collective-permute-start | bytes 1425416 | tf_op jit(solution)/shard_map/ppermute | solution.py:24
  26.3 10.8 %collective-permute-start.7 = (bf16[160,1024]{1,0:T(8,128)(2,1)S(1)}, bf16[160,1024]{1,0:T(8,128)(2,1)}, u32[]{:S(2)}, u32[]{:S(2)}) collective-permute-start(bf16[160,1024]{1,0:T(8,128)(2,1)S(1)} %get-tuple-element.125), channel_id=1, source_target_pairs={{0,8},{8,16},{16,24},{24,0},{1,9},{9,17},{17,25},{25,1},{2,10},{10... | collective-permute-start | bytes 983048 | tf_op jit(solution)/shard_map/ppermute | solution.py:18
  26.7 18.4 %collective-permute-start.8 = (bf16[160,1024]{1,0:T(8,128)(2,1)S(1)}, bf16[160,1024]{1,0:T(8,128)(2,1)}, u32[]{:S(2)}, u32[]{:S(2)}) collective-permute-start(bf16[160,1024]{1,0:T(8,128)(2,1)S(1)} %get-tuple-element.126), channel_id=1, source_target_pairs={{0,16},{8,24},{16,0},{24,8},{1,17},{9,25},{17,1},{25,9},{2,18},{10... | collective-permute-start | bytes 983048 | tf_op jit(solution)/shard_map/ppermute | solution.py:18
  29.4 15.7 %collective-permute-start.9 = (bf16[160,1024]{1,0:T(8,128)(2,1)S(1)}, bf16[160,1024]{1,0:T(8,128)(2,1)}, u32[]{:S(2)}, u32[]{:S(2)}) collective-permute-start(bf16[160,1024]{1,0:T(8,128)(2,1)S(1)} %get-tuple-element.127), channel_id=1, source_target_pairs={{0,24},{8,0},{16,8},{24,16},{1,25},{9,1},{17,9},{25,17},{2,26},{10... | collective-permute-start | bytes 983048 | tf_op jit(solution)/shard_map/ppermute | solution.py:18
  32.9 20.7 %collective-permute-start.13 = (bf16[512,896]{1,0:T(8,128)(2,1)S(1)}, bf16[512,896]{1,0:T(8,128)(2,1)S(1)}, u32[]{:S(2)}, u32[]{:S(2)}) collective-permute-start(bf16[512,896]{1,0:T(8,128)(2,1)S(1)} %constant_dynamic-slice_fusion.1), channel_id=1, source_target_pairs={{0,24},{8,0},{16,8},{24,16},{1,9},{9,17},{17,25},{25,1},{2,26},{10... | collective-permute-start | bytes 2752520 | tf_op jit(solution)/shard_map/ppermute | solution.py:24
  47.3 18.7 %collective-permute-start.12 = (bf16[512,1024]{1,0:T(8,128)(2,1)S(1)}, bf16[512,1024]{1,0:T(8,128)(2,1)S(1)}, u32[]{:S(2)}, u32[]{:S(2)}) collective-permute-start(bf16[512,1024]{1,0:T(8,128)(2,1)S(1)} %bitcast.67), channel_id=1, source_target_pairs={{0,1},{1,0},{2,3},{3,2},{4,5},{5,4},{6,7},{7,6},{8,9},{9,8},{10,11... | collective-permute-start | bytes 3145736 | tf_op jit(solution)/shard_map/ppermute | solution.py:262
  47.4 18.7 %collective-permute-start.11 = (bf16[512,1024]{1,0:T(8,128)(2,1)S(1)}, bf16[512,1024]{1,0:T(8,128)(2,1)S(1)}, u32[]{:S(2)}, u32[]{:S(2)}) collective-permute-start(bf16[512,1024]{1,0:T(8,128)(2,1)S(1)} %bitcast.68), channel_id=1, source_target_pairs={{0,2},{2,4},{4,6},{6,0},{1,7},{3,1},{5,3},{7,5},{8,10},{10,12},{12... | collective-permute-start | bytes 3145736 | tf_op jit(solution)/shard_map/ppermute | solution.py:24
  48.6 17.4 %collective-permute-start.15 = (bf16[64,3712]{1,0:T(8,128)(2,1)S(1)}, bf16[64,3712]{1,0:T(8,128)(2,1)S(1)}, u32[]{:S(2)}, u32[]{:S(2)}) collective-permute-start(bf16[64,3712]{1,0:T(8,128)(2,1)S(1)} %copy-done.11), channel_id=1, source_target_pairs={{0,32},{32,64},{64,96},{96,0},{1,97},{33,1},{65,33},{97,65},{2,34}... | collective-permute-start | bytes 1425416 | tf_op jit(solution)/shard_map/ppermute | solution.py:24
  51.6 14.4 %collective-permute-start.14 = (bf16[256,896]{1,0:T(8,128)(2,1)S(1)}, bf16[256,896]{1,0:T(8,128)(2,1)S(1)}, u32[]{:S(2)}, u32[]{:S(2)}) collective-permute-start(bf16[256,896]{1,0:T(8,128)(2,1)S(1)} %get-tuple-element.109), channel_id=1, source_target_pairs={{0,16},{8,24},{16,0},{24,8},{1,17},{9,25},{17,1},{25,9},{2,18},{10... | collective-permute-start | bytes 1376264 | tf_op jit(solution)/shard_map/ppermute | solution.py:24
  66.1 16.2 %collective-permute-start.18 = (bf16[512,1024]{1,0:T(8,128)(2,1)S(1)}, bf16[512,1024]{1,0:T(8,128)(2,1)S(1)}, u32[]{:S(2)}, u32[]{:S(2)}) collective-permute-start(bf16[512,1024]{1,0:T(8,128)(2,1)S(1)} %collective-permute-done.11.own0), channel_id=1, source_target_pairs={{0,1},{1,0},{2,3},{3,2},{4,5},{5,4},{6,7},{7,6},{8,9},{9,8},{10,11... | collective-permute-start | bytes 3145736 | tf_op jit(solution)/shard_map/ppermute | solution.py:278
  66.8 16.1 %collective-permute-start.17 = (bf16[512,1024]{1,0:T(8,128)(2,1)S(1)}, bf16[512,1024]{1,0:T(8,128)(2,1)}, u32[]{:S(2)}, u32[]{:S(2)}) collective-permute-start(bf16[512,1024]{1,0:T(8,128)(2,1)S(1)} %collective-permute-done.11.own0), channel_id=1, source_target_pairs={{0,2},{2,4},{4,6},{6,0},{1,7},{3,1},{5,3},{7,5},{8,10},{10,12},{12... | collective-permute-start | bytes 3145736 | tf_op jit(solution)/shard_map/ppermute | solution.py:24
  67.5 14.8 %collective-permute-start.19 = (bf16[256,896]{1,0:T(8,128)(2,1)S(1)}, bf16[256,896]{1,0:T(8,128)(2,1)S(1)}, u32[]{:S(2)}, u32[]{:S(2)}) collective-permute-start(bf16[256,896]{1,0:T(8,128)(2,1)S(1)} %get-tuple-element.66), channel_id=1, source_target_pairs={{0,16},{8,24},{16,0},{24,8},{1,17},{9,25},{17,1},{25,9},{2,18},{10... | collective-permute-start | bytes 1376264 | tf_op jit(solution)/shard_map/ppermute | solution.py:24
  68.3 14.8 %collective-permute-start.25 = (bf16[64,3712]{1,0:T(8,128)(2,1)S(1)}, bf16[64,3712]{1,0:T(8,128)(2,1)S(1)}, u32[]{:S(2)}, u32[]{:S(2)}) collective-permute-start(bf16[64,3712]{1,0:T(8,128)(2,1)S(1)} %collective-permute-done.15), channel_id=1, source_target_pairs={{0,32},{32,64},{64,96},{96,0},{1,97},{33,1},{65,33},{97,65},{2,34}... | collective-permute-start | bytes 1425416 | tf_op jit(solution)/shard_map/ppermute | solution.py:24
  83.0 16.4 %collective-permute-start.20 = (bf16[512,1024]{1,0:T(8,128)(2,1)}, bf16[512,1024]{1,0:T(8,128)(2,1)}, u32[]{:S(2)}, u32[]{:S(2)}) collective-permute-start(bf16[512,1024]{1,0:T(8,128)(2,1)} %collective-permute-done.17.own1), channel_id=1, source_target_pairs={{0,2},{2,4},{4,6},{6,0},{1,7},{3,1},{5,3},{7,5},{8,10},{10,12},{12... | collective-permute-start | bytes 3145736 | tf_op jit(solution)/shard_map/ppermute | solution.py:24
  83.2 25.5 %collective-permute-start.26 = (bf16[256,3712]{1,0:T(8,128)(2,1)S(1)}, bf16[256,3712]{1,0:T(8,128)(2,1)}, u32[]{:S(2)}, u32[]{:S(2)}) collective-permute-start(bf16[256,3712]{1,0:T(8,128)(2,1)S(1)} %constant_dynamic-update-slice_fusion.refs_0_.refs_4_), channel_id=1, source_target_pairs={{0,8},{8,16},{16,24},{24,0},{1,25},{9,1},{17,9},{25,17},{2,10},{10... | collective-permute-start | bytes 5701640 | tf_op jit(solution)/shard_map/ppermute | solution.py:24
  99.4 9.3 %collective-permute-start.27 = (bf16[512,1024]{1,0:T(8,128)(2,1)}, bf16[512,1024]{1,0:T(8,128)(2,1)S(1)}, u32[]{:S(2)}, u32[]{:S(2)}) collective-permute-start(bf16[512,1024]{1,0:T(8,128)(2,1)} %collective-permute-done.20.own1), channel_id=1, source_target_pairs={{0,1},{1,0},{2,3},{3,2},{4,5},{5,4},{6,7},{7,6},{8,9},{9,8},{10,11... | collective-permute-start | bytes 3145736 | tf_op jit(solution)/shard_map/ppermute | solution.py:290
  108.7 27.9 %collective-permute-start.28 = (bf16[256,3712]{1,0:T(8,128)(2,1)}, bf16[256,3712]{1,0:T(8,128)(2,1)S(1)}, u32[]{:S(2)}, u32[]{:S(2)}) collective-permute-start(bf16[256,3712]{1,0:T(8,128)(2,1)} %collective-permute-done.26.refs_1_.refs_5_), channel_id=1, source_target_pairs={{0,8},{8,16},{16,24},{24,0},{1,25},{9,1},{17,9},{25,17},{2,10},{10... | collective-permute-start | bytes 5701640 | tf_op jit(solution)/shard_map/ppermute | solution.py:24
  109.6 14.8 %collective-permute-start.22 = (bf16[4,2,32,896]{3,2,1,0:T(8,128)(2,1)}, bf16[4,2,32,896]{3,2,1,0:T(8,128)(2,1)S(1)}, u32[]{:S(2)}, u32[]{:S(2)}) collective-permute-start(bf16[4,2,32,896]{3,2,1,0:T(8,128)(2,1)} %get-tuple-element.78), channel_id=1, source_target_pairs={{0,32},{32,64},{64,96},{96,0},{1,33},{33,65},{65,97},{97,1},{2,34}... | collective-permute-start | bytes 1376264 | tf_op jit(solution)/shard_map/ppermute | solution.py:18
  109.8 24.5 %collective-permute-start.23 = (bf16[4,2,32,896]{3,2,1,0:T(8,128)(2,1)}, bf16[4,2,32,896]{3,2,1,0:T(8,128)(2,1)S(1)}, u32[]{:S(2)}, u32[]{:S(2)}) collective-permute-start(bf16[4,2,32,896]{3,2,1,0:T(8,128)(2,1)} %get-tuple-element.79), channel_id=1, source_target_pairs={{0,64},{32,96},{64,0},{96,32},{1,65},{33,97},{65,1},{97,33},{2,66}... | collective-permute-start | bytes 1376264 | tf_op jit(solution)/shard_map/ppermute | solution.py:18
  112.7 22.6 %collective-permute-start.24 = (bf16[4,2,32,896]{3,2,1,0:T(8,128)(2,1)}, bf16[4,2,32,896]{3,2,1,0:T(8,128)(2,1)}, u32[]{:S(2)}, u32[]{:S(2)}) collective-permute-start(bf16[4,2,32,896]{3,2,1,0:T(8,128)(2,1)} %get-tuple-element.80), channel_id=1, source_target_pairs={{0,96},{32,0},{64,32},{96,64},{1,97},{33,1},{65,33},{97,65},{2,98}... | collective-permute-start | bytes 1376264 | tf_op jit(solution)/shard_map/ppermute | solution.py:18
  123.8 26.1 %collective-permute-start.31 = (bf16[4,2,32,896]{3,2,1,0:T(8,128)(2,1)}, bf16[4,2,32,896]{3,2,1,0:T(8,128)(2,1)S(1)}, u32[]{:S(2)}, u32[]{:S(2)}) collective-permute-start(bf16[4,2,32,896]{3,2,1,0:T(8,128)(2,1)} %get-tuple-element.92), channel_id=1, source_target_pairs={{0,32},{32,64},{64,96},{96,0},{1,33},{33,65},{65,97},{97,1},{2,34}... | collective-permute-start | bytes 1376264 | tf_op jit(solution)/shard_map/ppermute | solution.py:18
  124.5 27.6 %collective-permute-start.32 = (bf16[4,2,32,896]{3,2,1,0:T(8,128)(2,1)}, bf16[4,2,32,896]{3,2,1,0:T(8,128)(2,1)S(1)}, u32[]{:S(2)}, u32[]{:S(2)}) collective-permute-start(bf16[4,2,32,896]{3,2,1,0:T(8,128)(2,1)} %get-tuple-element.93), channel_id=1, source_target_pairs={{0,64},{32,96},{64,0},{96,32},{1,65},{33,97},{65,1},{97,33},{2,66}... | collective-permute-start | bytes 1376264 | tf_op jit(solution)/shard_map/ppermute | solution.py:18
  134.3 18.4 %collective-permute-start.33 = (bf16[4,2,32,896]{3,2,1,0:T(8,128)(2,1)}, bf16[4,2,32,896]{3,2,1,0:T(8,128)(2,1)S(1)}, u32[]{:S(2)}, u32[]{:S(2)}) collective-permute-start(bf16[4,2,32,896]{3,2,1,0:T(8,128)(2,1)} %get-tuple-element.94), channel_id=1, source_target_pairs={{0,96},{32,0},{64,32},{96,64},{1,97},{33,1},{65,33},{97,65},{2,98}... | collective-permute-start | bytes 1376264 | tf_op jit(solution)/shard_map/ppermute | solution.py:18
  136.6 27.5 %collective-permute-start.35 = (bf16[256,3712]{1,0:T(8,128)(2,1)S(1)}, bf16[256,3712]{1,0:T(8,128)(2,1)}, u32[]{:S(2)}, u32[]{:S(2)}) collective-permute-start(bf16[256,3712]{1,0:T(8,128)(2,1)S(1)} %collective-permute-done.28.refs_2_.refs_6_), channel_id=1, source_target_pairs={{0,8},{8,16},{16,24},{24,0},{1,25},{9,1},{17,9},{25,17},{2,10},{10... | collective-permute-start | bytes 5701640 | tf_op jit(solution)/shard_map/ppermute | solution.py:24
  156.5 7.6 %collective-permute-start.36 = (bf16[4,80,1024]{2,1,0:T(8,128)(2,1)S(1)}, bf16[4,80,1024]{2,1,0:T(8,128)(2,1)S(1)}, u32[]{:S(2)}, u32[]{:S(2)}) collective-permute-start(bf16[4,80,1024]{2,1,0:T(8,128)(2,1)S(1)} %pad_maximum_fusion.1), channel_id=1, source_target_pairs={{0,1},{1,0},{2,3},{3,2},{4,5},{5,4},{6,7},{7,6},{8,9},{9,8},{10,11... | collective-permute-start | bytes 1966088 | tf_op jit(solution)/shard_map/ppermute | solution.py:311
  157.8 17.8 %collective-permute-start.39 = (bf16[4,32,896]{2,1,0:T(8,128)(2,1)}, bf16[4,32,896]{2,1,0:T(8,128)(2,1)S(1)}, u32[]{:S(2)}, u32[]{:S(2)}) collective-permute-start(bf16[4,32,896]{2,1,0:T(8,128)(2,1)} %get-tuple-element.112), channel_id=1, source_target_pairs={{0,8},{8,16},{16,24},{24,0},{1,9},{9,17},{17,25},{25,1},{2,10},{10... | collective-permute-start | bytes 688136 | tf_op jit(solution)/shard_map/ppermute | solution.py:18
  157.8 17.8 %collective-permute-start.38 = (bf16[4,32,896]{2,1,0:T(8,128)(2,1)}, bf16[4,32,896]{2,1,0:T(8,128)(2,1)S(1)}, u32[]{:S(2)}, u32[]{:S(2)}) collective-permute-start(bf16[4,32,896]{2,1,0:T(8,128)(2,1)} %get-tuple-element.113), channel_id=1, source_target_pairs={{0,16},{8,24},{16,0},{24,8},{1,17},{9,25},{17,1},{25,9},{2,18},{10... | collective-permute-start | bytes 688136 | tf_op jit(solution)/shard_map/ppermute | solution.py:18
  162.4 13.2 %collective-permute-start.37 = (bf16[4,32,896]{2,1,0:T(8,128)(2,1)}, bf16[4,32,896]{2,1,0:T(8,128)(2,1)S(1)}, u32[]{:S(2)}, u32[]{:S(2)}) collective-permute-start(bf16[4,32,896]{2,1,0:T(8,128)(2,1)} %get-tuple-element.114), channel_id=1, source_target_pairs={{0,24},{8,0},{16,8},{24,16},{1,25},{9,1},{17,9},{25,17},{2,26},{10... | collective-permute-start | bytes 688136 | tf_op jit(solution)/shard_map/ppermute | solution.py:18
  (35 other events, 399.2 us)

commit v5 on v4

--- a/solution.py
+++ b/solution.py
@@ -307,7 +307,7 @@
     for _ in range(3):
         left.append(apart(left[-1], "z", 1, -1))
     sum_b = total_of(terms_b).astype(BF16)
-    sum_b, left[3] = together(sum_b, left[3])
+    sum_b, left[2] = together(sum_b, left[2])
     left_other = lax.ppermute(jnp.stack(left), "c", SWAP)
 
     total = jnp.concatenate([sum_a, sum_b], axis=1)

time: 182 us -> 181 us (level)
    unnamed x59 -> x57, local copies, waits for them, and re-layouts: 5.03 us -> 4.33 us
where the time goes in v5:
time: 181 us; the launch traced here: 180 us
  waiting for transfers between devices  84.3 us (47%)
  starting transfers between devices  44.3 us (24%)
  Pallas kernels  33.5 us (19%)
  local copies, waits for them, and re-layouts  10.5 us (6%)
  other arithmetic  5.2 us (3%)
    ppermute x16, waiting for transfers between devices, apart(): return lax.ppermute(value, (axis, 'c'), perm)  57.4 us
    ppermute x18, starting transfers between devices, shift(): return lax.ppermute(value, axis, [(i, (i + by) % 4) for i in range(4)])  34 us
    ppermute x18, waiting for transfers between devices, shift(): return lax.ppermute(value, axis, [(i, (i + by) % 4) for i in range(4)])  25.4 us
    pallas_call x2, Pallas kernels, base_part(): pl.pallas_call(base_kernel, grid_spec=pltpu.PrefetchScalarGridSpec(num_sc...  19.4 us
    pallas_call x1, Pallas kernels, update_part(): pl.pallas_call(update_kernel, grid_spec=pltpu.PrefetchScalarGridSpec(num_...  10.7 us
    ppermute x16, starting transfers between devices, apart(): return lax.ppermute(value, (axis, 'c'), perm)  9.92 us
    unnamed x57, local copies, waits for them, and re-layouts  4.33 us
  transfers between devices with their start and end apart: 40, of which 21 were waited for; matrix products, arithmetic and copies ran while one was open for 6% of the time, Pallas kernels for 17%

profile of v5, /device:TPU:0, one launch (start us, length us, event | category | flops | bytes accessed | tf_op | source)
XLA Modules:
  0.0 179.8 jit_solution(13030872237906126478)
XLA Ops:
  1.7 2.1 %collective-permute-start = (bf16[48,1024]{1,0:T(8,128)(2,1)S(1)}, bf16[48,1024]{1,0:T(8,128)(2,1)S(1)}, u32[]{:S(2)}, u32[]{:S(2)}) collective-permute-start(bf16[48,1024]{1,0:T(8,128)(2,1)S(1)} %get-tuple-element.121), channel_id=1, source_target_pairs={{0,2},{2,4},{4,6},{6,0},{1,3},{3,5},{5,7},{7,1},{8,10},{10,12},{12... | collective-permute-start | bytes 294920 | tf_op jit(solution)/shard_map/ppermute | solution.py:18
  3.8 3.6 %collective-permute-start.1 = (bf16[48,1024]{1,0:T(8,128)(2,1)S(1)}, bf16[48,1024]{1,0:T(8,128)(2,1)S(1)}, u32[]{:S(2)}, u32[]{:S(2)}) collective-permute-start(bf16[48,1024]{1,0:T(8,128)(2,1)S(1)} %get-tuple-element.122), channel_id=1, source_target_pairs={{0,4},{2,6},{4,0},{6,2},{1,5},{3,7},{5,1},{7,3},{8,12},{10,14},{12... | collective-permute-start | bytes 294920 | tf_op jit(solution)/shard_map/ppermute | solution.py:18
  9.6 1.6 collective-permute-start.6
  12.1 3.1 %collective-permute-start.5 = (bf16[48,1024]{1,0:T(8,128)(2,1)S(1)}, bf16[48,1024]{1,0:T(8,128)(2,1)S(1)}, u32[]{:S(2)}, u32[]{:S(2)}) collective-permute-start(bf16[48,1024]{1,0:T(8,128)(2,1)S(1)} %get-tuple-element.117), channel_id=1, source_target_pairs={{0,96},{32,0},{64,32},{96,64},{1,97},{33,1},{65,33},{97,65},{2,98}... | collective-permute-start | bytes 294920 | tf_op jit(solution)/shard_map/ppermute | solution.py:18
  16.9 2.1 %collective-permute-done.5 = bf16[48,1024]{1,0:T(8,128)(2,1)S(1)} collective-permute-done((bf16[48,1024]{1,0:T(8,128)(2,1)S(1)}, bf16[48,1024]{1,0:T(8,128)(2,1)S(1)}, u32[]{:S(2)}, u32[]{:S(2)}) %collective-permute-start.5) | collective-permute-done | bytes 98336 | tf_op jit(solution)/shard_map/ppermute | solution.py:18
  19.0 2.7 %collective-permute-done.4 = bf16[48,1024]{1,0:T(8,128)(2,1)S(1)} collective-permute-done((bf16[48,1024]{1,0:T(8,128)(2,1)S(1)}, bf16[48,1024]{1,0:T(8,128)(2,1)S(1)}, u32[]{:S(2)}, u32[]{:S(2)}) %collective-permute-start.4) | collective-permute-done | bytes 98336 | tf_op jit(solution)/shard_map/ppermute | solution.py:18
  22.8 1.7 collective-permute-done.6.near
  24.5 1.6 collective-permute-start.10
  26.7 2.7 %collective-permute-start.8 = (bf16[160,1024]{1,0:T(8,128)(2,1)S(1)}, bf16[160,1024]{1,0:T(8,128)(2,1)}, u32[]{:S(2)}, u32[]{:S(2)}) collective-permute-start(bf16[160,1024]{1,0:T(8,128)(2,1)S(1)} %get-tuple-element.126), channel_id=1, source_target_pairs={{0,16},{8,24},{16,0},{24,8},{1,17},{9,25},{17,1},{25,9},{2,18},{10... | collective-permute-start | bytes 983048 | tf_op jit(solution)/shard_map/ppermute | solution.py:18
  29.4 1.4 collective-permute-start.9
  32.9 4.2 %collective-permute-done.7 = bf16[160,1024]{1,0:T(8,128)(2,1)} collective-permute-done((bf16[160,1024]{1,0:T(8,128)(2,1)S(1)}, bf16[160,1024]{1,0:T(8,128)(2,1)}, u32[]{:S(2)}, u32[]{:S(2)}) %collective-permute-start.7) | collective-permute-done | bytes 327712 | tf_op jit(solution)/shard_map/ppermute | solution.py:18
  37.1 7.9 %collective-permute-done.8 = bf16[160,1024]{1,0:T(8,128)(2,1)} collective-permute-done((bf16[160,1024]{1,0:T(8,128)(2,1)S(1)}, bf16[160,1024]{1,0:T(8,128)(2,1)}, u32[]{:S(2)}, u32[]{:S(2)}) %collective-permute-start.8) | collective-permute-done | bytes 327712 | tf_op jit(solution)/shard_map/ppermute | solution.py:18
  48.6 1.7 collective-permute-start.15
  53.6 12.5 %collective-permute-done.14.across0 = bf16[256,896]{1,0:T(8,128)(2,1)S(1)} collective-permute-done((bf16[256,896]{1,0:T(8,128)(2,1)S(1)}, bf16[256,896]{1,0:T(8,128)(2,1)S(1)}, u32[]{:S(2)}, u32[]{:S(2)}) %collective-permute-start.14) | collective-permute-done | bytes 458784 | tf_op jit(solution)/shard_map/ppermute | solution.py:24
  68.9 13.4 %collective-permute-done.19.across1 = bf16[256,896]{1,0:T(8,128)(2,1)S(1)} collective-permute-done((bf16[256,896]{1,0:T(8,128)(2,1)S(1)}, bf16[256,896]{1,0:T(8,128)(2,1)S(1)}, u32[]{:S(2)}, u32[]{:S(2)}) %collective-permute-start.19) | collective-permute-done | bytes 458784 | tf_op jit(solution)/shard_map/ppermute | solution.py:24
  84.3 1.5 collective-permute-done.21.other1
  86.8 9.7 %base.2 = (bf16[4,2,32,896]{3,2,1,0:T(8,128)(2,1)}, bf16[4,2,32,896]{3,2,1,0:T(8,128)(2,1)}, bf16[4,2,32,896]{3,2,1,0:T(8,128)(2,1)}, bf16[4,2,32,896]{3,2,1,0:T(8,128)(2,1)}) custom-call(s32[4]{0:T(128)} %pad_add_fusion.s_ref, bf16[512,1024]{1,0:T(8,128)(2,1)} %bitcast.69, bf16[512,1024]{1,0:T(8,128)(2,1)} %copy-done.19, ...), custom_call_target="tpu_custom_call" | custom-call | flops 3758096384 | bytes 9699328 | tf_op jit(solution)/shard_map/base/pallas_call | solution.py:71
  96.4 2.9 %collective-permute-done.20.own1 = bf16[512,1024]{1,0:T(8,128)(2,1)} collective-permute-done((bf16[512,1024]{1,0:T(8,128)(2,1)}, bf16[512,1024]{1,0:T(8,128)(2,1)}, u32[]{:S(2)}, u32[]{:S(2)}) %collective-permute-start.20) | collective-permute-done | bytes 1048608 | tf_op jit(solution)/shard_map/ppermute | solution.py:24
  99.4 9.3 %collective-permute-done.26.refs_1_.refs_5_ = bf16[256,3712]{1,0:T(8,128)(2,1)} collective-permute-done((bf16[256,3712]{1,0:T(8,128)(2,1)S(1)}, bf16[256,3712]{1,0:T(8,128)(2,1)}, u32[]{:S(2)}, u32[]{:S(2)}) %collective-permute-start.26) | collective-permute-done | bytes 1900576 | tf_op jit(solution)/shard_map/ppermute | solution.py:24
  109.8 3.0 %collective-permute-start.23 = (bf16[4,2,32,896]{3,2,1,0:T(8,128)(2,1)}, bf16[4,2,32,896]{3,2,1,0:T(8,128)(2,1)S(1)}, u32[]{:S(2)}, u32[]{:S(2)}) collective-permute-start(bf16[4,2,32,896]{3,2,1,0:T(8,128)(2,1)} %get-tuple-element.79), channel_id=1, source_target_pairs={{0,64},{32,96},{64,0},{96,32},{1,65},{33,97},{65,1},{97,33},{2,66}... | collective-permute-start | bytes 1376264 | tf_op jit(solution)/shard_map/ppermute | solution.py:18
  112.7 1.3 collective-permute-start.24
  114.1 9.7 %base.3 = (bf16[4,2,32,896]{3,2,1,0:T(8,128)(2,1)}, bf16[4,2,32,896]{3,2,1,0:T(8,128)(2,1)}, bf16[4,2,32,896]{3,2,1,0:T(8,128)(2,1)}, bf16[4,2,32,896]{3,2,1,0:T(8,128)(2,1)}) custom-call(s32[4]{0:T(128)} %pad_add_fusion.s_ref, bf16[512,1024]{1,0:T(8,128)(2,1)} %copy-done.18, bf16[512,1024]{1,0:T(8,128)(2,1)} %copy-done.21, ...), custom_call_target="tpu_custom_call" | custom-call | flops 3758096384 | bytes 9699328 | tf_op jit(solution)/shard_map/base/pallas_call | solution.py:71
  124.5 6.8 %collective-permute-start.31 = (bf16[4,2,32,896]{3,2,1,0:T(8,128)(2,1)}, bf16[4,2,32,896]{3,2,1,0:T(8,128)(2,1)S(1)}, u32[]{:S(2)}, u32[]{:S(2)}) collective-permute-start(bf16[4,2,32,896]{3,2,1,0:T(8,128)(2,1)} %get-tuple-element.93), channel_id=1, source_target_pairs={{0,64},{32,96},{64,0},{96,32},{1,65},{33,97},{65,1},{97,33},{2,66}... | collective-permute-start | bytes 1376264 | tf_op jit(solution)/shard_map/ppermute | solution.py:18
  131.2 3.0 %collective-permute-done.23 = bf16[4,2,32,896]{3,2,1,0:T(8,128)(2,1)S(1)} collective-permute-done((bf16[4,2,32,896]{3,2,1,0:T(8,128)(2,1)}, bf16[4,2,32,896]{3,2,1,0:T(8,128)(2,1)S(1)}, u32[]{:S(2)}, u32[]{:S(2)}) %collective-permute-start.23) | collective-permute-done | bytes 458784 | tf_op jit(solution)/shard_map/ppermute | solution.py:18
  137.3 6.0 %collective-permute-done.29.left1 = bf16[80,1024]{1,0:T(8,128)(2,1)S(1)} collective-permute-done((bf16[80,1024]{1,0:T(8,128)(2,1)S(1)}, bf16[80,1024]{1,0:T(8,128)(2,1)S(1)}, u32[]{:S(2)}, u32[]{:S(2)}) %collective-permute-start.29) | collective-permute-done | bytes 163872 | tf_op jit(solution)/shard_map/ppermute | solution.py:24
  143.3 6.5 %collective-permute-done.33.left2 = bf16[80,1024]{1,0:T(8,128)(2,1)S(1)} collective-permute-done((bf16[80,1024]{1,0:T(8,128)(2,1)S(1)}, bf16[80,1024]{1,0:T(8,128)(2,1)S(1)}, u32[]{:S(2)}, u32[]{:S(2)}) %collective-permute-start.33) | collective-permute-done | bytes 163872 | tf_op jit(solution)/shard_map/ppermute | solution.py:24
  149.8 2.2 %collective-permute-done.31 = bf16[4,2,32,896]{3,2,1,0:T(8,128)(2,1)S(1)} collective-permute-done((bf16[4,2,32,896]{3,2,1,0:T(8,128)(2,1)}, bf16[4,2,32,896]{3,2,1,0:T(8,128)(2,1)S(1)}, u32[]{:S(2)}, u32[]{:S(2)}) %collective-permute-start.31) | collective-permute-done | bytes 458784 | tf_op jit(solution)/shard_map/ppermute | solution.py:18
  152.9 3.4 %collective-permute-done.34.left3 = bf16[80,1024]{1,0:T(8,128)(2,1)S(1)} collective-permute-done((bf16[80,1024]{1,0:T(8,128)(2,1)S(1)}, bf16[80,1024]{1,0:T(8,128)(2,1)S(1)}, u32[]{:S(2)}, u32[]{:S(2)}) %collective-permute-start.34) | collective-permute-done | bytes 163872 | tf_op jit(solution)/shard_map/ppermute | solution.py:24
  157.7 4.6 %collective-permute-start.38 = (bf16[4,32,896]{2,1,0:T(8,128)(2,1)}, bf16[4,32,896]{2,1,0:T(8,128)(2,1)S(1)}, u32[]{:S(2)}, u32[]{:S(2)}) collective-permute-start(bf16[4,32,896]{2,1,0:T(8,128)(2,1)} %get-tuple-element.113), channel_id=1, source_target_pairs={{0,16},{8,24},{16,0},{24,8},{1,17},{9,25},{17,1},{25,9},{2,18},{10... | collective-permute-start | bytes 688136 | tf_op jit(solution)/shard_map/ppermute | solution.py:18
  162.3 1.6 collective-permute-start.37
  164.8 10.7 %update.1 = bf16[512,3584]{1,0:T(8,128)(2,1)} custom-call(s32[4]{0:T(128)} %pad_add_fusion.s_ref, bf16[80,1024]{1,0:T(8,128)(2,1)} %copy-done.3, bf16[80,1024]{1,0:T(8,128)(2,1)} %copy-done.7, bf16[80,1024]{1,0:T(8,128)(2,1)} %copy-done.8, bf16[80,1024]{1,0:T(8,128)(2,1)} %copy-done.9, bf16[4,80,1024]{2,1,0:T(8,128)(2,1)} %copy-done.6, ...), custom_call_target="tpu_custom_call" | custom-call | flops 3758096384 | bytes 12058624 | tf_op jit(solution)/shard_map/update/pallas_call | solution.py:170
  176.4 3.4 %outputs.1 = bf16[128,3584]{1,0:T(8,128)(2,1)} custom-call(s32[4]{0:T(128)} %pad_add_fusion.s_ref, bf16[4,32,896]{2,1,0:T(8,128)(2,1)} %get-tuple-element.102.refs_0_, bf16[4,32,896]{2,1,0:T(8,128)(2,1)} %collective-permute-done.37.refs_1_, bf16[4,32,896]{2,1,0:T(8,128)(2,1)} %copy-done.15, bf16[4,32,896]{2,1,0:T(8,128)(2,1)} %copy-done.14, ...), custom_call_target="tpu_custom_call" | custom-call | flops 29360128 | bytes 3670016 | tf_op jit(solution)/shard_map/outputs/pallas_call | solution.py:113
  (153 shorter events, 30.4 us)
Async XLA Ops:
  1.7 9.8 %collective-permute-start = (bf16[48,1024]{1,0:T(8,128)(2,1)S(1)}, bf16[48,1024]{1,0:T(8,128)(2,1)S(1)}, u32[]{:S(2)}, u32[]{:S(2)}) collective-permute-start(bf16[48,1024]{1,0:T(8,128)(2,1)S(1)} %get-tuple-element.121), channel_id=1, source_target_pairs={{0,2},{2,4},{4,6},{6,0},{1,3},{3,5},{5,7},{7,1},{8,10},{10,12},{12... | collective-permute-start | bytes 294920 | tf_op jit(solution)/shard_map/ppermute | solution.py:18
  3.8 8.2 %collective-permute-start.1 = (bf16[48,1024]{1,0:T(8,128)(2,1)S(1)}, bf16[48,1024]{1,0:T(8,128)(2,1)S(1)}, u32[]{:S(2)}, u32[]{:S(2)}) collective-permute-start(bf16[48,1024]{1,0:T(8,128)(2,1)S(1)} %get-tuple-element.122), channel_id=1, source_target_pairs={{0,4},{2,6},{4,0},{6,2},{1,5},{3,7},{5,1},{7,3},{8,12},{10,14},{12... | collective-permute-start | bytes 294920 | tf_op jit(solution)/shard_map/ppermute | solution.py:18
  9.6 14.8 %collective-permute-start.6 = (bf16[512,896]{1,0:T(8,128)(2,1)S(1)}, bf16[512,896]{1,0:T(8,128)(2,1)}, u32[]{:S(2)}, u32[]{:S(2)}) collective-permute-start(bf16[512,896]{1,0:T(8,128)(2,1)S(1)} %constant_dynamic-slice_fusion.4), channel_id=1, source_target_pairs={{0,8},{8,16},{16,24},{24,0},{1,25},{9,1},{17,9},{25,17},{2,10},{10... | collective-permute-start | bytes 2752520 | tf_op jit(solution)/shard_map/ppermute | solution.py:24
  12.1 7.0 %collective-permute-start.5 = (bf16[48,1024]{1,0:T(8,128)(2,1)S(1)}, bf16[48,1024]{1,0:T(8,128)(2,1)S(1)}, u32[]{:S(2)}, u32[]{:S(2)}) collective-permute-start(bf16[48,1024]{1,0:T(8,128)(2,1)S(1)} %get-tuple-element.117), channel_id=1, source_target_pairs={{0,96},{32,0},{64,32},{96,64},{1,97},{33,1},{65,33},{97,65},{2,98}... | collective-permute-start | bytes 294920 | tf_op jit(solution)/shard_map/ppermute | solution.py:18
  24.5 22.0 %collective-permute-start.10 = (bf16[64,3712]{1,0:T(8,128)(2,1)S(1)}, bf16[64,3712]{1,0:T(8,128)(2,1)S(1)}, u32[]{:S(2)}, u32[]{:S(2)}) collective-permute-start(bf16[64,3712]{1,0:T(8,128)(2,1)S(1)} %fusion.1), channel_id=1, source_target_pairs={{0,32},{32,64},{64,96},{96,0},{1,97},{33,1},{65,33},{97,65},{2,34}... | collective-permute-start | bytes 1425416 | tf_op jit(solution)/shard_map/ppermute | solution.py:24
  26.3 10.8 %collective-permute-start.7 = (bf16[160,1024]{1,0:T(8,128)(2,1)S(1)}, bf16[160,1024]{1,0:T(8,128)(2,1)}, u32[]{:S(2)}, u32[]{:S(2)}) collective-permute-start(bf16[160,1024]{1,0:T(8,128)(2,1)S(1)} %get-tuple-element.125), channel_id=1, source_target_pairs={{0,8},{8,16},{16,24},{24,0},{1,9},{9,17},{17,25},{25,1},{2,10},{10... | collective-permute-start | bytes 983048 | tf_op jit(solution)/shard_map/ppermute | solution.py:18
  26.7 18.4 %collective-permute-start.8 = (bf16[160,1024]{1,0:T(8,128)(2,1)S(1)}, bf16[160,1024]{1,0:T(8,128)(2,1)}, u32[]{:S(2)}, u32[]{:S(2)}) collective-permute-start(bf16[160,1024]{1,0:T(8,128)(2,1)S(1)} %get-tuple-element.126), channel_id=1, source_target_pairs={{0,16},{8,24},{16,0},{24,8},{1,17},{9,25},{17,1},{25,9},{2,18},{10... | collective-permute-start | bytes 983048 | tf_op jit(solution)/shard_map/ppermute | solution.py:18
  29.4 15.7 %collective-permute-start.9 = (bf16[160,1024]{1,0:T(8,128)(2,1)S(1)}, bf16[160,1024]{1,0:T(8,128)(2,1)}, u32[]{:S(2)}, u32[]{:S(2)}) collective-permute-start(bf16[160,1024]{1,0:T(8,128)(2,1)S(1)} %get-tuple-element.127), channel_id=1, source_target_pairs={{0,24},{8,0},{16,8},{24,16},{1,25},{9,1},{17,9},{25,17},{2,26},{10... | collective-permute-start | bytes 983048 | tf_op jit(solution)/shard_map/ppermute | solution.py:18
  32.9 20.7 %collective-permute-start.13 = (bf16[512,896]{1,0:T(8,128)(2,1)S(1)}, bf16[512,896]{1,0:T(8,128)(2,1)S(1)}, u32[]{:S(2)}, u32[]{:S(2)}) collective-permute-start(bf16[512,896]{1,0:T(8,128)(2,1)S(1)} %constant_dynamic-slice_fusion.1), channel_id=1, source_target_pairs={{0,24},{8,0},{16,8},{24,16},{1,9},{9,17},{17,25},{25,1},{2,26},{10... | collective-permute-start | bytes 2752520 | tf_op jit(solution)/shard_map/ppermute | solution.py:24
  47.3 18.7 %collective-permute-start.12 = (bf16[512,1024]{1,0:T(8,128)(2,1)S(1)}, bf16[512,1024]{1,0:T(8,128)(2,1)S(1)}, u32[]{:S(2)}, u32[]{:S(2)}) collective-permute-start(bf16[512,1024]{1,0:T(8,128)(2,1)S(1)} %bitcast.67), channel_id=1, source_target_pairs={{0,1},{1,0},{2,3},{3,2},{4,5},{5,4},{6,7},{7,6},{8,9},{9,8},{10,11... | collective-permute-start | bytes 3145736 | tf_op jit(solution)/shard_map/ppermute | solution.py:262
  47.4 18.7 %collective-permute-start.11 = (bf16[512,1024]{1,0:T(8,128)(2,1)S(1)}, bf16[512,1024]{1,0:T(8,128)(2,1)S(1)}, u32[]{:S(2)}, u32[]{:S(2)}) collective-permute-start(bf16[512,1024]{1,0:T(8,128)(2,1)S(1)} %bitcast.68), channel_id=1, source_target_pairs={{0,2},{2,4},{4,6},{6,0},{1,7},{3,1},{5,3},{7,5},{8,10},{10,12},{12... | collective-permute-start | bytes 3145736 | tf_op jit(solution)/shard_map/ppermute | solution.py:24
  48.6 17.4 %collective-permute-start.15 = (bf16[64,3712]{1,0:T(8,128)(2,1)S(1)}, bf16[64,3712]{1,0:T(8,128)(2,1)S(1)}, u32[]{:S(2)}, u32[]{:S(2)}) collective-permute-start(bf16[64,3712]{1,0:T(8,128)(2,1)S(1)} %copy-done.11), channel_id=1, source_target_pairs={{0,32},{32,64},{64,96},{96,0},{1,97},{33,1},{65,33},{97,65},{2,34}... | collective-permute-start | bytes 1425416 | tf_op jit(solution)/shard_map/ppermute | solution.py:24
  51.6 14.4 %collective-permute-start.14 = (bf16[256,896]{1,0:T(8,128)(2,1)S(1)}, bf16[256,896]{1,0:T(8,128)(2,1)S(1)}, u32[]{:S(2)}, u32[]{:S(2)}) collective-permute-start(bf16[256,896]{1,0:T(8,128)(2,1)S(1)} %get-tuple-element.109), channel_id=1, source_target_pairs={{0,16},{8,24},{16,0},{24,8},{1,17},{9,25},{17,1},{25,9},{2,18},{10... | collective-permute-start | bytes 1376264 | tf_op jit(solution)/shard_map/ppermute | solution.py:24
  66.1 16.2 %collective-permute-start.18 = (bf16[512,1024]{1,0:T(8,128)(2,1)S(1)}, bf16[512,1024]{1,0:T(8,128)(2,1)S(1)}, u32[]{:S(2)}, u32[]{:S(2)}) collective-permute-start(bf16[512,1024]{1,0:T(8,128)(2,1)S(1)} %collective-permute-done.11.own0), channel_id=1, source_target_pairs={{0,1},{1,0},{2,3},{3,2},{4,5},{5,4},{6,7},{7,6},{8,9},{9,8},{10,11... | collective-permute-start | bytes 3145736 | tf_op jit(solution)/shard_map/ppermute | solution.py:278
  66.8 16.1 %collective-permute-start.17 = (bf16[512,1024]{1,0:T(8,128)(2,1)S(1)}, bf16[512,1024]{1,0:T(8,128)(2,1)}, u32[]{:S(2)}, u32[]{:S(2)}) collective-permute-start(bf16[512,1024]{1,0:T(8,128)(2,1)S(1)} %collective-permute-done.11.own0), channel_id=1, source_target_pairs={{0,2},{2,4},{4,6},{6,0},{1,7},{3,1},{5,3},{7,5},{8,10},{10,12},{12... | collective-permute-start | bytes 3145736 | tf_op jit(solution)/shard_map/ppermute | solution.py:24
  67.4 14.8 %collective-permute-start.19 = (bf16[256,896]{1,0:T(8,128)(2,1)S(1)}, bf16[256,896]{1,0:T(8,128)(2,1)S(1)}, u32[]{:S(2)}, u32[]{:S(2)}) collective-permute-start(bf16[256,896]{1,0:T(8,128)(2,1)S(1)} %get-tuple-element.66), channel_id=1, source_target_pairs={{0,16},{8,24},{16,0},{24,8},{1,17},{9,25},{17,1},{25,9},{2,18},{10... | collective-permute-start | bytes 1376264 | tf_op jit(solution)/shard_map/ppermute | solution.py:24
  68.3 14.8 %collective-permute-start.25 = (bf16[64,3712]{1,0:T(8,128)(2,1)S(1)}, bf16[64,3712]{1,0:T(8,128)(2,1)S(1)}, u32[]{:S(2)}, u32[]{:S(2)}) collective-permute-start(bf16[64,3712]{1,0:T(8,128)(2,1)S(1)} %collective-permute-done.15), channel_id=1, source_target_pairs={{0,32},{32,64},{64,96},{96,0},{1,97},{33,1},{65,33},{97,65},{2,34}... | collective-permute-start | bytes 1425416 | tf_op jit(solution)/shard_map/ppermute | solution.py:24
  83.0 16.4 %collective-permute-start.20 = (bf16[512,1024]{1,0:T(8,128)(2,1)}, bf16[512,1024]{1,0:T(8,128)(2,1)}, u32[]{:S(2)}, u32[]{:S(2)}) collective-permute-start(bf16[512,1024]{1,0:T(8,128)(2,1)} %collective-permute-done.17.own1), channel_id=1, source_target_pairs={{0,2},{2,4},{4,6},{6,0},{1,7},{3,1},{5,3},{7,5},{8,10},{10,12},{12... | collective-permute-start | bytes 3145736 | tf_op jit(solution)/shard_map/ppermute | solution.py:24
  83.2 25.5 %collective-permute-start.26 = (bf16[256,3712]{1,0:T(8,128)(2,1)S(1)}, bf16[256,3712]{1,0:T(8,128)(2,1)}, u32[]{:S(2)}, u32[]{:S(2)}) collective-permute-start(bf16[256,3712]{1,0:T(8,128)(2,1)S(1)} %constant_dynamic-update-slice_fusion.refs_0_.refs_4_), channel_id=1, source_target_pairs={{0,8},{8,16},{16,24},{24,0},{1,25},{9,1},{17,9},{25,17},{2,10},{10... | collective-permute-start | bytes 5701640 | tf_op jit(solution)/shard_map/ppermute | solution.py:24
  99.4 9.3 %collective-permute-start.27 = (bf16[512,1024]{1,0:T(8,128)(2,1)}, bf16[512,1024]{1,0:T(8,128)(2,1)S(1)}, u32[]{:S(2)}, u32[]{:S(2)}) collective-permute-start(bf16[512,1024]{1,0:T(8,128)(2,1)} %collective-permute-done.20.own1), channel_id=1, source_target_pairs={{0,1},{1,0},{2,3},{3,2},{4,5},{5,4},{6,7},{7,6},{8,9},{9,8},{10,11... | collective-permute-start | bytes 3145736 | tf_op jit(solution)/shard_map/ppermute | solution.py:290
  108.7 27.9 %collective-permute-start.28 = (bf16[256,3712]{1,0:T(8,128)(2,1)}, bf16[256,3712]{1,0:T(8,128)(2,1)S(1)}, u32[]{:S(2)}, u32[]{:S(2)}) collective-permute-start(bf16[256,3712]{1,0:T(8,128)(2,1)} %collective-permute-done.26.refs_1_.refs_5_), channel_id=1, source_target_pairs={{0,8},{8,16},{16,24},{24,0},{1,25},{9,1},{17,9},{25,17},{2,10},{10... | collective-permute-start | bytes 5701640 | tf_op jit(solution)/shard_map/ppermute | solution.py:24
  109.6 14.8 %collective-permute-start.22 = (bf16[4,2,32,896]{3,2,1,0:T(8,128)(2,1)}, bf16[4,2,32,896]{3,2,1,0:T(8,128)(2,1)S(1)}, u32[]{:S(2)}, u32[]{:S(2)}) collective-permute-start(bf16[4,2,32,896]{3,2,1,0:T(8,128)(2,1)} %get-tuple-element.78), channel_id=1, source_target_pairs={{0,32},{32,64},{64,96},{96,0},{1,33},{33,65},{65,97},{97,1},{2,34}... | collective-permute-start | bytes 1376264 | tf_op jit(solution)/shard_map/ppermute | solution.py:18
  109.8 24.5 %collective-permute-start.23 = (bf16[4,2,32,896]{3,2,1,0:T(8,128)(2,1)}, bf16[4,2,32,896]{3,2,1,0:T(8,128)(2,1)S(1)}, u32[]{:S(2)}, u32[]{:S(2)}) collective-permute-start(bf16[4,2,32,896]{3,2,1,0:T(8,128)(2,1)} %get-tuple-element.79), channel_id=1, source_target_pairs={{0,64},{32,96},{64,0},{96,32},{1,65},{33,97},{65,1},{97,33},{2,66}... | collective-permute-start | bytes 1376264 | tf_op jit(solution)/shard_map/ppermute | solution.py:18
  112.7 22.6 %collective-permute-start.24 = (bf16[4,2,32,896]{3,2,1,0:T(8,128)(2,1)}, bf16[4,2,32,896]{3,2,1,0:T(8,128)(2,1)}, u32[]{:S(2)}, u32[]{:S(2)}) collective-permute-start(bf16[4,2,32,896]{3,2,1,0:T(8,128)(2,1)} %get-tuple-element.80), channel_id=1, source_target_pairs={{0,96},{32,0},{64,32},{96,64},{1,97},{33,1},{65,33},{97,65},{2,98}... | collective-permute-start | bytes 1376264 | tf_op jit(solution)/shard_map/ppermute | solution.py:18
  123.8 26.1 %collective-permute-start.30 = (bf16[4,2,32,896]{3,2,1,0:T(8,128)(2,1)}, bf16[4,2,32,896]{3,2,1,0:T(8,128)(2,1)S(1)}, u32[]{:S(2)}, u32[]{:S(2)}) collective-permute-start(bf16[4,2,32,896]{3,2,1,0:T(8,128)(2,1)} %get-tuple-element.92), channel_id=1, source_target_pairs={{0,32},{32,64},{64,96},{96,0},{1,33},{33,65},{65,97},{97,1},{2,34}... | collective-permute-start | bytes 1376264 | tf_op jit(solution)/shard_map/ppermute | solution.py:18
  124.5 27.6 %collective-permute-start.31 = (bf16[4,2,32,896]{3,2,1,0:T(8,128)(2,1)}, bf16[4,2,32,896]{3,2,1,0:T(8,128)(2,1)S(1)}, u32[]{:S(2)}, u32[]{:S(2)}) collective-permute-start(bf16[4,2,32,896]{3,2,1,0:T(8,128)(2,1)} %get-tuple-element.93), channel_id=1, source_target_pairs={{0,64},{32,96},{64,0},{96,32},{1,65},{33,97},{65,1},{97,33},{2,66}... | collective-permute-start | bytes 1376264 | tf_op jit(solution)/shard_map/ppermute | solution.py:18
  134.3 18.4 %collective-permute-start.32 = (bf16[4,2,32,896]{3,2,1,0:T(8,128)(2,1)}, bf16[4,2,32,896]{3,2,1,0:T(8,128)(2,1)S(1)}, u32[]{:S(2)}, u32[]{:S(2)}) collective-permute-start(bf16[4,2,32,896]{3,2,1,0:T(8,128)(2,1)} %get-tuple-element.94), channel_id=1, source_target_pairs={{0,96},{32,0},{64,32},{96,64},{1,97},{33,1},{65,33},{97,65},{2,98}... | collective-permute-start | bytes 1376264 | tf_op jit(solution)/shard_map/ppermute | solution.py:18
  136.6 27.5 %collective-permute-start.35 = (bf16[256,3712]{1,0:T(8,128)(2,1)S(1)}, bf16[256,3712]{1,0:T(8,128)(2,1)}, u32[]{:S(2)}, u32[]{:S(2)}) collective-permute-start(bf16[256,3712]{1,0:T(8,128)(2,1)S(1)} %collective-permute-done.28.refs_2_.refs_6_), channel_id=1, source_target_pairs={{0,8},{8,16},{16,24},{24,0},{1,25},{9,1},{17,9},{25,17},{2,10},{10... | collective-permute-start | bytes 5701640 | tf_op jit(solution)/shard_map/ppermute | solution.py:24
  156.5 7.5 %collective-permute-start.36 = (bf16[4,80,1024]{2,1,0:T(8,128)(2,1)S(1)}, bf16[4,80,1024]{2,1,0:T(8,128)(2,1)S(1)}, u32[]{:S(2)}, u32[]{:S(2)}) collective-permute-start(bf16[4,80,1024]{2,1,0:T(8,128)(2,1)S(1)} %pad_maximum_fusion.1), channel_id=1, source_target_pairs={{0,1},{1,0},{2,3},{3,2},{4,5},{5,4},{6,7},{7,6},{8,9},{9,8},{10,11... | collective-permute-start | bytes 1966088 | tf_op jit(solution)/shard_map/ppermute | solution.py:311
  157.7 17.8 %collective-permute-start.39 = (bf16[4,32,896]{2,1,0:T(8,128)(2,1)}, bf16[4,32,896]{2,1,0:T(8,128)(2,1)S(1)}, u32[]{:S(2)}, u32[]{:S(2)}) collective-permute-start(bf16[4,32,896]{2,1,0:T(8,128)(2,1)} %get-tuple-element.112), channel_id=1, source_target_pairs={{0,8},{8,16},{16,24},{24,0},{1,9},{9,17},{17,25},{25,1},{2,10},{10... | collective-permute-start | bytes 688136 | tf_op jit(solution)/shard_map/ppermute | solution.py:18
  157.7 17.9 %collective-permute-start.38 = (bf16[4,32,896]{2,1,0:T(8,128)(2,1)}, bf16[4,32,896]{2,1,0:T(8,128)(2,1)S(1)}, u32[]{:S(2)}, u32[]{:S(2)}) collective-permute-start(bf16[4,32,896]{2,1,0:T(8,128)(2,1)} %get-tuple-element.113), channel_id=1, source_target_pairs={{0,16},{8,24},{16,0},{24,8},{1,17},{9,25},{17,1},{25,9},{2,18},{10... | collective-permute-start | bytes 688136 | tf_op jit(solution)/shard_map/ppermute | solution.py:18
  162.3 13.3 %collective-permute-start.37 = (bf16[4,32,896]{2,1,0:T(8,128)(2,1)}, bf16[4,32,896]{2,1,0:T(8,128)(2,1)}, u32[]{:S(2)}, u32[]{:S(2)}) collective-permute-start(bf16[4,32,896]{2,1,0:T(8,128)(2,1)} %get-tuple-element.114), channel_id=1, source_target_pairs={{0,24},{8,0},{16,8},{24,16},{1,25},{9,1},{17,9},{25,17},{2,26},{10... | collective-permute-start | bytes 688136 | tf_op jit(solution)/shard_map/ppermute | solution.py:18
  (34 other events, 404.6 us)
